TPU v7x, 512 devices: a whole 4x8x8 slice. The times are simulated.
512 devices in a mesh: row: 16 (over y, core), col: 8 (over z), depth: 4 (over x).
Axes of the slice: x: 4, y: 8, z: 8, core: 2. Of those that a mesh axis runs over, the one named last changes fastest.
Arguments:
- density_tiles: bfloat16 [4, 16, 8, 4, 256, 256], P('depth', 'row', 'col'), may hold values from -0.75 to 0.75
- density_rows: int32 [4, 16, 8, 4], P('depth', 'row', 'col'), may hold values from 0 to 7, as said below
- square_tiles: bfloat16 [4, 16, 8, 2, 2, 256, 256], P('depth', 'row', 'col'), may hold values from -0.75 to 0.75
- square_cols: int32 [4, 16, 8, 2, 2], P('depth', 'row', 'col'), may hold values from 0 to 3, as said below
- keep_rows: int32 [16, 8, 12], P('row', 'col'), may hold values from 0 to 7, as said below
- keep_cols: int32 [16, 8, 12], P('row', 'col'), may hold values from 0 to 3
- square_kept: bfloat16 [16, 8, 12, 256, 256], P('row', 'col', 'depth'), may hold values from -3 to 3
Outputs:
- next_density: bfloat16 [16, 8, 12, 256, 256], P('row', 'col', 'depth')
Inputs may be any that keep to these rules, and one draw needn't show every extreme that they name: density_rows are distinct within one tile. square_cols are distinct within one piece. The pairs (keep_rows, keep_cols) are distinct within one tile.
All inputs are finite; a program needn't handle non-finite values.
Results may differ from a plain program's by a relative error of at most 0.001.
Values may be sent and summed in bfloat16 or wider, within the bound.
No kernel may reach another device: no remote copies, remote signals or barrier semaphores. Data moves between devices by JAX's collectives and lax.ppermute only.
A program may use at most 64 MiB of HBM per device.

v0:
```python
import jax
import jax.numpy as jnp
from jax import lax
from jax.sharding import PartitionSpec as P


def passed_along(value, axis, steps):
    count = lax.axis_size(axis)
    pairs = [(source, (source + steps) % count) for source in range(count)]
    return lax.ppermute(value, axis, pairs)


def body(density_tiles, density_rows, square_tiles, square_cols, keep_rows, keep_cols, square_kept):
    rows_count = lax.axis_size("row")
    cols_count = lax.axis_size("col")
    my_col = lax.axis_index("col")
    wanted_rows = keep_rows[0, 0]
    wanted_cols = keep_cols[0, 0]
    blocks = density_tiles.shape[-1]
    slots = wanted_rows.shape[0]

    def contribute(total, blocks_a, rows_a, blocks_b, cols_b):
        pick_a = (rows_a[None, :] == wanted_rows[:, None]).astype(jnp.bfloat16)
        chosen_a = jnp.einsum(
            "sa,axy->sxy", pick_a, blocks_a, preferred_element_type=jnp.float32
        ).astype(jnp.bfloat16)
        pick_b = (cols_b[None, :] == wanted_cols[:, None]).astype(jnp.bfloat16)
        chosen_b = jnp.einsum(
            "sb,bxy->sxy", pick_b, blocks_b, preferred_element_type=jnp.float32
        ).astype(jnp.bfloat16)
        return total + jnp.einsum(
            "sxy,syz->sxz", chosen_a, chosen_b, preferred_element_type=jnp.float32
        )

    empty = jnp.zeros((slots, blocks, blocks), jnp.float32)
    pieces_held = square_tiles.shape[3]

    def use_step(step, total, blocks_a, rows_a, blocks_b, cols_b):
        which = (my_col + step) // cols_count % pieces_held
        piece_b = lax.dynamic_index_in_dim(blocks_b, which, 0, keepdims=False)
        piece_cols = lax.dynamic_index_in_dim(cols_b, which, 0, keepdims=False)
        return contribute(total, blocks_a, rows_a, piece_b, piece_cols)

    def advance(step, carry):
        total, blocks_a, rows_a, blocks_b, cols_b = carry
        total = use_step(step, total, blocks_a, rows_a, blocks_b, cols_b)
        blocks_a, rows_a = passed_along((blocks_a, rows_a), "row", -1)
        blocks_b, cols_b = passed_along((blocks_b, cols_b), "col", -1)
        return (total, blocks_a, rows_a, blocks_b, cols_b)

    start = (
        empty,
        density_tiles[0, 0, 0],
        density_rows[0, 0, 0],
        square_tiles[0, 0, 0],
        square_cols[0, 0, 0],
    )
    total, blocks_a, rows_a, blocks_b, cols_b = lax.fori_loop(0, rows_count - 1, advance, start)
    total = use_step(rows_count - 1, total, blocks_a, rows_a, blocks_b, cols_b)
    shares = lax.psum_scatter(total, "depth", scatter_dimension=0, tiled=True)
    result = 3.0 * square_kept[0, 0].astype(jnp.float32) - 2.0 * shares
    return result.astype(jnp.bfloat16)[None, None]


def solution(mesh):
    placed = (
        P("depth", "row", "col", None, None, None),
        P("depth", "row", "col", None),
        P("depth", "row", "col", None, None, None, None),
        P("depth", "row", "col", None, None),
        P("row", "col", None),
        P("row", "col", None),
        P("row", "col", "depth", None, None),
    )
    return jax.shard_map(
        body,
        mesh=mesh,
        in_specs=placed,
        out_specs=P("row", "col", "depth", None, None),
        check_vma=False,
    )
```

profile of v0, /device:TPU:1, one launch (start us, length us, event | category | flops | bytes accessed | tf_op | source)
XLA Modules:
  0.0 369.7 jit_solution(12593225028081240410)
XLA Ops:
  10.4 302.5 %while.24 = (s32[]{:T(128)}, f32[12,256,256]{2,1,0:T(8,128)}, bf16[4,256,256]{2,1,0:T(8,128)(2,1)}, s32[4]{0:T(128)S(1)}, bf16[2,2,256,256]{3,2,1,0:T(8,128)(2,1...) while((s32[]{:T(128)}, f32[12,256,256]{2,1,0:T(8,128)}, ...), condition=%wide.region_1.2_spmd.clone, body=%wide.region_0.1_spmd.clone.sunk | while | flops 413663328 | bytes 20186048 | solution.py:58
  11.4 6.9 %collective-permute-start = (bf16[4,256,256]{2,1,0:T(8,128)(2,1)S(1)}, bf16[4,256,256]{2,1,0:T(8,128)(2,1)}, u32[]{:S(2)}, u32[]{:S(2)}) collective-permute-start(bf16[4,256,256]{2,1,0:T(8,128)(2,1)S(1)} %copy.48), channel_id=1, source_target_pairs={{0,480},{32,0},{64,32},{96,64},{128,96},{160,128},{192,160},{224,1... | collective-permute-start | bytes 1572872 | tf_op jit(solution)/shard_map/while/body/eval_jaxpr/ppermute | solution.py:10
  19.4 8.2 %collective-permute-start.2 = (bf16[2,2,256,256]{3,2,1,0:T(8,128)(2,1)S(1)}, bf16[2,2,256,256]{3,2,1,0:T(8,128)(2,1)}, u32[]{:S(2)}, u32[]{:S(2)}) collective-permute-start(bf16[2,2,256,256]{3,2,1,0:T(8,128)(2,1)S(1)} %copy.50), channel_id=1, source_target_pairs={{0,28},{4,0},{8,4},{12,8},{16,12},{20,16},{24,20},{28,24},{1,29},{... | collective-permute-start | bytes 1572872 | tf_op jit(solution)/shard_map/while/body/eval_jaxpr/ppermute | solution.py:10
  27.6 2.2 collective-permute-start.3
  30.6 2.1 fusion.37
  32.7 4.4 %select_add_fusion.2 = f32[12,256,256]{2,1,0:T(8,128)} fusion(f32[12,256,256]{2,1,0:T(8,128)} %get-tuple-element.356, bf16[12,256,256]{2,0,1:T(8,128)(2,1)S(1)} %fusion.36, bf16[12,256,256]{2,0,1:T(8,128)(2,1)} %fusion.37, pred[]{:T(512)S(6)} %compare.17), kind=kOutput, calls=%fused_computation.2.clone.1 | convolution fusion | flops 404226048 | bytes 9437185 | tf_op jit(solution)/shard_map/while/body/eval_jaxpr/sxy,syz->sxz/dot_general | solution.py:31
  41.8 5.4 %collective-permute-start.2 = (bf16[2,2,256,256]{3,2,1,0:T(8,128)(2,1)S(1)}, bf16[2,2,256,256]{3,2,1,0:T(8,128)(2,1)}, u32[]{:S(2)}, u32[]{:S(2)}) collective-permute-start(bf16[2,2,256,256]{3,2,1,0:T(8,128)(2,1)S(1)} %copy.50), channel_id=1, source_target_pairs={{0,28},{4,0},{8,4},{12,8},{16,12},{20,16},{24,20},{28,24},{1,29},{... | collective-permute-start | bytes 1572872 | tf_op jit(solution)/shard_map/while/body/eval_jaxpr/ppermute | solution.py:10
  50.0 2.1 fusion.37
  52.1 5.3 %select_add_fusion.2 = f32[12,256,256]{2,1,0:T(8,128)} fusion(f32[12,256,256]{2,1,0:T(8,128)} %get-tuple-element.356, bf16[12,256,256]{2,0,1:T(8,128)(2,1)S(1)} %fusion.36, bf16[12,256,256]{2,0,1:T(8,128)(2,1)} %fusion.37, pred[]{:T(512)S(6)} %compare.17), kind=kOutput, calls=%fused_computation.2.clone.1 | convolution fusion | flops 404226048 | bytes 9437185 | tf_op jit(solution)/shard_map/while/body/eval_jaxpr/sxy,syz->sxz/dot_general | solution.py:31
  61.5 5.4 %collective-permute-start.2 = (bf16[2,2,256,256]{3,2,1,0:T(8,128)(2,1)S(1)}, bf16[2,2,256,256]{3,2,1,0:T(8,128)(2,1)}, u32[]{:S(2)}, u32[]{:S(2)}) collective-permute-start(bf16[2,2,256,256]{3,2,1,0:T(8,128)(2,1)S(1)} %copy.50), channel_id=1, source_target_pairs={{0,28},{4,0},{8,4},{12,8},{16,12},{20,16},{24,20},{28,24},{1,29},{... | collective-permute-start | bytes 1572872 | tf_op jit(solution)/shard_map/while/body/eval_jaxpr/ppermute | solution.py:10
  69.6 2.1 fusion.37
  71.8 5.3 %select_add_fusion.2 = f32[12,256,256]{2,1,0:T(8,128)} fusion(f32[12,256,256]{2,1,0:T(8,128)} %get-tuple-element.356, bf16[12,256,256]{2,0,1:T(8,128)(2,1)S(1)} %fusion.36, bf16[12,256,256]{2,0,1:T(8,128)(2,1)} %fusion.37, pred[]{:T(512)S(6)} %compare.17), kind=kOutput, calls=%fused_computation.2.clone.1 | convolution fusion | flops 404226048 | bytes 9437185 | tf_op jit(solution)/shard_map/while/body/eval_jaxpr/sxy,syz->sxz/dot_general | solution.py:31
  81.1 5.4 %collective-permute-start.2 = (bf16[2,2,256,256]{3,2,1,0:T(8,128)(2,1)S(1)}, bf16[2,2,256,256]{3,2,1,0:T(8,128)(2,1)}, u32[]{:S(2)}, u32[]{:S(2)}) collective-permute-start(bf16[2,2,256,256]{3,2,1,0:T(8,128)(2,1)S(1)} %copy.50), channel_id=1, source_target_pairs={{0,28},{4,0},{8,4},{12,8},{16,12},{20,16},{24,20},{28,24},{1,29},{... | collective-permute-start | bytes 1572872 | tf_op jit(solution)/shard_map/while/body/eval_jaxpr/ppermute | solution.py:10
  89.3 2.1 fusion.37
  91.4 5.3 %select_add_fusion.2 = f32[12,256,256]{2,1,0:T(8,128)} fusion(f32[12,256,256]{2,1,0:T(8,128)} %get-tuple-element.356, bf16[12,256,256]{2,0,1:T(8,128)(2,1)S(1)} %fusion.36, bf16[12,256,256]{2,0,1:T(8,128)(2,1)} %fusion.37, pred[]{:T(512)S(6)} %compare.17), kind=kOutput, calls=%fused_computation.2.clone.1 | convolution fusion | flops 404226048 | bytes 9437185 | tf_op jit(solution)/shard_map/while/body/eval_jaxpr/sxy,syz->sxz/dot_general | solution.py:31
  100.8 5.4 %collective-permute-start.2 = (bf16[2,2,256,256]{3,2,1,0:T(8,128)(2,1)S(1)}, bf16[2,2,256,256]{3,2,1,0:T(8,128)(2,1)}, u32[]{:S(2)}, u32[]{:S(2)}) collective-permute-start(bf16[2,2,256,256]{3,2,1,0:T(8,128)(2,1)S(1)} %copy.50), channel_id=1, source_target_pairs={{0,28},{4,0},{8,4},{12,8},{16,12},{20,16},{24,20},{28,24},{1,29},{... | collective-permute-start | bytes 1572872 | tf_op jit(solution)/shard_map/while/body/eval_jaxpr/ppermute | solution.py:10
  108.9 2.1 fusion.37
  111.1 5.3 %select_add_fusion.2 = f32[12,256,256]{2,1,0:T(8,128)} fusion(f32[12,256,256]{2,1,0:T(8,128)} %get-tuple-element.356, bf16[12,256,256]{2,0,1:T(8,128)(2,1)S(1)} %fusion.36, bf16[12,256,256]{2,0,1:T(8,128)(2,1)} %fusion.37, pred[]{:T(512)S(6)} %compare.17), kind=kOutput, calls=%fused_computation.2.clone.1 | convolution fusion | flops 404226048 | bytes 9437185 | tf_op jit(solution)/shard_map/while/body/eval_jaxpr/sxy,syz->sxz/dot_general | solution.py:31
  120.4 5.4 %collective-permute-start.2 = (bf16[2,2,256,256]{3,2,1,0:T(8,128)(2,1)S(1)}, bf16[2,2,256,256]{3,2,1,0:T(8,128)(2,1)}, u32[]{:S(2)}, u32[]{:S(2)}) collective-permute-start(bf16[2,2,256,256]{3,2,1,0:T(8,128)(2,1)S(1)} %copy.50), channel_id=1, source_target_pairs={{0,28},{4,0},{8,4},{12,8},{16,12},{20,16},{24,20},{28,24},{1,29},{... | collective-permute-start | bytes 1572872 | tf_op jit(solution)/shard_map/while/body/eval_jaxpr/ppermute | solution.py:10
  128.6 2.1 fusion.37
  130.7 5.3 %select_add_fusion.2 = f32[12,256,256]{2,1,0:T(8,128)} fusion(f32[12,256,256]{2,1,0:T(8,128)} %get-tuple-element.356, bf16[12,256,256]{2,0,1:T(8,128)(2,1)S(1)} %fusion.36, bf16[12,256,256]{2,0,1:T(8,128)(2,1)} %fusion.37, pred[]{:T(512)S(6)} %compare.17), kind=kOutput, calls=%fused_computation.2.clone.1 | convolution fusion | flops 404226048 | bytes 9437185 | tf_op jit(solution)/shard_map/while/body/eval_jaxpr/sxy,syz->sxz/dot_general | solution.py:31
  140.1 5.4 %collective-permute-start.2 = (bf16[2,2,256,256]{3,2,1,0:T(8,128)(2,1)S(1)}, bf16[2,2,256,256]{3,2,1,0:T(8,128)(2,1)}, u32[]{:S(2)}, u32[]{:S(2)}) collective-permute-start(bf16[2,2,256,256]{3,2,1,0:T(8,128)(2,1)S(1)} %copy.50), channel_id=1, source_target_pairs={{0,28},{4,0},{8,4},{12,8},{16,12},{20,16},{24,20},{28,24},{1,29},{... | collective-permute-start | bytes 1572872 | tf_op jit(solution)/shard_map/while/body/eval_jaxpr/ppermute | solution.py:10
  148.2 2.1 fusion.37
  150.3 5.3 %select_add_fusion.2 = f32[12,256,256]{2,1,0:T(8,128)} fusion(f32[12,256,256]{2,1,0:T(8,128)} %get-tuple-element.356, bf16[12,256,256]{2,0,1:T(8,128)(2,1)S(1)} %fusion.36, bf16[12,256,256]{2,0,1:T(8,128)(2,1)} %fusion.37, pred[]{:T(512)S(6)} %compare.17), kind=kOutput, calls=%fused_computation.2.clone.1 | convolution fusion | flops 404226048 | bytes 9437185 | tf_op jit(solution)/shard_map/while/body/eval_jaxpr/sxy,syz->sxz/dot_general | solution.py:31
  159.7 5.4 %collective-permute-start.2 = (bf16[2,2,256,256]{3,2,1,0:T(8,128)(2,1)S(1)}, bf16[2,2,256,256]{3,2,1,0:T(8,128)(2,1)}, u32[]{:S(2)}, u32[]{:S(2)}) collective-permute-start(bf16[2,2,256,256]{3,2,1,0:T(8,128)(2,1)S(1)} %copy.50), channel_id=1, source_target_pairs={{0,28},{4,0},{8,4},{12,8},{16,12},{20,16},{24,20},{28,24},{1,29},{... | collective-permute-start | bytes 1572872 | tf_op jit(solution)/shard_map/while/body/eval_jaxpr/ppermute | solution.py:10
  170.0 5.3 %select_add_fusion.2 = f32[12,256,256]{2,1,0:T(8,128)} fusion(f32[12,256,256]{2,1,0:T(8,128)} %get-tuple-element.356, bf16[12,256,256]{2,0,1:T(8,128)(2,1)S(1)} %fusion.36, bf16[12,256,256]{2,0,1:T(8,128)(2,1)} %fusion.37, pred[]{:T(512)S(6)} %compare.17), kind=kOutput, calls=%fused_computation.2.clone.1 | convolution fusion | flops 404226048 | bytes 9437185 | tf_op jit(solution)/shard_map/while/body/eval_jaxpr/sxy,syz->sxz/dot_general | solution.py:31
  179.4 5.4 %collective-permute-start.2 = (bf16[2,2,256,256]{3,2,1,0:T(8,128)(2,1)S(1)}, bf16[2,2,256,256]{3,2,1,0:T(8,128)(2,1)}, u32[]{:S(2)}, u32[]{:S(2)}) collective-permute-start(bf16[2,2,256,256]{3,2,1,0:T(8,128)(2,1)S(1)} %copy.50), channel_id=1, source_target_pairs={{0,28},{4,0},{8,4},{12,8},{16,12},{20,16},{24,20},{28,24},{1,29},{... | collective-permute-start | bytes 1572872 | tf_op jit(solution)/shard_map/while/body/eval_jaxpr/ppermute | solution.py:10
  187.5 2.1 fusion.37
  189.6 5.3 %select_add_fusion.2 = f32[12,256,256]{2,1,0:T(8,128)} fusion(f32[12,256,256]{2,1,0:T(8,128)} %get-tuple-element.356, bf16[12,256,256]{2,0,1:T(8,128)(2,1)S(1)} %fusion.36, bf16[12,256,256]{2,0,1:T(8,128)(2,1)} %fusion.37, pred[]{:T(512)S(6)} %compare.17), kind=kOutput, calls=%fused_computation.2.clone.1 | convolution fusion | flops 404226048 | bytes 9437185 | tf_op jit(solution)/shard_map/while/body/eval_jaxpr/sxy,syz->sxz/dot_general | solution.py:31
  199.0 5.4 %collective-permute-start.2 = (bf16[2,2,256,256]{3,2,1,0:T(8,128)(2,1)S(1)}, bf16[2,2,256,256]{3,2,1,0:T(8,128)(2,1)}, u32[]{:S(2)}, u32[]{:S(2)}) collective-permute-start(bf16[2,2,256,256]{3,2,1,0:T(8,128)(2,1)S(1)} %copy.50), channel_id=1, source_target_pairs={{0,28},{4,0},{8,4},{12,8},{16,12},{20,16},{24,20},{28,24},{1,29},{... | collective-permute-start | bytes 1572872 | tf_op jit(solution)/shard_map/while/body/eval_jaxpr/ppermute | solution.py:10
  207.2 2.1 fusion.37
  209.3 5.3 %select_add_fusion.2 = f32[12,256,256]{2,1,0:T(8,128)} fusion(f32[12,256,256]{2,1,0:T(8,128)} %get-tuple-element.356, bf16[12,256,256]{2,0,1:T(8,128)(2,1)S(1)} %fusion.36, bf16[12,256,256]{2,0,1:T(8,128)(2,1)} %fusion.37, pred[]{:T(512)S(6)} %compare.17), kind=kOutput, calls=%fused_computation.2.clone.1 | convolution fusion | flops 404226048 | bytes 9437185 | tf_op jit(solution)/shard_map/while/body/eval_jaxpr/sxy,syz->sxz/dot_general | solution.py:31
  218.7 5.4 %collective-permute-start.2 = (bf16[2,2,256,256]{3,2,1,0:T(8,128)(2,1)S(1)}, bf16[2,2,256,256]{3,2,1,0:T(8,128)(2,1)}, u32[]{:S(2)}, u32[]{:S(2)}) collective-permute-start(bf16[2,2,256,256]{3,2,1,0:T(8,128)(2,1)S(1)} %copy.50), channel_id=1, source_target_pairs={{0,28},{4,0},{8,4},{12,8},{16,12},{20,16},{24,20},{28,24},{1,29},{... | collective-permute-start | bytes 1572872 | tf_op jit(solution)/shard_map/while/body/eval_jaxpr/ppermute | solution.py:10
  226.8 2.1 fusion.37
  228.9 5.3 %select_add_fusion.2 = f32[12,256,256]{2,1,0:T(8,128)} fusion(f32[12,256,256]{2,1,0:T(8,128)} %get-tuple-element.356, bf16[12,256,256]{2,0,1:T(8,128)(2,1)S(1)} %fusion.36, bf16[12,256,256]{2,0,1:T(8,128)(2,1)} %fusion.37, pred[]{:T(512)S(6)} %compare.17), kind=kOutput, calls=%fused_computation.2.clone.1 | convolution fusion | flops 404226048 | bytes 9437185 | tf_op jit(solution)/shard_map/while/body/eval_jaxpr/sxy,syz->sxz/dot_general | solution.py:31
  238.3 5.4 %collective-permute-start.2 = (bf16[2,2,256,256]{3,2,1,0:T(8,128)(2,1)S(1)}, bf16[2,2,256,256]{3,2,1,0:T(8,128)(2,1)}, u32[]{:S(2)}, u32[]{:S(2)}) collective-permute-start(bf16[2,2,256,256]{3,2,1,0:T(8,128)(2,1)S(1)} %copy.50), channel_id=1, source_target_pairs={{0,28},{4,0},{8,4},{12,8},{16,12},{20,16},{24,20},{28,24},{1,29},{... | collective-permute-start | bytes 1572872 | tf_op jit(solution)/shard_map/while/body/eval_jaxpr/ppermute | solution.py:10
  248.6 5.3 %select_add_fusion.2 = f32[12,256,256]{2,1,0:T(8,128)} fusion(f32[12,256,256]{2,1,0:T(8,128)} %get-tuple-element.356, bf16[12,256,256]{2,0,1:T(8,128)(2,1)S(1)} %fusion.36, bf16[12,256,256]{2,0,1:T(8,128)(2,1)} %fusion.37, pred[]{:T(512)S(6)} %compare.17), kind=kOutput, calls=%fused_computation.2.clone.1 | convolution fusion | flops 404226048 | bytes 9437185 | tf_op jit(solution)/shard_map/while/body/eval_jaxpr/sxy,syz->sxz/dot_general | solution.py:31
  257.9 5.4 %collective-permute-start.2 = (bf16[2,2,256,256]{3,2,1,0:T(8,128)(2,1)S(1)}, bf16[2,2,256,256]{3,2,1,0:T(8,128)(2,1)}, u32[]{:S(2)}, u32[]{:S(2)}) collective-permute-start(bf16[2,2,256,256]{3,2,1,0:T(8,128)(2,1)S(1)} %copy.50), channel_id=1, source_target_pairs={{0,28},{4,0},{8,4},{12,8},{16,12},{20,16},{24,20},{28,24},{1,29},{... | collective-permute-start | bytes 1572872 | tf_op jit(solution)/shard_map/while/body/eval_jaxpr/ppermute | solution.py:10
  266.1 2.1 fusion.37
  268.2 5.3 %select_add_fusion.2 = f32[12,256,256]{2,1,0:T(8,128)} fusion(f32[12,256,256]{2,1,0:T(8,128)} %get-tuple-element.356, bf16[12,256,256]{2,0,1:T(8,128)(2,1)S(1)} %fusion.36, bf16[12,256,256]{2,0,1:T(8,128)(2,1)} %fusion.37, pred[]{:T(512)S(6)} %compare.17), kind=kOutput, calls=%fused_computation.2.clone.1 | convolution fusion | flops 404226048 | bytes 9437185 | tf_op jit(solution)/shard_map/while/body/eval_jaxpr/sxy,syz->sxz/dot_general | solution.py:31
  277.6 5.4 %collective-permute-start.2 = (bf16[2,2,256,256]{3,2,1,0:T(8,128)(2,1)S(1)}, bf16[2,2,256,256]{3,2,1,0:T(8,128)(2,1)}, u32[]{:S(2)}, u32[]{:S(2)}) collective-permute-start(bf16[2,2,256,256]{3,2,1,0:T(8,128)(2,1)S(1)} %copy.50), channel_id=1, source_target_pairs={{0,28},{4,0},{8,4},{12,8},{16,12},{20,16},{24,20},{28,24},{1,29},{... | collective-permute-start | bytes 1572872 | tf_op jit(solution)/shard_map/while/body/eval_jaxpr/ppermute | solution.py:10
  285.8 2.1 fusion.37
  287.9 5.3 %select_add_fusion.2 = f32[12,256,256]{2,1,0:T(8,128)} fusion(f32[12,256,256]{2,1,0:T(8,128)} %get-tuple-element.356, bf16[12,256,256]{2,0,1:T(8,128)(2,1)S(1)} %fusion.36, bf16[12,256,256]{2,0,1:T(8,128)(2,1)} %fusion.37, pred[]{:T(512)S(6)} %compare.17), kind=kOutput, calls=%fused_computation.2.clone.1 | convolution fusion | flops 404226048 | bytes 9437185 | tf_op jit(solution)/shard_map/while/body/eval_jaxpr/sxy,syz->sxz/dot_general | solution.py:31
  297.2 5.4 %collective-permute-start.2 = (bf16[2,2,256,256]{3,2,1,0:T(8,128)(2,1)S(1)}, bf16[2,2,256,256]{3,2,1,0:T(8,128)(2,1)}, u32[]{:S(2)}, u32[]{:S(2)}) collective-permute-start(bf16[2,2,256,256]{3,2,1,0:T(8,128)(2,1)S(1)} %copy.50), channel_id=1, source_target_pairs={{0,28},{4,0},{8,4},{12,8},{16,12},{20,16},{24,20},{28,24},{1,29},{... | collective-permute-start | bytes 1572872 | tf_op jit(solution)/shard_map/while/body/eval_jaxpr/ppermute | solution.py:10
  305.4 2.1 fusion.37
  307.5 5.3 %select_add_fusion.2 = f32[12,256,256]{2,1,0:T(8,128)} fusion(f32[12,256,256]{2,1,0:T(8,128)} %get-tuple-element.356, bf16[12,256,256]{2,0,1:T(8,128)(2,1)S(1)} %fusion.36, bf16[12,256,256]{2,0,1:T(8,128)(2,1)} %fusion.37, pred[]{:T(512)S(6)} %compare.17), kind=kOutput, calls=%fused_computation.2.clone.1 | convolution fusion | flops 404226048 | bytes 9437185 | tf_op jit(solution)/shard_map/while/body/eval_jaxpr/sxy,syz->sxz/dot_general | solution.py:31
  316.6 2.7 convolution_add_fusion
  319.4 41.5 %reduce-scatter.2.cloned.1.call-done = f32[3,256,256]{2,1,0:T(8,128)} async-done(((f32[12,256,256]{2,1,0:T(8,128)}), f32[3,256,256]{2,1,0:T(8,128)}) %reduce-scatter.2.cloned.1.call-update) | async-done | bytes 786448 | tf_op jit(solution)/shard_map/reduce_scatter | solution.py:60
  (232 shorter events, 111.6 us)
Async XLA Ops:
  6.5 354.3 %reduce-scatter.2.cloned.1.call-start = ((), (), s32[]{:S(2)}) async-start(), calls=%async_computation.1 | async-start | bytes 3932160 | tf_op jit(solution)/shard_map/reduce_scatter | solution.py:60
  11.4 26.7 %collective-permute-start = (bf16[4,256,256]{2,1,0:T(8,128)(2,1)S(1)}, bf16[4,256,256]{2,1,0:T(8,128)(2,1)}, u32[]{:S(2)}, u32[]{:S(2)}) collective-permute-start(bf16[4,256,256]{2,1,0:T(8,128)(2,1)S(1)} %copy.48), channel_id=1, source_target_pairs={{0,480},{32,0},{64,32},{96,64},{128,96},{160,128},{192,160},{224,1... | collective-permute-start | bytes 1572872 | tf_op jit(solution)/shard_map/while/body/eval_jaxpr/ppermute | solution.py:10
  18.3 18.8 %collective-permute-start.1 = (s32[4]{0:T(128)S(1)}, s32[4]{0:T(128)S(1)}, u32[]{:S(2)}, u32[]{:S(2)}) collective-permute-start(s32[4]{0:T(128)S(1)} %copy.49), channel_id=1, source_target_pairs={{0,480},{32,0},{64,32},{96,64},{128,96},{160,128},{192,160},{224,1... | collective-permute-start | bytes 56 | tf_op jit(solution)/shard_map/while/body/eval_jaxpr/ppermute | solution.py:10
  19.4 18.8 %collective-permute-start.2 = (bf16[2,2,256,256]{3,2,1,0:T(8,128)(2,1)S(1)}, bf16[2,2,256,256]{3,2,1,0:T(8,128)(2,1)}, u32[]{:S(2)}, u32[]{:S(2)}) collective-permute-start(bf16[2,2,256,256]{3,2,1,0:T(8,128)(2,1)S(1)} %copy.50), channel_id=1, source_target_pairs={{0,28},{4,0},{8,4},{12,8},{16,12},{20,16},{24,20},{28,24},{1,29},{... | collective-permute-start | bytes 1572872 | tf_op jit(solution)/shard_map/while/body/eval_jaxpr/ppermute | solution.py:10
  27.6 10.6 %collective-permute-start.3 = (s32[2,2]{1,0:T(2,128)S(1)}, s32[2,2]{1,0:T(2,128)S(1)}, u32[]{:S(2)}, u32[]{:S(2)}) collective-permute-start(s32[2,2]{1,0:T(2,128)S(1)} %copy.51), channel_id=1, source_target_pairs={{0,28},{4,0},{8,4},{12,8},{16,12},{20,16},{24,20},{28,24},{1,29},{... | collective-permute-start | bytes 56 | tf_op jit(solution)/shard_map/while/body/eval_jaxpr/ppermute | solution.py:10
  39.2 18.2 %collective-permute-start = (bf16[4,256,256]{2,1,0:T(8,128)(2,1)S(1)}, bf16[4,256,256]{2,1,0:T(8,128)(2,1)}, u32[]{:S(2)}, u32[]{:S(2)}) collective-permute-start(bf16[4,256,256]{2,1,0:T(8,128)(2,1)S(1)} %copy.48), channel_id=1, source_target_pairs={{0,480},{32,0},{64,32},{96,64},{128,96},{160,128},{192,160},{224,1... | collective-permute-start | bytes 1572872 | tf_op jit(solution)/shard_map/while/body/eval_jaxpr/ppermute | solution.py:10
  40.8 16.6 %collective-permute-start.1 = (s32[4]{0:T(128)S(1)}, s32[4]{0:T(128)S(1)}, u32[]{:S(2)}, u32[]{:S(2)}) collective-permute-start(s32[4]{0:T(128)S(1)} %copy.49), channel_id=1, source_target_pairs={{0,480},{32,0},{64,32},{96,64},{128,96},{160,128},{192,160},{224,1... | collective-permute-start | bytes 56 | tf_op jit(solution)/shard_map/while/body/eval_jaxpr/ppermute | solution.py:10
  41.8 15.6 %collective-permute-start.2 = (bf16[2,2,256,256]{3,2,1,0:T(8,128)(2,1)S(1)}, bf16[2,2,256,256]{3,2,1,0:T(8,128)(2,1)}, u32[]{:S(2)}, u32[]{:S(2)}) collective-permute-start(bf16[2,2,256,256]{3,2,1,0:T(8,128)(2,1)S(1)} %copy.50), channel_id=1, source_target_pairs={{0,28},{4,0},{8,4},{12,8},{16,12},{20,16},{24,20},{28,24},{1,29},{... | collective-permute-start | bytes 1572872 | tf_op jit(solution)/shard_map/while/body/eval_jaxpr/ppermute | solution.py:10
  58.5 18.6 %collective-permute-start = (bf16[4,256,256]{2,1,0:T(8,128)(2,1)S(1)}, bf16[4,256,256]{2,1,0:T(8,128)(2,1)}, u32[]{:S(2)}, u32[]{:S(2)}) collective-permute-start(bf16[4,256,256]{2,1,0:T(8,128)(2,1)S(1)} %copy.48), channel_id=1, source_target_pairs={{0,480},{32,0},{64,32},{96,64},{128,96},{160,128},{192,160},{224,1... | collective-permute-start | bytes 1572872 | tf_op jit(solution)/shard_map/while/body/eval_jaxpr/ppermute | solution.py:10
  60.4 16.6 %collective-permute-start.1 = (s32[4]{0:T(128)S(1)}, s32[4]{0:T(128)S(1)}, u32[]{:S(2)}, u32[]{:S(2)}) collective-permute-start(s32[4]{0:T(128)S(1)} %copy.49), channel_id=1, source_target_pairs={{0,480},{32,0},{64,32},{96,64},{128,96},{160,128},{192,160},{224,1... | collective-permute-start | bytes 56 | tf_op jit(solution)/shard_map/while/body/eval_jaxpr/ppermute | solution.py:10
  61.5 15.6 %collective-permute-start.2 = (bf16[2,2,256,256]{3,2,1,0:T(8,128)(2,1)S(1)}, bf16[2,2,256,256]{3,2,1,0:T(8,128)(2,1)}, u32[]{:S(2)}, u32[]{:S(2)}) collective-permute-start(bf16[2,2,256,256]{3,2,1,0:T(8,128)(2,1)S(1)} %copy.50), channel_id=1, source_target_pairs={{0,28},{4,0},{8,4},{12,8},{16,12},{20,16},{24,20},{28,24},{1,29},{... | collective-permute-start | bytes 1572872 | tf_op jit(solution)/shard_map/while/body/eval_jaxpr/ppermute | solution.py:10
  78.1 18.6 %collective-permute-start = (bf16[4,256,256]{2,1,0:T(8,128)(2,1)S(1)}, bf16[4,256,256]{2,1,0:T(8,128)(2,1)}, u32[]{:S(2)}, u32[]{:S(2)}) collective-permute-start(bf16[4,256,256]{2,1,0:T(8,128)(2,1)S(1)} %copy.48), channel_id=1, source_target_pairs={{0,480},{32,0},{64,32},{96,64},{128,96},{160,128},{192,160},{224,1... | collective-permute-start | bytes 1572872 | tf_op jit(solution)/shard_map/while/body/eval_jaxpr/ppermute | solution.py:10
  80.1 16.6 %collective-permute-start.1 = (s32[4]{0:T(128)S(1)}, s32[4]{0:T(128)S(1)}, u32[]{:S(2)}, u32[]{:S(2)}) collective-permute-start(s32[4]{0:T(128)S(1)} %copy.49), channel_id=1, source_target_pairs={{0,480},{32,0},{64,32},{96,64},{128,96},{160,128},{192,160},{224,1... | collective-permute-start | bytes 56 | tf_op jit(solution)/shard_map/while/body/eval_jaxpr/ppermute | solution.py:10
  81.1 15.6 %collective-permute-start.2 = (bf16[2,2,256,256]{3,2,1,0:T(8,128)(2,1)S(1)}, bf16[2,2,256,256]{3,2,1,0:T(8,128)(2,1)}, u32[]{:S(2)}, u32[]{:S(2)}) collective-permute-start(bf16[2,2,256,256]{3,2,1,0:T(8,128)(2,1)S(1)} %copy.50), channel_id=1, source_target_pairs={{0,28},{4,0},{8,4},{12,8},{16,12},{20,16},{24,20},{28,24},{1,29},{... | collective-permute-start | bytes 1572872 | tf_op jit(solution)/shard_map/while/body/eval_jaxpr/ppermute | solution.py:10
  97.8 18.6 %collective-permute-start = (bf16[4,256,256]{2,1,0:T(8,128)(2,1)S(1)}, bf16[4,256,256]{2,1,0:T(8,128)(2,1)}, u32[]{:S(2)}, u32[]{:S(2)}) collective-permute-start(bf16[4,256,256]{2,1,0:T(8,128)(2,1)S(1)} %copy.48), channel_id=1, source_target_pairs={{0,480},{32,0},{64,32},{96,64},{128,96},{160,128},{192,160},{224,1... | collective-permute-start | bytes 1572872 | tf_op jit(solution)/shard_map/while/body/eval_jaxpr/ppermute | solution.py:10
  99.7 16.6 %collective-permute-start.1 = (s32[4]{0:T(128)S(1)}, s32[4]{0:T(128)S(1)}, u32[]{:S(2)}, u32[]{:S(2)}) collective-permute-start(s32[4]{0:T(128)S(1)} %copy.49), channel_id=1, source_target_pairs={{0,480},{32,0},{64,32},{96,64},{128,96},{160,128},{192,160},{224,1... | collective-permute-start | bytes 56 | tf_op jit(solution)/shard_map/while/body/eval_jaxpr/ppermute | solution.py:10
  100.8 15.6 %collective-permute-start.2 = (bf16[2,2,256,256]{3,2,1,0:T(8,128)(2,1)S(1)}, bf16[2,2,256,256]{3,2,1,0:T(8,128)(2,1)}, u32[]{:S(2)}, u32[]{:S(2)}) collective-permute-start(bf16[2,2,256,256]{3,2,1,0:T(8,128)(2,1)S(1)} %copy.50), channel_id=1, source_target_pairs={{0,28},{4,0},{8,4},{12,8},{16,12},{20,16},{24,20},{28,24},{1,29},{... | collective-permute-start | bytes 1572872 | tf_op jit(solution)/shard_map/while/body/eval_jaxpr/ppermute | solution.py:10
  117.4 18.6 %collective-permute-start = (bf16[4,256,256]{2,1,0:T(8,128)(2,1)S(1)}, bf16[4,256,256]{2,1,0:T(8,128)(2,1)}, u32[]{:S(2)}, u32[]{:S(2)}) collective-permute-start(bf16[4,256,256]{2,1,0:T(8,128)(2,1)S(1)} %copy.48), channel_id=1, source_target_pairs={{0,480},{32,0},{64,32},{96,64},{128,96},{160,128},{192,160},{224,1... | collective-permute-start | bytes 1572872 | tf_op jit(solution)/shard_map/while/body/eval_jaxpr/ppermute | solution.py:10
  119.4 16.6 %collective-permute-start.1 = (s32[4]{0:T(128)S(1)}, s32[4]{0:T(128)S(1)}, u32[]{:S(2)}, u32[]{:S(2)}) collective-permute-start(s32[4]{0:T(128)S(1)} %copy.49), channel_id=1, source_target_pairs={{0,480},{32,0},{64,32},{96,64},{128,96},{160,128},{192,160},{224,1... | collective-permute-start | bytes 56 | tf_op jit(solution)/shard_map/while/body/eval_jaxpr/ppermute | solution.py:10
  120.4 15.6 %collective-permute-start.2 = (bf16[2,2,256,256]{3,2,1,0:T(8,128)(2,1)S(1)}, bf16[2,2,256,256]{3,2,1,0:T(8,128)(2,1)}, u32[]{:S(2)}, u32[]{:S(2)}) collective-permute-start(bf16[2,2,256,256]{3,2,1,0:T(8,128)(2,1)S(1)} %copy.50), channel_id=1, source_target_pairs={{0,28},{4,0},{8,4},{12,8},{16,12},{20,16},{24,20},{28,24},{1,29},{... | collective-permute-start | bytes 1572872 | tf_op jit(solution)/shard_map/while/body/eval_jaxpr/ppermute | solution.py:10
  137.1 18.6 %collective-permute-start = (bf16[4,256,256]{2,1,0:T(8,128)(2,1)S(1)}, bf16[4,256,256]{2,1,0:T(8,128)(2,1)}, u32[]{:S(2)}, u32[]{:S(2)}) collective-permute-start(bf16[4,256,256]{2,1,0:T(8,128)(2,1)S(1)} %copy.48), channel_id=1, source_target_pairs={{0,480},{32,0},{64,32},{96,64},{128,96},{160,128},{192,160},{224,1... | collective-permute-start | bytes 1572872 | tf_op jit(solution)/shard_map/while/body/eval_jaxpr/ppermute | solution.py:10
  139.0 16.6 %collective-permute-start.1 = (s32[4]{0:T(128)S(1)}, s32[4]{0:T(128)S(1)}, u32[]{:S(2)}, u32[]{:S(2)}) collective-permute-start(s32[4]{0:T(128)S(1)} %copy.49), channel_id=1, source_target_pairs={{0,480},{32,0},{64,32},{96,64},{128,96},{160,128},{192,160},{224,1... | collective-permute-start | bytes 56 | tf_op jit(solution)/shard_map/while/body/eval_jaxpr/ppermute | solution.py:10
  140.1 15.6 %collective-permute-start.2 = (bf16[2,2,256,256]{3,2,1,0:T(8,128)(2,1)S(1)}, bf16[2,2,256,256]{3,2,1,0:T(8,128)(2,1)}, u32[]{:S(2)}, u32[]{:S(2)}) collective-permute-start(bf16[2,2,256,256]{3,2,1,0:T(8,128)(2,1)S(1)} %copy.50), channel_id=1, source_target_pairs={{0,28},{4,0},{8,4},{12,8},{16,12},{20,16},{24,20},{28,24},{1,29},{... | collective-permute-start | bytes 1572872 | tf_op jit(solution)/shard_map/while/body/eval_jaxpr/ppermute | solution.py:10
  156.7 18.6 %collective-permute-start = (bf16[4,256,256]{2,1,0:T(8,128)(2,1)S(1)}, bf16[4,256,256]{2,1,0:T(8,128)(2,1)}, u32[]{:S(2)}, u32[]{:S(2)}) collective-permute-start(bf16[4,256,256]{2,1,0:T(8,128)(2,1)S(1)} %copy.48), channel_id=1, source_target_pairs={{0,480},{32,0},{64,32},{96,64},{128,96},{160,128},{192,160},{224,1... | collective-permute-start | bytes 1572872 | tf_op jit(solution)/shard_map/while/body/eval_jaxpr/ppermute | solution.py:10
  158.7 16.6 %collective-permute-start.1 = (s32[4]{0:T(128)S(1)}, s32[4]{0:T(128)S(1)}, u32[]{:S(2)}, u32[]{:S(2)}) collective-permute-start(s32[4]{0:T(128)S(1)} %copy.49), channel_id=1, source_target_pairs={{0,480},{32,0},{64,32},{96,64},{128,96},{160,128},{192,160},{224,1... | collective-permute-start | bytes 56 | tf_op jit(solution)/shard_map/while/body/eval_jaxpr/ppermute | solution.py:10
  159.7 15.6 %collective-permute-start.2 = (bf16[2,2,256,256]{3,2,1,0:T(8,128)(2,1)S(1)}, bf16[2,2,256,256]{3,2,1,0:T(8,128)(2,1)}, u32[]{:S(2)}, u32[]{:S(2)}) collective-permute-start(bf16[2,2,256,256]{3,2,1,0:T(8,128)(2,1)S(1)} %copy.50), channel_id=1, source_target_pairs={{0,28},{4,0},{8,4},{12,8},{16,12},{20,16},{24,20},{28,24},{1,29},{... | collective-permute-start | bytes 1572872 | tf_op jit(solution)/shard_map/while/body/eval_jaxpr/ppermute | solution.py:10
  165.1 10.2 %collective-permute-start.3 = (s32[2,2]{1,0:T(2,128)S(1)}, s32[2,2]{1,0:T(2,128)S(1)}, u32[]{:S(2)}, u32[]{:S(2)}) collective-permute-start(s32[2,2]{1,0:T(2,128)S(1)} %copy.51), channel_id=1, source_target_pairs={{0,28},{4,0},{8,4},{12,8},{16,12},{20,16},{24,20},{28,24},{1,29},{... | collective-permute-start | bytes 56 | tf_op jit(solution)/shard_map/while/body/eval_jaxpr/ppermute | solution.py:10
  176.4 18.6 %collective-permute-start = (bf16[4,256,256]{2,1,0:T(8,128)(2,1)S(1)}, bf16[4,256,256]{2,1,0:T(8,128)(2,1)}, u32[]{:S(2)}, u32[]{:S(2)}) collective-permute-start(bf16[4,256,256]{2,1,0:T(8,128)(2,1)S(1)} %copy.48), channel_id=1, source_target_pairs={{0,480},{32,0},{64,32},{96,64},{128,96},{160,128},{192,160},{224,1... | collective-permute-start | bytes 1572872 | tf_op jit(solution)/shard_map/while/body/eval_jaxpr/ppermute | solution.py:10
  178.3 16.6 %collective-permute-start.1 = (s32[4]{0:T(128)S(1)}, s32[4]{0:T(128)S(1)}, u32[]{:S(2)}, u32[]{:S(2)}) collective-permute-start(s32[4]{0:T(128)S(1)} %copy.49), channel_id=1, source_target_pairs={{0,480},{32,0},{64,32},{96,64},{128,96},{160,128},{192,160},{224,1... | collective-permute-start | bytes 56 | tf_op jit(solution)/shard_map/while/body/eval_jaxpr/ppermute | solution.py:10
  179.4 15.6 %collective-permute-start.2 = (bf16[2,2,256,256]{3,2,1,0:T(8,128)(2,1)S(1)}, bf16[2,2,256,256]{3,2,1,0:T(8,128)(2,1)}, u32[]{:S(2)}, u32[]{:S(2)}) collective-permute-start(bf16[2,2,256,256]{3,2,1,0:T(8,128)(2,1)S(1)} %copy.50), channel_id=1, source_target_pairs={{0,28},{4,0},{8,4},{12,8},{16,12},{20,16},{24,20},{28,24},{1,29},{... | collective-permute-start | bytes 1572872 | tf_op jit(solution)/shard_map/while/body/eval_jaxpr/ppermute | solution.py:10
  196.0 18.6 %collective-permute-start = (bf16[4,256,256]{2,1,0:T(8,128)(2,1)S(1)}, bf16[4,256,256]{2,1,0:T(8,128)(2,1)}, u32[]{:S(2)}, u32[]{:S(2)}) collective-permute-start(bf16[4,256,256]{2,1,0:T(8,128)(2,1)S(1)} %copy.48), channel_id=1, source_target_pairs={{0,480},{32,0},{64,32},{96,64},{128,96},{160,128},{192,160},{224,1... | collective-permute-start | bytes 1572872 | tf_op jit(solution)/shard_map/while/body/eval_jaxpr/ppermute | solution.py:10
  198.0 16.6 %collective-permute-start.1 = (s32[4]{0:T(128)S(1)}, s32[4]{0:T(128)S(1)}, u32[]{:S(2)}, u32[]{:S(2)}) collective-permute-start(s32[4]{0:T(128)S(1)} %copy.49), channel_id=1, source_target_pairs={{0,480},{32,0},{64,32},{96,64},{128,96},{160,128},{192,160},{224,1... | collective-permute-start | bytes 56 | tf_op jit(solution)/shard_map/while/body/eval_jaxpr/ppermute | solution.py:10
  199.0 15.6 %collective-permute-start.2 = (bf16[2,2,256,256]{3,2,1,0:T(8,128)(2,1)S(1)}, bf16[2,2,256,256]{3,2,1,0:T(8,128)(2,1)}, u32[]{:S(2)}, u32[]{:S(2)}) collective-permute-start(bf16[2,2,256,256]{3,2,1,0:T(8,128)(2,1)S(1)} %copy.50), channel_id=1, source_target_pairs={{0,28},{4,0},{8,4},{12,8},{16,12},{20,16},{24,20},{28,24},{1,29},{... | collective-permute-start | bytes 1572872 | tf_op jit(solution)/shard_map/while/body/eval_jaxpr/ppermute | solution.py:10
  215.7 18.6 %collective-permute-start = (bf16[4,256,256]{2,1,0:T(8,128)(2,1)S(1)}, bf16[4,256,256]{2,1,0:T(8,128)(2,1)}, u32[]{:S(2)}, u32[]{:S(2)}) collective-permute-start(bf16[4,256,256]{2,1,0:T(8,128)(2,1)S(1)} %copy.48), channel_id=1, source_target_pairs={{0,480},{32,0},{64,32},{96,64},{128,96},{160,128},{192,160},{224,1... | collective-permute-start | bytes 1572872 | tf_op jit(solution)/shard_map/while/body/eval_jaxpr/ppermute | solution.py:10
  217.6 16.6 %collective-permute-start.1 = (s32[4]{0:T(128)S(1)}, s32[4]{0:T(128)S(1)}, u32[]{:S(2)}, u32[]{:S(2)}) collective-permute-start(s32[4]{0:T(128)S(1)} %copy.49), channel_id=1, source_target_pairs={{0,480},{32,0},{64,32},{96,64},{128,96},{160,128},{192,160},{224,1... | collective-permute-start | bytes 56 | tf_op jit(solution)/shard_map/while/body/eval_jaxpr/ppermute | solution.py:10
  218.7 15.6 %collective-permute-start.2 = (bf16[2,2,256,256]{3,2,1,0:T(8,128)(2,1)S(1)}, bf16[2,2,256,256]{3,2,1,0:T(8,128)(2,1)}, u32[]{:S(2)}, u32[]{:S(2)}) collective-permute-start(bf16[2,2,256,256]{3,2,1,0:T(8,128)(2,1)S(1)} %copy.50), channel_id=1, source_target_pairs={{0,28},{4,0},{8,4},{12,8},{16,12},{20,16},{24,20},{28,24},{1,29},{... | collective-permute-start | bytes 1572872 | tf_op jit(solution)/shard_map/while/body/eval_jaxpr/ppermute | solution.py:10
  235.3 18.6 %collective-permute-start = (bf16[4,256,256]{2,1,0:T(8,128)(2,1)S(1)}, bf16[4,256,256]{2,1,0:T(8,128)(2,1)}, u32[]{:S(2)}, u32[]{:S(2)}) collective-permute-start(bf16[4,256,256]{2,1,0:T(8,128)(2,1)S(1)} %copy.48), channel_id=1, source_target_pairs={{0,480},{32,0},{64,32},{96,64},{128,96},{160,128},{192,160},{224,1... | collective-permute-start | bytes 1572872 | tf_op jit(solution)/shard_map/while/body/eval_jaxpr/ppermute | solution.py:10
  237.3 16.6 %collective-permute-start.1 = (s32[4]{0:T(128)S(1)}, s32[4]{0:T(128)S(1)}, u32[]{:S(2)}, u32[]{:S(2)}) collective-permute-start(s32[4]{0:T(128)S(1)} %copy.49), channel_id=1, source_target_pairs={{0,480},{32,0},{64,32},{96,64},{128,96},{160,128},{192,160},{224,1... | collective-permute-start | bytes 56 | tf_op jit(solution)/shard_map/while/body/eval_jaxpr/ppermute | solution.py:10
  238.3 15.6 %collective-permute-start.2 = (bf16[2,2,256,256]{3,2,1,0:T(8,128)(2,1)S(1)}, bf16[2,2,256,256]{3,2,1,0:T(8,128)(2,1)}, u32[]{:S(2)}, u32[]{:S(2)}) collective-permute-start(bf16[2,2,256,256]{3,2,1,0:T(8,128)(2,1)S(1)} %copy.50), channel_id=1, source_target_pairs={{0,28},{4,0},{8,4},{12,8},{16,12},{20,16},{24,20},{28,24},{1,29},{... | collective-permute-start | bytes 1572872 | tf_op jit(solution)/shard_map/while/body/eval_jaxpr/ppermute | solution.py:10
  255.0 18.6 %collective-permute-start = (bf16[4,256,256]{2,1,0:T(8,128)(2,1)S(1)}, bf16[4,256,256]{2,1,0:T(8,128)(2,1)}, u32[]{:S(2)}, u32[]{:S(2)}) collective-permute-start(bf16[4,256,256]{2,1,0:T(8,128)(2,1)S(1)} %copy.48), channel_id=1, source_target_pairs={{0,480},{32,0},{64,32},{96,64},{128,96},{160,128},{192,160},{224,1... | collective-permute-start | bytes 1572872 | tf_op jit(solution)/shard_map/while/body/eval_jaxpr/ppermute | solution.py:10
  256.9 16.6 %collective-permute-start.1 = (s32[4]{0:T(128)S(1)}, s32[4]{0:T(128)S(1)}, u32[]{:S(2)}, u32[]{:S(2)}) collective-permute-start(s32[4]{0:T(128)S(1)} %copy.49), channel_id=1, source_target_pairs={{0,480},{32,0},{64,32},{96,64},{128,96},{160,128},{192,160},{224,1... | collective-permute-start | bytes 56 | tf_op jit(solution)/shard_map/while/body/eval_jaxpr/ppermute | solution.py:10
  257.9 15.6 %collective-permute-start.2 = (bf16[2,2,256,256]{3,2,1,0:T(8,128)(2,1)S(1)}, bf16[2,2,256,256]{3,2,1,0:T(8,128)(2,1)}, u32[]{:S(2)}, u32[]{:S(2)}) collective-permute-start(bf16[2,2,256,256]{3,2,1,0:T(8,128)(2,1)S(1)} %copy.50), channel_id=1, source_target_pairs={{0,28},{4,0},{8,4},{12,8},{16,12},{20,16},{24,20},{28,24},{1,29},{... | collective-permute-start | bytes 1572872 | tf_op jit(solution)/shard_map/while/body/eval_jaxpr/ppermute | solution.py:10
  274.6 18.6 %collective-permute-start = (bf16[4,256,256]{2,1,0:T(8,128)(2,1)S(1)}, bf16[4,256,256]{2,1,0:T(8,128)(2,1)}, u32[]{:S(2)}, u32[]{:S(2)}) collective-permute-start(bf16[4,256,256]{2,1,0:T(8,128)(2,1)S(1)} %copy.48), channel_id=1, source_target_pairs={{0,480},{32,0},{64,32},{96,64},{128,96},{160,128},{192,160},{224,1... | collective-permute-start | bytes 1572872 | tf_op jit(solution)/shard_map/while/body/eval_jaxpr/ppermute | solution.py:10
  276.5 16.6 %collective-permute-start.1 = (s32[4]{0:T(128)S(1)}, s32[4]{0:T(128)S(1)}, u32[]{:S(2)}, u32[]{:S(2)}) collective-permute-start(s32[4]{0:T(128)S(1)} %copy.49), channel_id=1, source_target_pairs={{0,480},{32,0},{64,32},{96,64},{128,96},{160,128},{192,160},{224,1... | collective-permute-start | bytes 56 | tf_op jit(solution)/shard_map/while/body/eval_jaxpr/ppermute | solution.py:10
  277.6 15.6 %collective-permute-start.2 = (bf16[2,2,256,256]{3,2,1,0:T(8,128)(2,1)S(1)}, bf16[2,2,256,256]{3,2,1,0:T(8,128)(2,1)}, u32[]{:S(2)}, u32[]{:S(2)}) collective-permute-start(bf16[2,2,256,256]{3,2,1,0:T(8,128)(2,1)S(1)} %copy.50), channel_id=1, source_target_pairs={{0,28},{4,0},{8,4},{12,8},{16,12},{20,16},{24,20},{28,24},{1,29},{... | collective-permute-start | bytes 1572872 | tf_op jit(solution)/shard_map/while/body/eval_jaxpr/ppermute | solution.py:10
  294.3 18.6 %collective-permute-start = (bf16[4,256,256]{2,1,0:T(8,128)(2,1)S(1)}, bf16[4,256,256]{2,1,0:T(8,128)(2,1)}, u32[]{:S(2)}, u32[]{:S(2)}) collective-permute-start(bf16[4,256,256]{2,1,0:T(8,128)(2,1)S(1)} %copy.48), channel_id=1, source_target_pairs={{0,480},{32,0},{64,32},{96,64},{128,96},{160,128},{192,160},{224,1... | collective-permute-start | bytes 1572872 | tf_op jit(solution)/shard_map/while/body/eval_jaxpr/ppermute | solution.py:10
  296.2 16.6 %collective-permute-start.1 = (s32[4]{0:T(128)S(1)}, s32[4]{0:T(128)S(1)}, u32[]{:S(2)}, u32[]{:S(2)}) collective-permute-start(s32[4]{0:T(128)S(1)} %copy.49), channel_id=1, source_target_pairs={{0,480},{32,0},{64,32},{96,64},{128,96},{160,128},{192,160},{224,1... | collective-permute-start | bytes 56 | tf_op jit(solution)/shard_map/while/body/eval_jaxpr/ppermute | solution.py:10
  297.2 15.6 %collective-permute-start.2 = (bf16[2,2,256,256]{3,2,1,0:T(8,128)(2,1)S(1)}, bf16[2,2,256,256]{3,2,1,0:T(8,128)(2,1)}, u32[]{:S(2)}, u32[]{:S(2)}) collective-permute-start(bf16[2,2,256,256]{3,2,1,0:T(8,128)(2,1)S(1)} %copy.50), channel_id=1, source_target_pairs={{0,28},{4,0},{8,4},{12,8},{16,12},{20,16},{24,20},{28,24},{1,29},{... | collective-permute-start | bytes 1572872 | tf_op jit(solution)/shard_map/while/body/eval_jaxpr/ppermute | solution.py:10
  (19 other events, 192.1 us)
Sparse Core Ops, SparseCore 0:
  319.5 41.3 reduce-scatter.1
where the time goes:
time: 372 us; the launch traced here: 370 us
  starting transfers between devices  146 us (39%)
  matrix products  127 us (34%)
  waiting for transfers between devices  42.7 us (11%)
  local copies, waits for them, and re-layouts  36.6 us (10%)
  between operations  13.5 us (4%)
    ppermute x60, starting transfers between devices, passed_along(): return lax.ppermute(value, axis, pairs)  146 us
    dot_general x16, matrix products, contribute(): jnp.einsum('sxy,syz->sxz', chosen_a, chosen_b, preferred_element_type=jnp...  81.4 us
    reduce_scatter x1, waiting for transfers between devices, body(): shares = lax.psum_scatter(total, 'depth', scatter_dimension=0, tiled=True)  41.5 us
    dot_general x16, matrix products, contribute(): jnp.einsum('sb,bxy->sxy', pick_b, blocks_b, preferred_element_type=jnp.fl...  32.3 us
    while x60, local copies, waits for them, and re-layouts  31.3 us
    dot_general x16, matrix products, contribute(): jnp.einsum('sa,axy->sxy', pick_a, blocks_a, preferred_element_type=jnp.fl...  13.3 us
  transfers between devices with their start and end apart: 61, of which 2 were waited for; matrix products, arithmetic and copies ran while one was open for 37% of the time, Pallas kernels for 0%

commit v1 on v0

v1 whole, which is shorter than its diff:
```python
import functools

import jax
import jax.numpy as jnp
from jax import lax
from jax.experimental import pallas as pl
from jax.experimental.pallas import tpu as pltpu
from jax.sharding import PartitionSpec as P

GROUP = 4
LEVELS = 32000.0
FINER = 16.0


def lists_kernel(steps, slots, place, rows_all, cols_all, want_rows, want_cols, list_a, list_b, counts, kept):
    held_a, held_b, pieces, tile_rows, tile_cols, owners = steps
    holders = owners * pieces
    my_row, my_col = place[0], place[1]

    def clear(index, carry):
        kept[index] = -1
        return carry

    lax.fori_loop(0, tile_rows * tile_cols, clear, 0)

    def mark(slot, carry):
        kept[want_rows[slot] * tile_cols + want_cols[slot]] = slot
        counts[slot] = 0
        return carry

    lax.fori_loop(0, slots, mark, 0)

    def blank(index, carry):
        list_a[index] = holders * held_a
        list_b[index] = 0
        return carry

    lax.fori_loop(0, slots * holders, blank, 0)

    def visit(step, carry):
        apart = step // pieces
        piece = step % pieces
        owner = lax.rem(my_col + apart, owners)
        holder = lax.rem(my_row + owner - my_col + piece * owners + holders, holders)
        for a in range(held_a):
            row = rows_all[holder * held_a + a]
            for b in range(held_b):
                col = cols_all[(owner * pieces + piece) * held_b + b]
                slot = kept[row * tile_cols + col]

                @pl.when(slot >= 0)
                def _():
                    count = counts[slot]
                    list_a[slot * holders + count] = holder * held_a + a
                    list_b[slot * holders + count] = step * held_b + b
                    counts[slot] = count + 1

        return carry

    lax.fori_loop(0, holders, visit, 0)


def product_kernel(slots, holders, shares, list_a, list_b, counts, a_all, *rest):
    parts, (coded, total, a_here, b_here, a_sem, b_sem) = rest[:-6], rest[-6:]
    blk = a_all.shape[1]
    each = slots // shares
    count_a = a_all.shape[0]
    copy_a = pltpu.make_async_copy(a_all, a_here.at[pl.ds(0, count_a)], a_sem)
    copy_a.start()
    copies = []
    at = 0
    for index, part in enumerate(parts):
        size = part.shape[0]
        copies.append(pltpu.make_async_copy(part, b_here.at[pl.ds(at, size)], b_sem.at[index]))
        copies[-1].start()
        at += size
    a_here[count_a] = jnp.zeros(a_here.shape[1:], a_here.dtype)
    for copy in copies:
        copy.wait()
    copy_a.wait()

    def grouped(slot, group):
        first = slot * holders + group * GROUP
        left = jnp.concatenate([a_here[list_a[first + n]] for n in range(GROUP)], axis=1)
        right = jnp.concatenate([b_here[list_b[first + n]] for n in range(GROUP)], axis=0)
        return jnp.dot(left, right, preferred_element_type=jnp.float32)

    def one_slot(slot, carry):
        total[...] = grouped(slot, 0)

        def one_group(group, inner):
            total[...] += grouped(slot, group)
            return inner

        lax.fori_loop(1, (counts[slot] + GROUP - 1) // GROUP, one_group, 0)
        largest = jnp.maximum(jnp.max(jnp.abs(total[...]), axis=0, keepdims=True), 1e-30)
        power = jnp.ceil(FINER * jnp.log2(largest / LEVELS))
        share, inside = slot // each, lax.rem(slot, each)
        values = jnp.round(total[...] * jnp.exp2(power * (-1.0 / FINER)))
        coded[share, pl.ds(pl.multiple_of(inside * blk, blk), blk), :] = values.astype(jnp.int32).astype(jnp.int16)
        powers = jnp.broadcast_to(power, (16, blk)).astype(jnp.int32).astype(jnp.int16)
        coded[share, pl.ds(pl.multiple_of(each * blk + inside * 16, 16), 16), :] = powers
        return carry

    lax.fori_loop(0, slots, one_slot, 0)


def finish_kernel(coded, square_kept, out):
    shares = coded.shape[0]
    each, blk = square_kept.shape[0], square_kept.shape[1]
    for slot in range(each):
        cube = jnp.zeros((blk, blk), jnp.float32)
        for share in range(shares):
            power = coded[share, pl.ds(each * blk + slot * 16, 16), :].astype(jnp.int32).astype(jnp.float32)[:1]
            values = coded[share, pl.ds(slot * blk, blk), :].astype(jnp.int32).astype(jnp.float32)
            cube = cube + values * jnp.exp2(power * (1.0 / FINER))
        out[slot] = (3.0 * square_kept[slot].astype(jnp.float32) - 2.0 * cube).astype(out.dtype)


def shifted(value, axis, steps):
    count = lax.axis_size(axis)
    return lax.ppermute(value, axis, [(source, (source + steps) % count) for source in range(count)])


def body(density_tiles, density_rows, square_tiles, square_cols, keep_rows, keep_cols, square_kept):
    n_row, n_col, n_depth = lax.axis_size("row"), lax.axis_size("col"), lax.axis_size("depth")
    tile_a = density_tiles[0, 0, 0]
    pieces, held_b, blk = square_tiles.shape[3], square_tiles.shape[4], square_tiles.shape[5]
    held_a = tile_a.shape[0]
    tile_b = square_tiles[0, 0, 0].reshape(pieces * held_b, blk, blk)
    slots = keep_rows.shape[-1]
    half = n_col // 2
    cut = tile_b.shape[0] // 2

    a_all = lax.all_gather(tile_a, "row", axis=0, tiled=True)

    my_rows, my_cols = density_rows[0, 0, 0], square_cols[0, 0, 0].reshape(-1)
    rows_all = lax.all_to_all(jnp.tile(my_rows, (n_row, 1)), "row", 0, 0, tiled=True).reshape(-1)
    cols_all = lax.all_to_all(jnp.tile(my_cols, (n_col, 1)), "col", 0, 0, tiled=True).reshape(-1)

    up = [tile_b]
    down = [tile_b]
    for step in range(1, half + 1):
        send_up, send_down = up[-1], down[-1]
        if step == 2:
            send_up, send_down, rows_all = lax.optimization_barrier((send_up, send_down, rows_all))
        if step == 3:
            send_up, send_down, cols_all = lax.optimization_barrier((send_up, send_down, cols_all))
        if step == half:
            send_up, send_down = send_up[:cut], send_down[cut:]
        up.append(shifted(send_up, "col", 1))
        down.append(shifted(send_down, "col", -1))
    parts = down[:half] + [up[half], down[half]] + up[1:half][::-1]

    place = jnp.stack([lax.axis_index("row"), lax.axis_index("col")]).astype(jnp.int32)

    tile_rows, tile_cols = 8, 4
    smem = pl.BlockSpec(memory_space=pltpu.SMEM)
    steps = (held_a, held_b, pieces, tile_rows, tile_cols, n_col)
    list_a, list_b, counts = pl.pallas_call(
        functools.partial(lists_kernel, steps, slots),
        out_shape=[
            jax.ShapeDtypeStruct((slots * n_row,), jnp.int32),
            jax.ShapeDtypeStruct((slots * n_row,), jnp.int32),
            jax.ShapeDtypeStruct((slots,), jnp.int32),
        ],
        in_specs=[smem] * 5,
        out_specs=[smem] * 3,
        scratch_shapes=[pltpu.SMEM((tile_rows * tile_cols,), jnp.int32)],
        name="lists",
    )(place, rows_all, cols_all, keep_rows[0, 0], keep_cols[0, 0])

    each = slots // n_depth
    coded = pl.pallas_call(
        functools.partial(product_kernel, slots, n_row, n_depth),
        out_shape=jax.ShapeDtypeStruct((n_depth, each * (blk + 16), blk), jnp.int16),
        in_specs=[smem] * 3 + [pl.BlockSpec(memory_space=pl.ANY)] * (1 + len(parts)),
        out_specs=pl.BlockSpec(memory_space=pltpu.VMEM),
        scratch_shapes=[
            pltpu.VMEM((blk, blk), jnp.float32),
            pltpu.VMEM((n_row * held_a + 1, blk, blk), jnp.bfloat16),
            pltpu.VMEM((n_col * pieces * held_b, blk, blk), jnp.bfloat16),
            pltpu.SemaphoreType.DMA,
            pltpu.SemaphoreType.DMA((len(parts),)),
        ],
        compiler_params=pltpu.CompilerParams(vmem_limit_bytes=60 * 1024 * 1024),
        cost_estimate=pl.CostEstimate(flops=2 * 64 * blk**3, bytes_accessed=16 * 2**20, transcendentals=0),
        name="products",
    )(list_a, list_b, counts, a_all, *parts)

    coded = lax.all_to_all(coded, "depth", 0, 0, tiled=True)
    result = pl.pallas_call(
        finish_kernel,
        out_shape=jax.ShapeDtypeStruct((each, blk, blk), jnp.bfloat16),
        compiler_params=pltpu.CompilerParams(vmem_limit_bytes=32 * 1024 * 1024),
        cost_estimate=pl.CostEstimate(flops=2**21, bytes_accessed=3 * 2**20, transcendentals=0),
        name="finish",
    )(coded, square_kept[0, 0])
    return result[None, None]


def solution(mesh):
    placed = (
        P("depth", "row", "col", None, None, None),
        P("depth", "row", "col", None),
        P("depth", "row", "col", None, None, None, None),
        P("depth", "row", "col", None, None),
        P("row", "col", None),
        P("row", "col", None),
        P("row", "col", "depth", None, None),
    )
    return jax.shard_map(
        body,
        mesh=mesh,
        in_specs=placed,
        out_specs=P("row", "col", "depth", None, None),
        check_vma=False,
    )
```

time: 372 us -> 133 us (0.36)
  the two profiles are of different devices: /device:TPU:1 before, /device:TPU:2 now
where the time goes in v1:
time: 133 us
  blocking collectives  47.6 us (36%)
  starting transfers between devices  34.7 us (26%)
  Pallas kernels  17.9 us (13%)
  between operations  13.6 us (10%)
  waiting for transfers between devices  12.4 us (9%)
  local copies, waits for them, and re-layouts  4.84 us (4%)
  other arithmetic  1.89 us (1%)
    ppermute x8, starting transfers between devices, shifted(): lax.ppermute(value, axis, [(source, (source + steps) % count) for source...  34.7 us
    all_to_all x1, blocking collectives, body(): coded = lax.all_to_all(coded, 'depth', 0, 0, tiled=True)  22.2 us
    all_to_all x1, blocking collectives, body(): lax.all_to_all(jnp.tile(my_rows, (n_row, 1)), 'row', 0, 0, tiled=True)  14.6 us
    pallas_call x1, Pallas kernels, body(): pl.pallas_call(functools.partial(product_kernel, slots, n_row, n_depth),...  12.5 us
    ppermute x8, waiting for transfers between devices, shifted(): lax.ppermute(value, axis, [(source, (source + steps) % count) for source...  11.6 us
    all_to_all x1, blocking collectives, body(): lax.all_to_all(jnp.tile(my_cols, (n_col, 1)), 'col', 0, 0, tiled=True)  10.8 us
    pallas_call x1, Pallas kernels, body(): pl.pallas_call(functools.partial(lists_kernel, steps, slots), out_shape=[...  4.06 us
  transfers between devices with their start and end apart: 9, of which 2 were waited for; matrix products, arithmetic and copies ran while one was open for 5% of the time, Pallas kernels for 3%

profile of v1, /device:TPU:2, one launch (start us, length us, event | category | flops | bytes accessed | tf_op | source)
XLA Modules:
  0.0 132.9 jit_solution(4265251321439265461)
XLA Ops:
  6.5 0.0 all-gather.3.cloned.1.call-start
  6.5 0.7 all-gather.3.cloned.1.call-update
  7.3 10.9 %collective-permute-start.1 = (bf16[4,256,256]{2,1,0:T(8,128)(2,1)}, bf16[4,256,256]{2,1,0:T(8,128)(2,1)S(1)}, u32[]{:S(2)}, u32[]{:S(2)}) collective-permute-start(bf16[4,256,256]{2,1,0:T(8,128)(2,1)} %bitcast.12), channel_id=1, source_target_pairs={{0,28},{4,0},{8,4},{12,8},{16,12},{20,16},{24,20},{28,24},{1,29},{... | collective-permute-start | bytes 1572872 | tf_op jit(solution)/shard_map/ppermute | solution.py:122
  18.2 1.9 %collective-permute-start = (bf16[4,256,256]{2,1,0:T(8,128)(2,1)}, bf16[4,256,256]{2,1,0:T(8,128)(2,1)S(1)}, u32[]{:S(2)}, u32[]{:S(2)}) collective-permute-start(bf16[4,256,256]{2,1,0:T(8,128)(2,1)} %bitcast.13), channel_id=1, source_target_pairs={{0,4},{4,8},{8,12},{12,16},{16,20},{20,24},{24,28},{28,0},{1,5},{5... | collective-permute-start | bytes 1572872 | tf_op jit(solution)/shard_map/ppermute | solution.py:122
  20.1 0.7 tile.17
  20.8 14.6 %all_to_all.17 = s32[16,1,4]{2,1,0:T(1,128)S(1)} all-to-all(s32[16,1,4]{2,1,0:T(1,128)S(1)} %tile.17), channel_id=1, replica_groups=mesh['row'=16,'col'=8,'depth'=4] {'row'}, dimensions={0} | all-to-all | bytes 512 | tf_op jit(solution)/shard_map/all_to_all | solution.py:138
  35.4 0.5 broadcast.16
  35.9 0.7 reduce.6
  36.6 0.7 reshape.27.rows_all
  37.2 0.0 collective-permute-done.1.rest_1_
  37.3 0.0 copy-start.3
  37.3 0.0 collective-permute-done.rest_8_
  37.3 0.0 copy-start.4
  37.3 1.9 %collective-permute-start.2 = (bf16[4,256,256]{2,1,0:T(8,128)(2,1)S(1)}, bf16[4,256,256]{2,1,0:T(8,128)(2,1)S(1)}, u32[]{:S(2)}, u32[]{:S(2)}) collective-permute-start(bf16[4,256,256]{2,1,0:T(8,128)(2,1)S(1)} %collective-permute-done.rest_8_), channel_id=1, source_target_pairs={{0,4},{4,8},{8,12},{12,16},{16,20},{20,24},{24,28},{28,0},{1,5},{5... | collective-permute-start | bytes 1572872 | tf_op jit(solution)/shard_map/ppermute | solution.py:122
  39.2 5.1 %collective-permute-start.3 = (bf16[4,256,256]{2,1,0:T(8,128)(2,1)S(1)}, bf16[4,256,256]{2,1,0:T(8,128)(2,1)S(1)}, u32[]{:S(2)}, u32[]{:S(2)}) collective-permute-start(bf16[4,256,256]{2,1,0:T(8,128)(2,1)S(1)} %collective-permute-done.1.rest_1_), channel_id=1, source_target_pairs={{0,28},{4,0},{8,4},{12,8},{16,12},{20,16},{24,20},{28,24},{1,29},{... | collective-permute-start | bytes 1572872 | tf_op jit(solution)/shard_map/ppermute | solution.py:122
  44.3 0.8 tile.18
  45.1 10.8 %all_to_all.18 = s32[8,1,4]{2,1,0:T(1,128)S(1)} all-to-all(s32[8,1,4]{2,1,0:T(1,128)S(1)} %tile.19), channel_id=1, replica_groups=mesh['row'=16,'col'=8,'depth'=4] {'col'}, dimensions={0} | all-to-all | bytes 256 | tf_op jit(solution)/shard_map/all_to_all | solution.py:139
  55.9 0.7 reduce.7
  56.5 0.7 reshape.28.cols_all
  57.2 0.0 collective-permute-done.2.rest_7_
  57.2 0.0 collective-permute-done.3.rest_2_
  57.2 0.0 copy-start.6
  57.2 5.4 %collective-permute-start.4 = (bf16[4,256,256]{2,1,0:T(8,128)(2,1)S(1)}, bf16[4,256,256]{2,1,0:T(8,128)(2,1)S(1)}, u32[]{:S(2)}, u32[]{:S(2)}) collective-permute-start(bf16[4,256,256]{2,1,0:T(8,128)(2,1)S(1)} %collective-permute-done.3.rest_2_), channel_id=1, source_target_pairs={{0,28},{4,0},{8,4},{12,8},{16,12},{20,16},{24,20},{28,24},{1,29},{... | collective-permute-start | bytes 1572872 | tf_op jit(solution)/shard_map/ppermute | solution.py:122
  62.6 1.9 %collective-permute-start.5 = (bf16[4,256,256]{2,1,0:T(8,128)(2,1)S(1)}, bf16[4,256,256]{2,1,0:T(8,128)(2,1)S(1)}, u32[]{:S(2)}, u32[]{:S(2)}) collective-permute-start(bf16[4,256,256]{2,1,0:T(8,128)(2,1)S(1)} %collective-permute-done.2.rest_7_), channel_id=1, source_target_pairs={{0,4},{4,8},{8,12},{12,16},{16,20},{20,24},{24,28},{28,0},{1,5},{5... | collective-permute-start | bytes 1572872 | tf_op jit(solution)/shard_map/ppermute | solution.py:122
  64.5 8.4 %collective-permute-done.4.rest_3_ = bf16[4,256,256]{2,1,0:T(8,128)(2,1)S(1)} collective-permute-done((bf16[4,256,256]{2,1,0:T(8,128)(2,1)S(1)}, bf16[4,256,256]{2,1,0:T(8,128)(2,1)S(1)}, u32[]{:S(2)}, u32[]{:S(2)}) %collective-permute-start.4) | collective-permute-done | bytes 524320 | tf_op jit(solution)/shard_map/ppermute | solution.py:122
  73.0 0.8 slice.9
  73.7 5.6 %collective-permute-start.7 = (bf16[2,256,256]{2,1,0:T(8,128)(2,1)}, bf16[2,256,256]{2,1,0:T(8,128)(2,1)S(1)}, u32[]{:S(2)}, u32[]{:S(2)}) collective-permute-start(bf16[2,256,256]{2,1,0:T(8,128)(2,1)} %slice.9), channel_id=1, source_target_pairs={{0,28},{4,0},{8,4},{12,8},{16,12},{20,16},{24,20},{28,24},{1,29},{... | collective-permute-start | bytes 786440 | tf_op jit(solution)/shard_map/ppermute | solution.py:122
  79.3 0.0 collective-permute-done.5.rest_6_
  79.3 0.0 copy-start.2
  79.4 0.8 slice.8
  80.1 1.9 %collective-permute-start.6 = (bf16[2,256,256]{2,1,0:T(8,128)(2,1)}, bf16[2,256,256]{2,1,0:T(8,128)(2,1)}, u32[]{:S(2)}, u32[]{:S(2)}) collective-permute-start(bf16[2,256,256]{2,1,0:T(8,128)(2,1)} %slice.8), channel_id=1, source_target_pairs={{0,4},{4,8},{8,12},{12,16},{16,20},{20,24},{24,28},{28,0},{1,5},{5... | collective-permute-start | bytes 786440 | tf_op jit(solution)/shard_map/ppermute | solution.py:122
  82.1 0.6 pad_add_fusion.place
  82.6 4.1 %lists.1 = (s32[192]{0:T(256)}, s32[192]{0:T(256)}, s32[12]{0:T(128)}) custom-call(s32[2]{0:T(128)} %pad_add_fusion.place, s32[64]{0:T(128)} %reshape.27.rows_all, s32[32]{0:T(128)} %reshape.28.cols_all, s32[12]{0:T(128)} %bitcast.17, s32[12]{0:T(128)} %bitcast.18), custom_call_target="tpu_custom_call" | custom-call | tf_op jit(solution)/shard_map/lists/pallas_call | solution.py:160
  86.7 0.0 collective-permute-done.7.rest_5_
  86.7 0.0 copy-start.7
  86.7 3.2 %collective-permute-done.6.rest_4_ = bf16[2,256,256]{2,1,0:T(8,128)(2,1)} collective-permute-done((bf16[2,256,256]{2,1,0:T(8,128)(2,1)}, bf16[2,256,256]{2,1,0:T(8,128)(2,1)}, u32[]{:S(2)}, u32[]{:S(2)}) %collective-permute-start.6) | collective-permute-done | bytes 262176 | tf_op jit(solution)/shard_map/ppermute | solution.py:122
  89.9 0.0 copy-done.3
  89.9 0.0 copy-done.4
  89.9 0.0 copy-done.5
  89.9 0.0 copy-done.6
  89.9 0.0 copy-done.1
  89.9 0.0 copy-done.2
  90.0 0.0 copy-done.7
  90.0 12.5 %products.1 = s16[4,816,256]{2,1,0:T(8,128)(2,1)} custom-call(s32[192]{0:T(256)} %get-tuple-element.18.list_a, s32[192]{0:T(256)} %get-tuple-element.19.list_b, s32[12]{0:T(128)} %get-tuple-element.20.counts, bf16[64,256,256]{2,1,0:T(8,128)(2,1)} %bitcast.11, bf16[4,256,256]{2,1,0:T(8,128)(2,1)} %bitcast.14, bf16[4,256,256]{2,1,0:T(8,128)(2,1)} %copy-done.3, ...), custom_call_target="tpu_custom_call" | custom-call | flops 2147483648 | bytes 16777216 | tf_op jit(solution)/shard_map/products/pallas_call | solution.py:174
  102.5 0.0 copy-start
  102.5 22.2 %all_to_all.19.coded = s16[4,816,256]{2,1,0:T(8,128)(2,1)S(1)} all-to-all(s16[4,816,256]{2,1,0:T(8,128)(2,1)} %products.1), channel_id=1, replica_groups=mesh['row'=16,'col'=8,'depth'=4] {'depth'}, dimensions={0} | all-to-all | bytes 3342336 | tf_op jit(solution)/shard_map/all_to_all | solution.py:191
  124.8 0.0 copy-done
  124.8 1.3 finish.1
  (4 shorter events, 0.0 us)
Async XLA Ops:
  6.5 83.4 %all-gather.3.cloned.1.call-start = ((), (), s32[]{:S(2)}) async-start(), calls=%async_computation.3 | async-start | bytes 8912896 | tf_op jit(solution)/shard_map/all_gather | solution.py:135
  7.3 30.0 %collective-permute-start.1 = (bf16[4,256,256]{2,1,0:T(8,128)(2,1)}, bf16[4,256,256]{2,1,0:T(8,128)(2,1)S(1)}, u32[]{:S(2)}, u32[]{:S(2)}) collective-permute-start(bf16[4,256,256]{2,1,0:T(8,128)(2,1)} %bitcast.12), channel_id=1, source_target_pairs={{0,28},{4,0},{8,4},{12,8},{16,12},{20,16},{24,20},{28,24},{1,29},{... | collective-permute-start | bytes 1572872 | tf_op jit(solution)/shard_map/ppermute | solution.py:122
  18.2 19.0 %collective-permute-start = (bf16[4,256,256]{2,1,0:T(8,128)(2,1)}, bf16[4,256,256]{2,1,0:T(8,128)(2,1)S(1)}, u32[]{:S(2)}, u32[]{:S(2)}) collective-permute-start(bf16[4,256,256]{2,1,0:T(8,128)(2,1)} %bitcast.13), channel_id=1, source_target_pairs={{0,4},{4,8},{8,12},{12,16},{16,20},{20,24},{24,28},{28,0},{1,5},{5... | collective-permute-start | bytes 1572872 | tf_op jit(solution)/shard_map/ppermute | solution.py:122
  37.3 52.7 %copy-start.3 = (bf16[4,256,256]{2,1,0:T(8,128)(2,1)}, bf16[4,256,256]{2,1,0:T(8,128)(2,1)S(1)}, u32[]{:S(2)}) copy-start(bf16[4,256,256]{2,1,0:T(8,128)(2,1)S(1)} %collective-permute-done.1.rest_1_) | copy-start | bytes 1572868
  37.3 52.7 %copy-start.4 = (bf16[4,256,256]{2,1,0:T(8,128)(2,1)}, bf16[4,256,256]{2,1,0:T(8,128)(2,1)S(1)}, u32[]{:S(2)}) copy-start(bf16[4,256,256]{2,1,0:T(8,128)(2,1)S(1)} %collective-permute-done.rest_8_) | copy-start | bytes 1572868
  37.3 19.9 %collective-permute-start.2 = (bf16[4,256,256]{2,1,0:T(8,128)(2,1)S(1)}, bf16[4,256,256]{2,1,0:T(8,128)(2,1)S(1)}, u32[]{:S(2)}, u32[]{:S(2)}) collective-permute-start(bf16[4,256,256]{2,1,0:T(8,128)(2,1)S(1)} %collective-permute-done.rest_8_), channel_id=1, source_target_pairs={{0,4},{4,8},{8,12},{12,16},{16,20},{20,24},{24,28},{28,0},{1,5},{5... | collective-permute-start | bytes 1572872 | tf_op jit(solution)/shard_map/ppermute | solution.py:122
  39.2 18.0 %collective-permute-start.3 = (bf16[4,256,256]{2,1,0:T(8,128)(2,1)S(1)}, bf16[4,256,256]{2,1,0:T(8,128)(2,1)S(1)}, u32[]{:S(2)}, u32[]{:S(2)}) collective-permute-start(bf16[4,256,256]{2,1,0:T(8,128)(2,1)S(1)} %collective-permute-done.1.rest_1_), channel_id=1, source_target_pairs={{0,28},{4,0},{8,4},{12,8},{16,12},{20,16},{24,20},{28,24},{1,29},{... | collective-permute-start | bytes 1572872 | tf_op jit(solution)/shard_map/ppermute | solution.py:122
  57.2 32.7 %copy-start.5 = (bf16[4,256,256]{2,1,0:T(8,128)(2,1)}, bf16[4,256,256]{2,1,0:T(8,128)(2,1)S(1)}, u32[]{:S(2)}) copy-start(bf16[4,256,256]{2,1,0:T(8,128)(2,1)S(1)} %collective-permute-done.2.rest_7_) | copy-start | bytes 1572868
  57.2 32.7 %copy-start.6 = (bf16[4,256,256]{2,1,0:T(8,128)(2,1)}, bf16[4,256,256]{2,1,0:T(8,128)(2,1)S(1)}, u32[]{:S(2)}) copy-start(bf16[4,256,256]{2,1,0:T(8,128)(2,1)S(1)} %collective-permute-done.3.rest_2_) | copy-start | bytes 1572868
  57.2 15.8 %collective-permute-start.4 = (bf16[4,256,256]{2,1,0:T(8,128)(2,1)S(1)}, bf16[4,256,256]{2,1,0:T(8,128)(2,1)S(1)}, u32[]{:S(2)}, u32[]{:S(2)}) collective-permute-start(bf16[4,256,256]{2,1,0:T(8,128)(2,1)S(1)} %collective-permute-done.3.rest_2_), channel_id=1, source_target_pairs={{0,28},{4,0},{8,4},{12,8},{16,12},{20,16},{24,20},{28,24},{1,29},{... | collective-permute-start | bytes 1572872 | tf_op jit(solution)/shard_map/ppermute | solution.py:122
  62.6 16.7 %collective-permute-start.5 = (bf16[4,256,256]{2,1,0:T(8,128)(2,1)S(1)}, bf16[4,256,256]{2,1,0:T(8,128)(2,1)S(1)}, u32[]{:S(2)}, u32[]{:S(2)}) collective-permute-start(bf16[4,256,256]{2,1,0:T(8,128)(2,1)S(1)} %collective-permute-done.2.rest_7_), channel_id=1, source_target_pairs={{0,4},{4,8},{8,12},{12,16},{16,20},{20,24},{24,28},{28,0},{1,5},{5... | collective-permute-start | bytes 1572872 | tf_op jit(solution)/shard_map/ppermute | solution.py:122
  73.0 17.0 %copy-start.1 = (bf16[4,256,256]{2,1,0:T(8,128)(2,1)}, bf16[4,256,256]{2,1,0:T(8,128)(2,1)S(1)}, u32[]{:S(2)}) copy-start(bf16[4,256,256]{2,1,0:T(8,128)(2,1)S(1)} %collective-permute-done.4.rest_3_) | copy-start | bytes 1572868
  73.7 12.9 %collective-permute-start.7 = (bf16[2,256,256]{2,1,0:T(8,128)(2,1)}, bf16[2,256,256]{2,1,0:T(8,128)(2,1)S(1)}, u32[]{:S(2)}, u32[]{:S(2)}) collective-permute-start(bf16[2,256,256]{2,1,0:T(8,128)(2,1)} %slice.9), channel_id=1, source_target_pairs={{0,28},{4,0},{8,4},{12,8},{16,12},{20,16},{24,20},{28,24},{1,29},{... | collective-permute-start | bytes 786440 | tf_op jit(solution)/shard_map/ppermute | solution.py:122
  79.3 10.6 %copy-start.2 = (bf16[4,256,256]{2,1,0:T(8,128)(2,1)}, bf16[4,256,256]{2,1,0:T(8,128)(2,1)S(1)}, u32[]{:S(2)}) copy-start(bf16[4,256,256]{2,1,0:T(8,128)(2,1)S(1)} %collective-permute-done.5.rest_6_) | copy-start | bytes 1572868
  80.1 9.8 %collective-permute-start.6 = (bf16[2,256,256]{2,1,0:T(8,128)(2,1)}, bf16[2,256,256]{2,1,0:T(8,128)(2,1)}, u32[]{:S(2)}, u32[]{:S(2)}) collective-permute-start(bf16[2,256,256]{2,1,0:T(8,128)(2,1)} %slice.8), channel_id=1, source_target_pairs={{0,4},{4,8},{8,12},{12,16},{16,20},{20,24},{24,28},{28,0},{1,5},{5... | collective-permute-start | bytes 786440 | tf_op jit(solution)/shard_map/ppermute | solution.py:122
  86.7 3.3 %copy-start.7 = (bf16[2,256,256]{2,1,0:T(8,128)(2,1)}, bf16[2,256,256]{2,1,0:T(8,128)(2,1)S(1)}, u32[]{:S(2)}) copy-start(bf16[2,256,256]{2,1,0:T(8,128)(2,1)S(1)} %collective-permute-done.7.rest_5_) | copy-start | bytes 786436
  102.5 22.2 %copy-start = (bf16[1,1,3,256,256]{4,3,2,1,0:T(8,128)(2,1)S(1)}, bf16[1,1,3,256,256]{4,3,2,1,0:T(8,128)(2,1)}, u32[]{:S(2)}) copy-start(bf16[1,1,3,256,256]{4,3,2,1,0:T(8,128)(2,1)} %param.13) | copy-start | bytes 1179652
Sparse Core Ops, SparseCore 0:
  9.5 63.0 all-gather.2

commit v2 on v0

v2 whole, which is shorter than its diff:
```python
import functools

import jax
import jax.numpy as jnp
from jax import lax
from jax.experimental import pallas as pl
from jax.experimental.pallas import tpu as pltpu
from jax.sharding import PartitionSpec as P

GROUP = 4
LEVELS = 32000.0
FINER = 16.0
PAD = 16
VMEM_BYTES = 28 * 1024 * 1024
LANES = 128


def prepare_kernel(sizes, place, rows, cols, tile_a, tile_b, out_a, out_b):
    held_a, held_b, blk, cut, owners = sizes
    whole_a, piece = held_a * blk, held_b * blk
    my_row, my_col = place[0], place[1]
    out_a[pl.ds(0, whole_a), :] = tile_a[...]
    out_b[pl.ds(0, piece), :] = tile_b[pl.ds(0, piece), :]
    out_b[pl.ds(cut, piece), :] = tile_b[pl.ds(piece, piece), :]
    lane = lax.broadcasted_iota(jnp.int32, (PAD, blk), 1) & (LANES // 2 - 1)
    spread = jnp.zeros((PAD, blk), jnp.int32)
    for a in range(held_a):
        spread = jnp.where(lane == my_row * held_a + a, rows[a] + 1, spread)
    out_a[pl.ds(whole_a, PAD), :] = spread.astype(jnp.float32).astype(out_a.dtype)
    spread = jnp.zeros((PAD, blk), jnp.int32)
    for index in range(cols.shape[0]):
        first = (my_col + index // held_b * owners) * held_a + index % held_b
        spread = jnp.where(lane == first, cols[index] + 1, spread)
    out_b[pl.ds(piece, PAD), :] = spread.astype(jnp.float32).astype(out_b.dtype)


def listed(rows_seen, cols_seen, keep_rows, keep_cols, my_row, my_col, sizes):
    slots, held_a, held_b, holders, owners = sizes
    lane = lax.broadcasted_iota(jnp.int32, (LANES, LANES), 0)
    holder = lax.broadcasted_iota(jnp.int32, (LANES, LANES), 1)
    mine = (lane < holders * held_a) & ((lane // held_a) == holder)
    pick_a = jnp.where(mine, lane + 1, 0)
    apart = (holder - my_row + holders) & (owners - 1)
    piece = ((holder + my_col - my_row + holders) & (holders - 1)) // owners
    pick_b = jnp.where(mine, (apart * 2 + piece) * held_b + (lane & (held_a - 1)) + 1, 0)
    before = jnp.where(lane <= holder, 1, 0)

    def numbers(seen, wanted, pick):
        sublane = lax.broadcasted_iota(jnp.int32, seen.shape, 0)
        target = jnp.full(seen.shape, -1, jnp.int32)
        for slot in range(slots):
            target = jnp.where(sublane == slot, wanted[slot] + 1, target)
        hits = jnp.where(seen == target.astype(jnp.float32), 1.0, 0.0).astype(jnp.bfloat16)
        pick = pick.astype(jnp.float32).astype(jnp.bfloat16)
        return jnp.dot(hits, pick, preferred_element_type=jnp.float32)

    number_a = numbers(rows_seen, keep_rows, pick_a)
    number_b = numbers(cols_seen, keep_cols, pick_b)
    both = jnp.where((number_a > 0) & (number_b > 0), 1.0, 0.0)
    before = before.astype(jnp.float32).astype(jnp.bfloat16)
    place = jnp.dot(both.astype(jnp.bfloat16), before, preferred_element_type=jnp.float32)
    code = (number_a - 1.0) + 128.0 * (number_b - 1.0)
    lane = lax.broadcasted_iota(jnp.int32, both.shape, 1)
    count = jnp.sum(both, axis=1, keepdims=True)
    result = jnp.where(lane == LANES - 1, count, 0.0)
    nothing = 128.0 * owners * 2 * held_b
    for at in range(holders):
        value = jnp.sum(jnp.where(place == at + 1.0, both * code, 0.0), axis=1, keepdims=True)
        result = jnp.where(lane == at, jnp.where(count > at, value, nothing), result)
    return result.astype(jnp.int32)


def multiply(sizes, lists, a_all, b_all, first, total):
    held_a, held_b, blk, cut = sizes

    def block_a(code):
        number = code & 127
        return a_all[number // held_a, pl.ds(pl.multiple_of(lax.rem(number, held_a) * blk, blk), blk), :]

    def block_b(code):
        number = code >> 7
        piece, inside = lax.rem(number // held_b, 2), lax.rem(number, held_b)
        return b_all[number // (2 * held_b), pl.ds(pl.multiple_of(piece * cut + inside * blk, PAD), blk), :]

    def grouped(slot, group):
        codes = [lists[slot, group * GROUP + n] for n in range(GROUP)]
        left = jnp.concatenate([block_a(code) for code in codes], axis=1)
        right = jnp.concatenate([block_b(code) for code in codes], axis=0)
        return jnp.dot(left, right, preferred_element_type=jnp.float32)

    count = total.shape[0]
    for index in range(count):
        total[index] = grouped(first + index, 0)
    for index in range(count):
        slot = first + index

        def one_group(group, carry, index=index, slot=slot):
            total[index] += grouped(slot, group)
            return carry

        lax.fori_loop(1, (lists[slot, LANES - 1] + GROUP - 1) // GROUP, one_group, 0)


def encode(total, index, coded, inside, blk, each):
    largest = jnp.maximum(jnp.max(jnp.abs(total[index]), axis=0, keepdims=True), 1e-30)
    power = jnp.ceil(FINER * jnp.log2(largest / LEVELS))
    values = jnp.round(total[index] * jnp.exp2(power * (-1.0 / FINER)))
    coded[pl.ds(inside * blk, blk), :] = values.astype(jnp.int32).astype(jnp.int16)
    powers = jnp.broadcast_to(power, (PAD, blk)).astype(jnp.int32).astype(jnp.int16)
    coded[pl.ds(each * blk + inside * PAD, PAD), :] = powers


def target(place, steps, shares, each):
    return lax.rem(place[2] + steps, shares) * each


def far_kernel(sizes, shares, place, keep_rows, keep_cols, a_all, *rest):
    parts, (coded, lists, b_all, total, scalar, sem) = rest[:-6], rest[-6:]
    held_a, held_b, blk, cut = sizes
    holders, owners, slots = a_all.shape[0], b_all.shape[0] - 1, keep_rows.shape[0]
    each = slots // shares
    my_row, my_col = place[0], place[1]
    for part, (owner, first) in zip(parts, rows_of(owners, cut)):
        b_all[owner, pl.ds(first, part.shape[0]), :] = part[...]
    b_all[owners, pl.ds(0, blk), :] = jnp.zeros((blk, blk), b_all.dtype)
    rows_seen = jnp.sum(a_all[:, pl.ds(held_a * blk, PAD), pl.ds(0, LANES)].astype(jnp.float32), axis=0)
    cols_seen = jnp.sum(b_all[pl.ds(0, owners), pl.ds(cut - PAD, PAD), pl.ds(0, LANES)].astype(jnp.float32), axis=0)
    turn = (my_row - my_col + holders) & (holders - 1)
    cols_seen = pltpu.roll(cols_seen, turn * held_a, 1)
    lists[...] = listed(
        rows_seen, cols_seen, keep_rows, keep_cols, my_row, my_col, (slots, held_a, held_b, holders, owners)
    )
    copy = pltpu.make_async_copy(lists, scalar, sem)
    copy.start()
    copy.wait()
    multiply(sizes, scalar, a_all, b_all, target(place, 2, shares, each), total)
    for index in range(each):
        encode(total, index, coded, index, blk, each)


def near_kernel(sizes, shares, each, place, lists, a_all, b_all, coded_up, coded_down, total_up, total_down):
    blk = sizes[2]
    multiply(sizes, lists, a_all, b_all, target(place, 1, shares, each), total_up)
    multiply(sizes, lists, a_all, b_all, target(place, shares - 1, shares, each), total_down)
    for index in range(each):
        encode(total_up, index, coded_up, index, blk, each)
        encode(total_down, index, coded_down, index, blk, each)


def own_kernel(sizes, shares, each, place, lists, a_all, b_all, total):
    multiply(sizes, lists, a_all, b_all, target(place, 0, shares, each), total)


def finish_kernel(far, up, down, own, square_kept, out):
    each, blk = square_kept.shape[0], square_kept.shape[1]
    for slot in range(each):
        cube = own[slot]
        for coded in (far, up, down):
            power = coded[pl.ds(each * blk + slot * PAD, PAD), :].astype(jnp.int32).astype(jnp.float32)[:1]
            values = coded[pl.ds(slot * blk, blk), :].astype(jnp.int32).astype(jnp.float32)
            cube = cube + values * jnp.exp2(power * (1.0 / FINER))
        out[slot] = (3.0 * square_kept[slot].astype(jnp.float32) - 2.0 * cube).astype(out.dtype)


def rows_of(owners, cut):
    half = owners // 2
    return [(apart, 0) for apart in range(half)] + [(half, 0), (half, cut)] + [(apart, 0) for apart in range(half + 1, owners)]


def shifted(value, axis, steps):
    count = lax.axis_size(axis)
    return lax.ppermute(value, axis, [(source, (source + steps) % count) for source in range(count)])


def body(density_tiles, density_rows, square_tiles, square_cols, keep_rows, keep_cols, square_kept):
    n_row, n_col, n_depth = lax.axis_size("row"), lax.axis_size("col"), lax.axis_size("depth")
    my_row, my_col = lax.axis_index("row"), lax.axis_index("col")
    held_a, blk = density_tiles.shape[3], density_tiles.shape[4]
    pieces, held_b = square_tiles.shape[3], square_tiles.shape[4]
    slots = keep_rows.shape[-1]
    half = n_col // 2
    cut = held_b * blk + PAD
    place = jnp.stack([my_row, my_col, lax.axis_index("depth")]).astype(jnp.int32)
    smem = pl.BlockSpec(memory_space=pltpu.SMEM)
    whole = pl.BlockSpec(memory_space=pltpu.VMEM)
    params = pltpu.CompilerParams(vmem_limit_bytes=VMEM_BYTES)
    tile_a, tile_b = pl.pallas_call(
        functools.partial(prepare_kernel, (held_a, held_b, blk, cut, n_col)),
        out_shape=[
            jax.ShapeDtypeStruct((held_a * blk + PAD, blk), jnp.bfloat16),
            jax.ShapeDtypeStruct((cut + held_b * blk, blk), jnp.bfloat16),
        ],
        in_specs=[smem] * 3 + [whole] * 2,
        out_specs=[whole] * 2,
        compiler_params=params,
        name="prepare",
    )(
        place,
        density_rows[0, 0, 0],
        square_cols[0, 0, 0].reshape(-1),
        density_tiles[0, 0, 0].reshape(held_a * blk, blk),
        square_tiles[0, 0, 0].reshape(pieces * held_b * blk, blk),
    )
    a_all = lax.all_gather(tile_a, "row")

    up, down = [tile_b], [tile_b]
    for step in range(1, half + 1):
        send_up, send_down = up[-1], down[-1]
        if step == half:
            send_up, send_down = send_up[:cut], send_down[cut:]
        up.append(shifted(send_up, "col", 1))
        down.append(shifted(send_down, "col", -1))
    parts = down[:half] + [up[half], down[half]] + up[1:half][::-1]

    each = slots // n_depth
    sizes = (held_a, held_b, blk, cut)
    coded = jax.ShapeDtypeStruct((each * (blk + PAD), blk), jnp.int16)
    summed = (each, blk, blk)

    def cost(count):
        return pl.CostEstimate(flops=8 * count * blk**3, bytes_accessed=count * 2**20, transcendentals=0)

    far, lists, b_all = pl.pallas_call(
        functools.partial(far_kernel, sizes, n_depth),
        out_shape=[
            coded,
            jax.ShapeDtypeStruct((PAD, LANES), jnp.int32),
            jax.ShapeDtypeStruct((n_col + 1, cut + held_b * blk, blk), jnp.bfloat16),
        ],
        in_specs=[smem] * 3 + [whole] * (1 + len(parts)),
        out_specs=[whole] * 3,
        scratch_shapes=[
            pltpu.VMEM(summed, jnp.float32),
            pltpu.SMEM((PAD, LANES), jnp.int32),
            pltpu.SemaphoreType.DMA,
        ],
        compiler_params=params,
        cost_estimate=cost(each),
        name="far",
    )(place, keep_rows[0, 0], keep_cols[0, 0], a_all, *parts)
    far = shifted(far, "depth", 2)
    up, down = pl.pallas_call(
        functools.partial(near_kernel, sizes, n_depth, each),
        out_shape=[coded] * 2,
        in_specs=[smem] * 2 + [whole] * 2,
        out_specs=[whole] * 2,
        scratch_shapes=[pltpu.VMEM(summed, jnp.float32)] * 2,
        compiler_params=params,
        cost_estimate=cost(2 * each),
        name="near",
    )(place, lists, a_all, b_all)
    up = shifted(up, "depth", 1)
    down = shifted(down, "depth", -1)
    own = pl.pallas_call(
        functools.partial(own_kernel, sizes, n_depth, each),
        out_shape=jax.ShapeDtypeStruct(summed, jnp.float32),
        in_specs=[smem] * 2 + [whole] * 2,
        out_specs=whole,
        compiler_params=params,
        cost_estimate=cost(each),
        name="own",
    )(place, lists, a_all, b_all)
    result = pl.pallas_call(
        finish_kernel,
        out_shape=jax.ShapeDtypeStruct(summed, jnp.bfloat16),
        compiler_params=params,
        cost_estimate=pl.CostEstimate(flops=2**21, bytes_accessed=3 * 2**20, transcendentals=0),
        name="finish",
    )(far, up, down, own, square_kept[0, 0])
    return result[None, None]


def solution(mesh):
    placed = (
        P("depth", "row", "col", None, None, None),
        P("depth", "row", "col", None),
        P("depth", "row", "col", None, None, None, None),
        P("depth", "row", "col", None, None),
        P("row", "col", None),
        P("row", "col", None),
        P("row", "col", "depth", None, None),
    )
    return jax.shard_map(
        body,
        mesh=mesh,
        in_specs=placed,
        out_specs=P("row", "col", "depth", None, None),
        check_vma=False,
    )
```

time: 372 us -> 119 us (0.32)
  the two profiles are of different devices: /device:TPU:1 before, /device:TPU:30 now
where the time goes in v2:
time: 119 us; the launch traced here: 118 us
  starting transfers between devices  43.7 us (37%)
  waiting for transfers between devices  39.9 us (34%)
  between operations  13.6 us (11%)
  local copies, waits for them, and re-layouts  11 us (9%)
  Pallas kernels  10.1 us (8%)
    ppermute x11, starting transfers between devices, shifted(): lax.ppermute(value, axis, [(source, (source + steps) % count) for source...  43.7 us
    ppermute x11, waiting for transfers between devices, shifted(): lax.ppermute(value, axis, [(source, (source + steps) % count) for source...  39.9 us
    unnamed x24, local copies, waits for them, and re-layouts  10.2 us
    pallas_call x1, Pallas kernels, body(): pl.pallas_call(functools.partial(far_kernel, sizes, n_depth), out_shape=[...  3.3 us
    pallas_call x1, Pallas kernels, body(): pl.pallas_call(functools.partial(near_kernel, sizes, n_depth, each), out_...  2.82 us
  transfers between devices with their start and end apart: 12, of which 6 were waited for; matrix products, arithmetic and copies ran while one was open for 0% of the time, Pallas kernels for 3%

profile of v2, /device:TPU:30, one launch (start us, length us, event | category | flops | bytes accessed | tf_op | source)
XLA Modules:
  0.0 118.3 jit_solution(14823911068531763506)
XLA Ops:
  6.5 0.0 all-gather.3.cloned.1.call-start
  6.5 0.8 reshape_squeeze.9.cols
  7.3 0.1 pad_add_fusion.place
  7.4 0.0 copy-start.4
  7.4 1.0 copy-done.4
  8.4 0.0 copy-start.5
  8.4 1.0 copy-done.5
  9.5 0.0 copy-start.9
  9.5 0.7 copy-done.9
  10.1 1.5 %prepare.1 = (bf16[1040,256]{1,0:T(8,128)(2,1)}, bf16[1040,256]{1,0:T(8,128)(2,1)S(1)}) custom-call(s32[3]{0:T(128)S(1)} %pad_add_fusion.place, s32[4]{0:T(128)S(1)} %bitcast.17, s32[4]{0:T(128)S(1)} %reshape_squeeze.9.cols, bf16[1024,256]{1,0:T(8,128)(2,1)S(1)} %bitcast.14, bf16[1024,256]{1,0:T(8,128)(2,1)S(1)} %bitcast.15), custom_call_target="tpu_custom_call" | custom-call | tf_op jit(solution)/shard_map/prepare/pallas_call | solution.py:187
  11.6 0.0 all-gather.3.cloned.1.call-update
  11.6 4.3 %collective-permute-start.3 = (bf16[1040,256]{1,0:T(8,128)(2,1)S(1)}, bf16[1040,256]{1,0:T(8,128)(2,1)S(1)}, u32[]{:S(2)}, u32[]{:S(2)}) collective-permute-start(bf16[1040,256]{1,0:T(8,128)(2,1)S(1)} %get-tuple-element.13.rest_0_), channel_id=1, source_target_pairs={{0,4},{4,8},{8,12},{12,16},{16,20},{20,24},{24,28},{28,0},{1,5},{5... | collective-permute-start | bytes 1597448 | tf_op jit(solution)/shard_map/ppermute | solution.py:172
  15.9 8.6 %collective-permute-start = (bf16[1040,256]{1,0:T(8,128)(2,1)S(1)}, bf16[1040,256]{1,0:T(8,128)(2,1)S(1)}, u32[]{:S(2)}, u32[]{:S(2)}) collective-permute-start(bf16[1040,256]{1,0:T(8,128)(2,1)S(1)} %get-tuple-element.13.rest_0_), channel_id=1, source_target_pairs={{0,28},{4,0},{8,4},{12,8},{16,12},{20,16},{24,20},{28,24},{1,29},{... | collective-permute-start | bytes 1597448 | tf_op jit(solution)/shard_map/ppermute | solution.py:172
  24.5 10.2 %collective-permute-done.3.rest_8_ = bf16[1040,256]{1,0:T(8,128)(2,1)S(1)} collective-permute-done((bf16[1040,256]{1,0:T(8,128)(2,1)S(1)}, bf16[1040,256]{1,0:T(8,128)(2,1)S(1)}, u32[]{:S(2)}, u32[]{:S(2)}) %collective-permute-start.3) | collective-permute-done | bytes 532512 | tf_op jit(solution)/shard_map/ppermute | solution.py:172
  34.6 1.9 %collective-permute-start.4 = (bf16[1040,256]{1,0:T(8,128)(2,1)S(1)}, bf16[1040,256]{1,0:T(8,128)(2,1)S(1)}, u32[]{:S(2)}, u32[]{:S(2)}) collective-permute-start(bf16[1040,256]{1,0:T(8,128)(2,1)S(1)} %collective-permute-done.3.rest_8_), channel_id=1, source_target_pairs={{0,4},{4,8},{8,12},{12,16},{16,20},{20,24},{24,28},{28,0},{1,5},{5... | collective-permute-start | bytes 1597448 | tf_op jit(solution)/shard_map/ppermute | solution.py:172
  36.5 0.0 collective-permute-done.rest_1_
  36.6 5.1 %collective-permute-start.1 = (bf16[1040,256]{1,0:T(8,128)(2,1)S(1)}, bf16[1040,256]{1,0:T(8,128)(2,1)S(1)}, u32[]{:S(2)}, u32[]{:S(2)}) collective-permute-start(bf16[1040,256]{1,0:T(8,128)(2,1)S(1)} %collective-permute-done.rest_1_), channel_id=1, source_target_pairs={{0,28},{4,0},{8,4},{12,8},{16,12},{20,16},{24,20},{28,24},{1,29},{... | collective-permute-start | bytes 1597448 | tf_op jit(solution)/shard_map/ppermute | solution.py:172
  41.7 9.4 %collective-permute-done.4.rest_7_ = bf16[1040,256]{1,0:T(8,128)(2,1)S(1)} collective-permute-done((bf16[1040,256]{1,0:T(8,128)(2,1)S(1)}, bf16[1040,256]{1,0:T(8,128)(2,1)S(1)}, u32[]{:S(2)}, u32[]{:S(2)}) %collective-permute-start.4) | collective-permute-done | bytes 532512 | tf_op jit(solution)/shard_map/ppermute | solution.py:172
  51.1 1.9 %collective-permute-start.5 = (bf16[1040,256]{1,0:T(8,128)(2,1)S(1)}, bf16[1040,256]{1,0:T(8,128)(2,1)S(1)}, u32[]{:S(2)}, u32[]{:S(2)}) collective-permute-start(bf16[1040,256]{1,0:T(8,128)(2,1)S(1)} %collective-permute-done.4.rest_7_), channel_id=1, source_target_pairs={{0,4},{4,8},{8,12},{12,16},{16,20},{20,24},{24,28},{28,0},{1,5},{5... | collective-permute-start | bytes 1597448 | tf_op jit(solution)/shard_map/ppermute | solution.py:172
  53.0 0.0 collective-permute-done.1.rest_2_
  53.0 0.0 copy-start.2
  53.0 5.1 %collective-permute-start.2 = (bf16[1040,256]{1,0:T(8,128)(2,1)S(1)}, bf16[1040,256]{1,0:T(8,128)(2,1)S(1)}, u32[]{:S(2)}, u32[]{:S(2)}) collective-permute-start(bf16[1040,256]{1,0:T(8,128)(2,1)S(1)} %collective-permute-done.1.rest_2_), channel_id=1, source_target_pairs={{0,28},{4,0},{8,4},{12,8},{16,12},{20,16},{24,20},{28,24},{1,29},{... | collective-permute-start | bytes 1597448 | tf_op jit(solution)/shard_map/ppermute | solution.py:172
  58.2 8.6 %collective-permute-done.5.rest_6_ = bf16[1040,256]{1,0:T(8,128)(2,1)S(1)} collective-permute-done((bf16[1040,256]{1,0:T(8,128)(2,1)S(1)}, bf16[1040,256]{1,0:T(8,128)(2,1)S(1)}, u32[]{:S(2)}, u32[]{:S(2)}) %collective-permute-start.5) | collective-permute-done | bytes 532512 | tf_op jit(solution)/shard_map/ppermute | solution.py:172
  66.8 1.9 %collective-permute-start.6 = (bf16[528,256]{1,0:T(8,128)(2,1)S(1)}, bf16[528,256]{1,0:T(8,128)(2,1)S(1)}, u32[]{:S(2)}, u32[]{:S(2)}) collective-permute-start(bf16[528,256]{1,0:T(8,128)(2,1)S(1)} %slice.8), channel_id=1, source_target_pairs={{0,4},{4,8},{8,12},{12,16},{16,20},{20,24},{24,28},{28,0},{1,5},{5... | collective-permute-start | bytes 811016 | tf_op jit(solution)/shard_map/ppermute | solution.py:172
  68.7 0.0 collective-permute-done.2.rest_3_
  68.7 0.0 copy-done.2
  68.8 5.1 %collective-permute-start.7 = (bf16[512,256]{1,0:T(8,128)(2,1)S(1)}, bf16[512,256]{1,0:T(8,128)(2,1)S(1)}, u32[]{:S(2)}, u32[]{:S(2)}) collective-permute-start(bf16[512,256]{1,0:T(8,128)(2,1)S(1)} %slice.9), channel_id=1, source_target_pairs={{0,28},{4,0},{8,4},{12,8},{16,12},{20,16},{24,20},{28,24},{1,29},{... | collective-permute-start | bytes 786440 | tf_op jit(solution)/shard_map/ppermute | solution.py:172
  73.9 3.9 %collective-permute-done.7.rest_5_ = bf16[512,256]{1,0:T(8,128)(2,1)S(1)} collective-permute-done((bf16[512,256]{1,0:T(8,128)(2,1)S(1)}, bf16[512,256]{1,0:T(8,128)(2,1)S(1)}, u32[]{:S(2)}, u32[]{:S(2)}) %collective-permute-start.7) | collective-permute-done | bytes 262176 | tf_op jit(solution)/shard_map/ppermute | solution.py:172
  77.8 0.7 copy-done.7
  78.5 0.0 collective-permute-done.6.rest_4_
  78.5 3.4 %copy-done = bf16[16640,256]{1,0:T(8,128)(2,1)S(1)} copy-done((bf16[16640,256]{1,0:T(8,128)(2,1)S(1)}, bf16[16640,256]{1,0:T(8,128)(2,1)}, u32[]{:S(2)}) %copy-start) | copy-done | bytes 8519704
  81.9 1.0 copy-done.3
  83.0 0.9 copy-done.8
  83.9 0.7 copy-done.10
  84.6 0.7 copy-done.11
  85.2 3.3 %far.1 = (s16[816,256]{1,0:T(8,128)(2,1)S(1)}, s32[16,128]{1,0:T(8,128)S(1)}, bf16[9,1040,256]{2,1,0:T(8,128)(2,1)S(1)}) custom-call(s32[3]{0:T(128)S(1)} %pad_add_fusion.place, s32[12]{0:T(128)S(1)} %bitcast.18, s32[12]{0:T(128)S(1)} %bitcast.19, bf16[16,1040,256]{2,1,0:T(8,128)(2,1)S(1)} %bitcast.11, bf16[1040,256]{1,0:T(8,128)(2,1)S(1)} %get-tuple-element.13.rest_0_, ...), custom_call_target="tpu_custom_call" | custom-call | flops 402653184 | bytes 3145728 | tf_op jit(solution)/shard_map/far/pallas_call | solution.py:223
  88.5 3.0 %collective-permute-start.8 = (s16[816,256]{1,0:T(8,128)(2,1)S(1)}, s16[816,256]{1,0:T(8,128)(2,1)S(1)}, u32[]{:S(2)}, u32[]{:S(2)}) collective-permute-start(s16[816,256]{1,0:T(8,128)(2,1)S(1)} %get-tuple-element.14), channel_id=1, source_target_pairs={{0,2},{1,3},{2,0},{3,1},{4,6},{5,7},{6,4},{7,5},{8,10},{9,11},{10,... | collective-permute-start | bytes 1253384 | tf_op jit(solution)/shard_map/ppermute | solution.py:172
  91.5 0.0 copy-done.1
  91.5 2.8 %near.1 = (s16[816,256]{1,0:T(8,128)(2,1)S(1)}, s16[816,256]{1,0:T(8,128)(2,1)S(1)}) custom-call(s32[3]{0:T(128)S(1)} %pad_add_fusion.place, s32[16,128]{1,0:T(8,128)S(1)} %get-tuple-element.15.lists, bf16[16,1040,256]{2,1,0:T(8,128)(2,1)S(1)} %bitcast.12, bf16[9,1040,256]{2,1,0:T(8,128)(2,1)S(1)} %get-tuple-element.16.b_all), custom_call_target="tpu_custom_call" | custom-call | flops 805306368 | bytes 6291456 | tf_op jit(solution)/shard_map/near/pallas_call | solution.py:242
  94.4 0.0 copy-start.6
  94.4 4.8 %collective-permute-start.9 = (s16[816,256]{1,0:T(8,128)(2,1)S(1)}, s16[816,256]{1,0:T(8,128)(2,1)S(1)}, u32[]{:S(2)}, u32[]{:S(2)}) collective-permute-start(s16[816,256]{1,0:T(8,128)(2,1)S(1)} %get-tuple-element.17), channel_id=1, source_target_pairs={{0,1},{1,2},{2,3},{3,0},{4,5},{5,6},{6,7},{7,4},{8,9},{9,10},{10,1... | collective-permute-start | bytes 1253384 | tf_op jit(solution)/shard_map/ppermute | solution.py:172
  99.2 1.9 %collective-permute-start.10 = (s16[816,256]{1,0:T(8,128)(2,1)S(1)}, s16[816,256]{1,0:T(8,128)(2,1)S(1)}, u32[]{:S(2)}, u32[]{:S(2)}) collective-permute-start(s16[816,256]{1,0:T(8,128)(2,1)S(1)} %get-tuple-element.18), channel_id=1, source_target_pairs={{0,3},{1,0},{2,1},{3,2},{4,7},{5,4},{6,5},{7,6},{8,11},{9,8},{10,9... | collective-permute-start | bytes 1253384 | tf_op jit(solution)/shard_map/ppermute | solution.py:172
  101.1 1.3 %own.1 = f32[3,256,256]{2,1,0:T(8,128)S(1)} custom-call(s32[3]{0:T(128)S(1)} %pad_add_fusion.place, s32[16,128]{1,0:T(8,128)S(1)} %get-tuple-element.15.lists, bf16[16,1040,256]{2,1,0:T(8,128)(2,1)S(1)} %bitcast.13, bf16[9,1040,256]{2,1,0:T(8,128)(2,1)S(1)} %get-tuple-element.16.b_all), custom_call_target="tpu_custom_call" | custom-call | flops 402653184 | bytes 3145728 | tf_op jit(solution)/shard_map/own/pallas_call | solution.py:254
  102.4 0.0 collective-permute-done.8.far
  102.4 4.8 %collective-permute-done.9.up = s16[816,256]{1,0:T(8,128)(2,1)S(1)} collective-permute-done((s16[816,256]{1,0:T(8,128)(2,1)S(1)}, s16[816,256]{1,0:T(8,128)(2,1)S(1)}, u32[]{:S(2)}, u32[]{:S(2)}) %collective-permute-start.9) | collective-permute-done | bytes 417824 | tf_op jit(solution)/shard_map/ppermute | solution.py:172
  107.2 3.1 %collective-permute-done.10.down = s16[816,256]{1,0:T(8,128)(2,1)S(1)} collective-permute-done((s16[816,256]{1,0:T(8,128)(2,1)S(1)}, s16[816,256]{1,0:T(8,128)(2,1)S(1)}, u32[]{:S(2)}, u32[]{:S(2)}) %collective-permute-start.10) | collective-permute-done | bytes 417824 | tf_op jit(solution)/shard_map/ppermute | solution.py:172
  110.3 0.0 copy-done.6
  110.3 1.2 finish.1
  (10 shorter events, 0.1 us)
Async XLA Ops:
  6.5 72.0 %all-gather.3.cloned.1.call-start = ((), (), s32[]{:S(2)}) async-start(), calls=%async_computation | async-start | bytes 9052160 | tf_op jit(solution)/shard_map/all_gather | solution.py:204
  7.4 1.0 copy-start.4
  8.4 1.0 copy-start.5
  9.5 0.7 copy-start.9
  11.6 23.0 %collective-permute-start.3 = (bf16[1040,256]{1,0:T(8,128)(2,1)S(1)}, bf16[1040,256]{1,0:T(8,128)(2,1)S(1)}, u32[]{:S(2)}, u32[]{:S(2)}) collective-permute-start(bf16[1040,256]{1,0:T(8,128)(2,1)S(1)} %get-tuple-element.13.rest_0_), channel_id=1, source_target_pairs={{0,4},{4,8},{8,12},{12,16},{16,20},{20,24},{24,28},{28,0},{1,5},{5... | collective-permute-start | bytes 1597448 | tf_op jit(solution)/shard_map/ppermute | solution.py:172
  15.9 20.7 %collective-permute-start = (bf16[1040,256]{1,0:T(8,128)(2,1)S(1)}, bf16[1040,256]{1,0:T(8,128)(2,1)S(1)}, u32[]{:S(2)}, u32[]{:S(2)}) collective-permute-start(bf16[1040,256]{1,0:T(8,128)(2,1)S(1)} %get-tuple-element.13.rest_0_), channel_id=1, source_target_pairs={{0,28},{4,0},{8,4},{12,8},{16,12},{20,16},{24,20},{28,24},{1,29},{... | collective-permute-start | bytes 1597448 | tf_op jit(solution)/shard_map/ppermute | solution.py:172
  34.6 16.5 %collective-permute-start.4 = (bf16[1040,256]{1,0:T(8,128)(2,1)S(1)}, bf16[1040,256]{1,0:T(8,128)(2,1)S(1)}, u32[]{:S(2)}, u32[]{:S(2)}) collective-permute-start(bf16[1040,256]{1,0:T(8,128)(2,1)S(1)} %collective-permute-done.3.rest_8_), channel_id=1, source_target_pairs={{0,4},{4,8},{8,12},{12,16},{16,20},{20,24},{24,28},{28,0},{1,5},{5... | collective-permute-start | bytes 1597448 | tf_op jit(solution)/shard_map/ppermute | solution.py:172
  36.6 16.5 %collective-permute-start.1 = (bf16[1040,256]{1,0:T(8,128)(2,1)S(1)}, bf16[1040,256]{1,0:T(8,128)(2,1)S(1)}, u32[]{:S(2)}, u32[]{:S(2)}) collective-permute-start(bf16[1040,256]{1,0:T(8,128)(2,1)S(1)} %collective-permute-done.rest_1_), channel_id=1, source_target_pairs={{0,28},{4,0},{8,4},{12,8},{16,12},{20,16},{24,20},{28,24},{1,29},{... | collective-permute-start | bytes 1597448 | tf_op jit(solution)/shard_map/ppermute | solution.py:172
  51.1 15.7 %collective-permute-start.5 = (bf16[1040,256]{1,0:T(8,128)(2,1)S(1)}, bf16[1040,256]{1,0:T(8,128)(2,1)S(1)}, u32[]{:S(2)}, u32[]{:S(2)}) collective-permute-start(bf16[1040,256]{1,0:T(8,128)(2,1)S(1)} %collective-permute-done.4.rest_7_), channel_id=1, source_target_pairs={{0,4},{4,8},{8,12},{12,16},{16,20},{20,24},{24,28},{28,0},{1,5},{5... | collective-permute-start | bytes 1597448 | tf_op jit(solution)/shard_map/ppermute | solution.py:172
  53.0 15.7 %copy-start.2 = (bf16[1040,256]{1,0:T(8,128)(2,1)}, bf16[1040,256]{1,0:T(8,128)(2,1)S(1)}, u32[]{:S(2)}) copy-start(bf16[1040,256]{1,0:T(8,128)(2,1)S(1)} %collective-permute-done.1.rest_2_) | copy-start | bytes 1597444
  53.0 15.7 %collective-permute-start.2 = (bf16[1040,256]{1,0:T(8,128)(2,1)S(1)}, bf16[1040,256]{1,0:T(8,128)(2,1)S(1)}, u32[]{:S(2)}, u32[]{:S(2)}) collective-permute-start(bf16[1040,256]{1,0:T(8,128)(2,1)S(1)} %collective-permute-done.1.rest_2_), channel_id=1, source_target_pairs={{0,28},{4,0},{8,4},{12,8},{16,12},{20,16},{24,20},{28,24},{1,29},{... | collective-permute-start | bytes 1597448 | tf_op jit(solution)/shard_map/ppermute | solution.py:172
  66.8 11.7 %collective-permute-start.6 = (bf16[528,256]{1,0:T(8,128)(2,1)S(1)}, bf16[528,256]{1,0:T(8,128)(2,1)S(1)}, u32[]{:S(2)}, u32[]{:S(2)}) collective-permute-start(bf16[528,256]{1,0:T(8,128)(2,1)S(1)} %slice.8), channel_id=1, source_target_pairs={{0,4},{4,8},{8,12},{12,16},{16,20},{20,24},{24,28},{28,0},{1,5},{5... | collective-permute-start | bytes 811016 | tf_op jit(solution)/shard_map/ppermute | solution.py:172
  68.8 9.0 %collective-permute-start.7 = (bf16[512,256]{1,0:T(8,128)(2,1)S(1)}, bf16[512,256]{1,0:T(8,128)(2,1)S(1)}, u32[]{:S(2)}, u32[]{:S(2)}) collective-permute-start(bf16[512,256]{1,0:T(8,128)(2,1)S(1)} %slice.9), channel_id=1, source_target_pairs={{0,28},{4,0},{8,4},{12,8},{16,12},{20,16},{24,20},{28,24},{1,29},{... | collective-permute-start | bytes 786440 | tf_op jit(solution)/shard_map/ppermute | solution.py:172
  77.8 0.7 copy-start.7
  78.5 3.4 %copy-start = (bf16[16640,256]{1,0:T(8,128)(2,1)S(1)}, bf16[16640,256]{1,0:T(8,128)(2,1)}, u32[]{:S(2)}) copy-start(bf16[16640,256]{1,0:T(8,128)(2,1)} %all-gather.3.cloned.1.call-done) | copy-start | bytes 25559044
  81.9 1.0 copy-start.3
  83.0 0.9 copy-start.8
  83.9 0.7 copy-start.10
  84.6 0.7 copy-start.11
  85.2 6.3 %copy-start.1 = (bf16[16640,256]{1,0:T(8,128)(2,1)S(1)}, bf16[16640,256]{1,0:T(8,128)(2,1)}, u32[]{:S(2)}) copy-start(bf16[16640,256]{1,0:T(8,128)(2,1)} %all-gather.3.cloned.1.call-done) | copy-start | bytes 25559044
  88.5 13.9 %collective-permute-start.8 = (s16[816,256]{1,0:T(8,128)(2,1)S(1)}, s16[816,256]{1,0:T(8,128)(2,1)S(1)}, u32[]{:S(2)}, u32[]{:S(2)}) collective-permute-start(s16[816,256]{1,0:T(8,128)(2,1)S(1)} %get-tuple-element.14), channel_id=1, source_target_pairs={{0,2},{1,3},{2,0},{3,1},{4,6},{5,7},{6,4},{7,5},{8,10},{9,11},{10,... | collective-permute-start | bytes 1253384 | tf_op jit(solution)/shard_map/ppermute | solution.py:172
  94.4 15.9 %copy-start.6 = (bf16[1,1,3,256,256]{4,3,2,1,0:T(8,128)(2,1)S(1)}, bf16[1,1,3,256,256]{4,3,2,1,0:T(8,128)(2,1)}, u32[]{:S(2)}) copy-start(bf16[1,1,3,256,256]{4,3,2,1,0:T(8,128)(2,1)} %param.13) | copy-start | bytes 1179652
  94.4 12.8 %collective-permute-start.9 = (s16[816,256]{1,0:T(8,128)(2,1)S(1)}, s16[816,256]{1,0:T(8,128)(2,1)S(1)}, u32[]{:S(2)}, u32[]{:S(2)}) collective-permute-start(s16[816,256]{1,0:T(8,128)(2,1)S(1)} %get-tuple-element.17), channel_id=1, source_target_pairs={{0,1},{1,2},{2,3},{3,0},{4,5},{5,6},{6,7},{7,4},{8,9},{9,10},{10,1... | collective-permute-start | bytes 1253384 | tf_op jit(solution)/shard_map/ppermute | solution.py:172
  99.2 11.1 %collective-permute-start.10 = (s16[816,256]{1,0:T(8,128)(2,1)S(1)}, s16[816,256]{1,0:T(8,128)(2,1)S(1)}, u32[]{:S(2)}, u32[]{:S(2)}) collective-permute-start(s16[816,256]{1,0:T(8,128)(2,1)S(1)} %get-tuple-element.18), channel_id=1, source_target_pairs={{0,3},{1,0},{2,1},{3,2},{4,7},{5,4},{6,5},{7,6},{8,11},{9,8},{10,9... | collective-permute-start | bytes 1253384 | tf_op jit(solution)/shard_map/ppermute | solution.py:172
Sparse Core Ops, SparseCore 0:
  11.7 62.9 all-gather.2

commit v3 on v2

--- a/solution.py
+++ b/solution.py
@@ -11,38 +11,77 @@
 LEVELS = 32000.0
 FINER = 16.0
 PAD = 16
-VMEM_BYTES = 28 * 1024 * 1024
+VMEM_BYTES = 18 * 1024 * 1024
+CORES = 2
 LANES = 128
 
 
-def prepare_kernel(sizes, place, rows, cols, tile_a, tile_b, out_a, out_b):
+def prepare_kernel(sizes, place, rows, cols, tile_a, tile_b, out_a, out_b, sems):
     held_a, held_b, blk, cut, owners = sizes
     whole_a, piece = held_a * blk, held_b * blk
     my_row, my_col = place[0], place[1]
-    out_a[pl.ds(0, whole_a), :] = tile_a[...]
-    out_b[pl.ds(0, piece), :] = tile_b[pl.ds(0, piece), :]
-    out_b[pl.ds(cut, piece), :] = tile_b[pl.ds(piece, piece), :]
+    copies = [
+        pltpu.make_async_copy(tile_a, out_a.at[pl.ds(0, whole_a), :], sems.at[0]),
+        pltpu.make_async_copy(tile_b.at[pl.ds(0, piece), :], out_b.at[pl.ds(0, piece), :], sems.at[1]),
+        pltpu.make_async_copy(tile_b.at[pl.ds(piece, piece), :], out_b.at[pl.ds(cut, piece), :], sems.at[2]),
+    ]
+    for copy in copies:
+        copy.start()
     lane = lax.broadcasted_iota(jnp.int32, (PAD, blk), 1) & (LANES // 2 - 1)
     spread = jnp.zeros((PAD, blk), jnp.int32)
     for a in range(held_a):
         spread = jnp.where(lane == my_row * held_a + a, rows[a] + 1, spread)
     out_a[pl.ds(whole_a, PAD), :] = spread.astype(jnp.float32).astype(out_a.dtype)
     spread = jnp.zeros((PAD, blk), jnp.int32)
-    for index in range(cols.shape[0]):
+    for index in range(2 * held_b):
         first = (my_col + index // held_b * owners) * held_a + index % held_b
-        spread = jnp.where(lane == first, cols[index] + 1, spread)
+        spread = jnp.where(lane == first, cols[index // held_b, index % held_b] + 1, spread)
     out_b[pl.ds(piece, PAD), :] = spread.astype(jnp.float32).astype(out_b.dtype)
+    for copy in copies:
+        copy.wait()
+
+
+def turned(distance, forward, count):
+    distance = jnp.where(forward, distance, count - distance) & (count - 1)
+    rank = jnp.zeros_like(distance)
+    for place, steps in enumerate(arrivals(count)):
+        rank = jnp.where(distance == steps % count, place, rank)
+    return rank
+
+
+def arrivals(count):
+    order, low, high = [0, 1], 0, 1
+    while len(order) < count:
+        order += [low - 1, low - 2]
+        low -= 2
+        if len(order) < count:
+            order += [high + 1, high + 2]
+            high += 2
+    return order
+
+
+def starts_forward(core, position):
+    return lax.rem(core + position, 2) == 0
 
 
 def listed(rows_seen, cols_seen, keep_rows, keep_cols, my_row, my_col, sizes):
     slots, held_a, held_b, holders, owners = sizes
+    chips = holders // CORES
+    my_core, my_chip = lax.rem(my_row, CORES), my_row // CORES
+    holder = lax.broadcasted_iota(jnp.int32, (8, LANES), 1)
+    core, chip = holder & (CORES - 1), (holder // CORES) & (chips - 1)
+    forward = ((core + my_chip) & 1) == 0
+    rank_a = turned((chip - my_chip + chips) & (chips - 1), forward, chips)
+    rank_a = rank_a + jnp.where(core == my_core, 0, chips)
+    offset = (holder + my_col - my_row + holders) & (holders - 1)
+    owner, piece = offset & (owners - 1), offset // owners
+    rank_b = turned((owner - my_col + owners) & (owners - 1), starts_forward(my_core, my_col), owners)
+    rank_a, rank_b = rank_a[:1] * held_a, ((rank_b * 2 + piece) * held_b)[:1]
     lane = lax.broadcasted_iota(jnp.int32, (LANES, LANES), 0)
     holder = lax.broadcasted_iota(jnp.int32, (LANES, LANES), 1)
     mine = (lane < holders * held_a) & ((lane // held_a) == holder)
-    pick_a = jnp.where(mine, lane + 1, 0)
-    apart = (holder - my_row + holders) & (owners - 1)
-    piece = ((holder + my_col - my_row + holders) & (holders - 1)) // owners
-    pick_b = jnp.where(mine, (apart * 2 + piece) * held_b + (lane & (held_a - 1)) + 1, 0)
+    pick_a = jnp.where(mine, rank_a + (lane & (held_a - 1)) + 1, 0)
+    pick_b = jnp.where(mine, rank_b + (lane & (held_a - 1)) + 1, 0)
     before = jnp.where(lane <= holder, 1, 0)
 
     def numbers(seen, wanted, pick):
@@ -114,15 +153,29 @@
     return lax.rem(place[2] + steps, shares) * each
 
 
-def far_kernel(sizes, shares, place, keep_rows, keep_cols, a_all, *rest):
-    parts, (coded, lists, b_all, total, scalar, sem) = rest[:-6], rest[-6:]
+def join_kernel(*refs):
+    parts, whole = refs[:-1], refs[-1]
+    at = 0
+    for part in parts:
+        size = part.shape[0]
+        whole[pl.ds(at, size)] = part[...]
+        at += size
+    blk = whole.shape[2]
+    whole[at, pl.ds(0, blk), :] = jnp.zeros((blk, blk), whole.dtype)
+
+
+def far_kernel(sizes, shares, count_a, place, keep_rows, keep_cols, *rest):
+    parts_a, b_all = rest[:count_a], rest[count_a]
+    coded, lists, a_all, total, scalar, sem = rest[count_a + 1 :]
     held_a, held_b, blk, cut = sizes
     holders, owners, slots = a_all.shape[0], b_all.shape[0] - 1, keep_rows.shape[0]
     each = slots // shares
     my_row, my_col = place[0], place[1]
-    for part, (owner, first) in zip(parts, rows_of(owners, cut)):
-        b_all[owner, pl.ds(first, part.shape[0]), :] = part[...]
-    b_all[owners, pl.ds(0, blk), :] = jnp.zeros((blk, blk), b_all.dtype)
+    at = 0
+    for part in parts_a:
+        size = part.shape[0]
+        a_all[pl.ds(at, size)] = part[...]
+        at += size
     rows_seen = jnp.sum(a_all[:, pl.ds(held_a * blk, PAD), pl.ds(0, LANES)].astype(jnp.float32), axis=0)
     cols_seen = jnp.sum(b_all[pl.ds(0, owners), pl.ds(cut - PAD, PAD), pl.ds(0, LANES)].astype(jnp.float32), axis=0)
     turn = (my_row - my_col + holders) & (holders - 1)
@@ -162,14 +215,28 @@
         out[slot] = (3.0 * square_kept[slot].astype(jnp.float32) - 2.0 * cube).astype(out.dtype)
 
 
-def rows_of(owners, cut):
-    half = owners // 2
-    return [(apart, 0) for apart in range(half)] + [(half, 0), (half, cut)] + [(apart, 0) for apart in range(half + 1, owners)]
+def exchanged(value, axes, sizes, axis, first):
+    rows, cols = sizes
+    pairs = []
+    for row in range(rows):
+        for col in range(cols):
+            core, chip = row % CORES, row // CORES
+            count, position = (rows // CORES, chip) if axis == "row" else (cols, col)
+            forward = ((core + position) % 2 == 0) == first
+            other = (position + (1 if forward else -1)) % count
+            partner = (other * CORES + core, col) if axis == "row" else (row, other)
+            pairs.append((row * cols + col, partner[0] * cols + partner[1]))
+    return lax.ppermute(value, axes, pairs)
 
 
 def shifted(value, axis, steps):
     count = lax.axis_size(axis)
     return lax.ppermute(value, axis, [(source, (source + steps) % count) for source in range(count)])
+
+
+def siblings(value):
+    count = lax.axis_size("row")
+    return lax.ppermute(value, "row", [(source, source ^ 1) for source in range(count)])
 
 
 def body(density_tiles, density_rows, square_tiles, square_cols, keep_rows, keep_cols, square_kept):
@@ -178,7 +245,6 @@
     held_a, blk = density_tiles.shape[3], density_tiles.shape[4]
     pieces, held_b = square_tiles.shape[3], square_tiles.shape[4]
     slots = keep_rows.shape[-1]
-    half = n_col // 2
     cut = held_b * blk + PAD
     place = jnp.stack([my_row, my_col, lax.axis_index("depth")]).astype(jnp.int32)
     smem = pl.BlockSpec(memory_space=pltpu.SMEM)
@@ -190,27 +256,39 @@
             jax.ShapeDtypeStruct((held_a * blk + PAD, blk), jnp.bfloat16),
             jax.ShapeDtypeStruct((cut + held_b * blk, blk), jnp.bfloat16),
         ],
-        in_specs=[smem] * 3 + [whole] * 2,
+        in_specs=[smem] * 3 + [pl.BlockSpec(memory_space=pl.ANY)] * 2,
         out_specs=[whole] * 2,
-        compiler_params=params,
+        scratch_shapes=[pltpu.SemaphoreType.DMA((3,))],
+        compiler_params=pltpu.CompilerParams(vmem_limit_bytes=60 * 1024 * 1024),
         name="prepare",
     )(
         place,
         density_rows[0, 0, 0],
-        square_cols[0, 0, 0].reshape(-1),
+        square_cols[0, 0, 0],
         density_tiles[0, 0, 0].reshape(held_a * blk, blk),
         square_tiles[0, 0, 0].reshape(pieces * held_b * blk, blk),
     )
-    a_all = lax.all_gather(tile_a, "row")
-
-    up, down = [tile_b], [tile_b]
-    for step in range(1, half + 1):
-        send_up, send_down = up[-1], down[-1]
-        if step == half:
-            send_up, send_down = send_up[:cut], send_down[cut:]
-        up.append(shifted(send_up, "col", 1))
-        down.append(shifted(send_down, "col", -1))
-    parts = down[:half] + [up[half], down[half]] + up[1:half][::-1]
+    tile_a, tile_b = tile_a[None], tile_b[None]
+
+    def swap(value, axis, turn):
+        return exchanged(value, ("row", "col"), (n_row, n_col), axis, turn % 2 == 0)
+
+    def both(turn, pair):
+        return [swap(pair[0], "row", turn), swap(pair[1], "col", turn)]
+
+    tiles = (tile_a, tile_b)
+    first = both(0, tiles)
+    second = both(1, tiles)
+    second = [jnp.concatenate(two) for two in zip(second, both(1, first))]
+    third = both(0, second)
+    fourth = both(1, third)
+    from_sibling = [
+        siblings(jnp.concatenate([tile_a, first[0], second[0]])),
+        siblings(third[0]),
+        siblings(fourth[0]),
+    ]
+    chain_a, chain_b = [list(parts) for parts in zip(tiles, first, second, third, fourth)]
+    parts_a, parts_b = chain_a + from_sibling, chain_b
 
     each = slots // n_depth
     sizes = (held_a, held_b, blk, cut)
@@ -220,14 +298,23 @@
     def cost(count):
         return pl.CostEstimate(flops=8 * count * blk**3, bytes_accessed=count * 2**20, transcendentals=0)
 
-    far, lists, b_all = pl.pallas_call(
-        functools.partial(far_kernel, sizes, n_depth),
+    b_all = pl.pallas_call(
+        join_kernel,
+        out_shape=jax.ShapeDtypeStruct((n_col + 1, cut + held_b * blk, blk), jnp.bfloat16),
+        in_specs=[whole] * len(parts_b),
+        out_specs=whole,
+        compiler_params=params,
+        cost_estimate=pl.CostEstimate(flops=10 * 10**9, bytes_accessed=8 * 2**20, transcendentals=0),
+        name="join",
+    )(*parts_b)
+    far, lists, a_all = pl.pallas_call(
+        functools.partial(far_kernel, sizes, n_depth, len(parts_a)),
         out_shape=[
             coded,
             jax.ShapeDtypeStruct((PAD, LANES), jnp.int32),
-            jax.ShapeDtypeStruct((n_col + 1, cut + held_b * blk, blk), jnp.bfloat16),
+            jax.ShapeDtypeStruct((n_row, held_a * blk + PAD, blk), jnp.bfloat16),
         ],
-        in_specs=[smem] * 3 + [whole] * (1 + len(parts)),
+        in_specs=[smem] * 3 + [whole] * (len(parts_a) + 1),
         out_specs=[whole] * 3,
         scratch_shapes=[
             pltpu.VMEM(summed, jnp.float32),
@@ -237,7 +324,7 @@
         compiler_params=params,
         cost_estimate=cost(each),
         name="far",
-    )(place, keep_rows[0, 0], keep_cols[0, 0], a_all, *parts)
+    )(place, keep_rows[0, 0], keep_cols[0, 0], *parts_a, b_all)
     far = shifted(far, "depth", 2)
     up, down = pl.pallas_call(
         functools.partial(near_kernel, sizes, n_depth, each),

time: 119 us -> 108 us (0.908)
  the two profiles are of different devices: /device:TPU:30 before, /device:TPU:1 now
where the time goes in v3:
time: 108 us
  starting transfers between devices  61.4 us (57%)
  waiting for transfers between devices  32.4 us (30%)
  Pallas kernels  12.4 us (11%)
    ppermute x10, starting transfers between devices, exchanged(): return lax.ppermute(value, axes, pairs)  36.8 us
    ppermute x10, waiting for transfers between devices, exchanged(): return lax.ppermute(value, axes, pairs)  22.5 us
    ppermute x3, starting transfers between devices, siblings(): lax.ppermute(value, 'row', [(source, source ^ 1) for source in range(coun...  13.7 us
    ppermute x3, starting transfers between devices, shifted(): lax.ppermute(value, axis, [(source, (source + steps) % count) for source...  10.9 us
    ppermute x3, waiting for transfers between devices, shifted(): lax.ppermute(value, axis, [(source, (source + steps) % count) for source...  7.99 us
    pallas_call x1, Pallas kernels, body(): pl.pallas_call(functools.partial(far_kernel, sizes, n_depth, len(parts_a)...  3.57 us
    pallas_call x1, Pallas kernels, body(): pl.pallas_call(functools.partial(prepare_kernel, (held_a, held_b, blk, cu...  2.94 us
    pallas_call x1, Pallas kernels, body(): pl.pallas_call(functools.partial(near_kernel, sizes, n_depth, each), out_...  2.81 us
  transfers between devices with their start and end apart: 16, of which 9 were waited for; matrix products, arithmetic and copies ran while one was open for 0% of the time, Pallas kernels for 4%

profile of v3, /device:TPU:1, one launch (start us, length us, event | category | flops | bytes accessed | tf_op | source)
XLA Modules:
  0.0 107.7 jit_solution(2522840311003959210)
XLA Ops:
  0.0 0.6 pad_add_fusion.place
  0.6 2.9 %prepare.1 = (bf16[1040,256]{1,0:T(8,128)(2,1)}, bf16[1040,256]{1,0:T(8,128)(2,1)}) custom-call(s32[3]{0:T(128)} %pad_add_fusion.place, s32[4]{0:T(128)} %bitcast.26, s32[2,2]{1,0:T(2,128)} %bitcast.25, bf16[1024,256]{1,0:T(8,128)(2,1)} %bitcast.23, bf16[1024,256]{1,0:T(8,128)(2,1)} %bitcast.24), custom_call_target="tpu_custom_call" | custom-call | tf_op jit(solution)/shard_map/prepare/pallas_call | solution.py:253
  3.6 5.9 %collective-permute-start = (bf16[1,1040,256]{2,1,0:T(8,128)(2,1)}, bf16[1,1040,256]{2,1,0:T(8,128)(2,1)S(1)}, u32[]{:S(2)}, u32[]{:S(2)}) collective-permute-start(bf16[1,1040,256]{2,1,0:T(8,128)(2,1)} %bitcast.13), channel_id=1, source_target_pairs={{0,64},{4,68},{8,72},{12,76},{16,80},{20,84},{24,88},{28,92},{32,4... | collective-permute-start | bytes 1597448 | tf_op jit(solution)/shard_map/ppermute | solution.py:229
  9.5 10.7 %collective-permute-start.8 = (bf16[1,1040,256]{2,1,0:T(8,128)(2,1)}, bf16[1,1040,256]{2,1,0:T(8,128)(2,1)S(1)}, u32[]{:S(2)}, u32[]{:S(2)}) collective-permute-start(bf16[1,1040,256]{2,1,0:T(8,128)(2,1)} %bitcast.20), channel_id=1, source_target_pairs={{0,4},{4,0},{8,12},{12,8},{16,20},{20,16},{24,28},{28,24},{32,60},... | collective-permute-start | bytes 1597448 | tf_op jit(solution)/shard_map/ppermute | solution.py:229
  20.2 1.9 %collective-permute-start.9 = (bf16[1,1040,256]{2,1,0:T(8,128)(2,1)}, bf16[1,1040,256]{2,1,0:T(8,128)(2,1)S(1)}, u32[]{:S(2)}, u32[]{:S(2)}) collective-permute-start(bf16[1,1040,256]{2,1,0:T(8,128)(2,1)} %bitcast.21), channel_id=1, source_target_pairs={{0,28},{4,8},{8,4},{12,16},{16,12},{20,24},{24,20},{28,0},{32,36},... | collective-permute-start | bytes 1597448 | tf_op jit(solution)/shard_map/ppermute | solution.py:229
  22.1 1.9 %collective-permute-start.1 = (bf16[1,1040,256]{2,1,0:T(8,128)(2,1)}, bf16[1,1040,256]{2,1,0:T(8,128)(2,1)S(1)}, u32[]{:S(2)}, u32[]{:S(2)}) collective-permute-start(bf16[1,1040,256]{2,1,0:T(8,128)(2,1)} %bitcast.14), channel_id=1, source_target_pairs={{0,448},{4,452},{8,456},{12,460},{16,464},{20,468},{24,472},{28,47... | collective-permute-start | bytes 1597448 | tf_op jit(solution)/shard_map/ppermute | solution.py:229
  24.1 0.0 collective-permute-done.rest_1_
  24.1 3.4 %collective-permute-start.2 = (bf16[1,1040,256]{2,1,0:T(8,128)(2,1)S(1)}, bf16[1,1040,256]{2,1,0:T(8,128)(2,1)S(1)}, u32[]{:S(2)}, u32[]{:S(2)}) collective-permute-start(bf16[1,1040,256]{2,1,0:T(8,128)(2,1)S(1)} %collective-permute-done.rest_1_), channel_id=1, source_target_pairs={{0,448},{4,452},{8,456},{12,460},{16,464},{20,468},{24,472},{28,47... | collective-permute-start | bytes 1597448 | tf_op jit(solution)/shard_map/ppermute | solution.py:229
  27.4 3.8 %collective-permute-done.8.refs_1_ = bf16[1,1040,256]{2,1,0:T(8,128)(2,1)S(1)} collective-permute-done((bf16[1,1040,256]{2,1,0:T(8,128)(2,1)}, bf16[1,1040,256]{2,1,0:T(8,128)(2,1)S(1)}, u32[]{:S(2)}, u32[]{:S(2)}) %collective-permute-start.8) | collective-permute-done | bytes 532512 | tf_op jit(solution)/shard_map/ppermute | solution.py:229
  31.3 1.9 %collective-permute-start.10 = (bf16[1,1040,256]{2,1,0:T(8,128)(2,1)S(1)}, bf16[1,1040,256]{2,1,0:T(8,128)(2,1)S(1)}, u32[]{:S(2)}, u32[]{:S(2)}) collective-permute-start(bf16[1,1040,256]{2,1,0:T(8,128)(2,1)S(1)} %collective-permute-done.8.refs_1_), channel_id=1, source_target_pairs={{0,28},{4,8},{8,4},{12,16},{16,12},{20,24},{24,20},{28,0},{32,36},... | collective-permute-start | bytes 1597448 | tf_op jit(solution)/shard_map/ppermute | solution.py:229
  33.2 0.0 collective-permute-done.9
  33.3 0.0 collective-permute-done.1
  33.3 0.0 copy-start
  33.3 5.0 %collective-permute-done.2 = bf16[1,1040,256]{2,1,0:T(8,128)(2,1)S(1)} collective-permute-done((bf16[1,1040,256]{2,1,0:T(8,128)(2,1)S(1)}, bf16[1,1040,256]{2,1,0:T(8,128)(2,1)S(1)}, u32[]{:S(2)}, u32[]{:S(2)}) %collective-permute-start.2) | collective-permute-done | bytes 532512 | tf_op jit(solution)/shard_map/ppermute | solution.py:229
  38.4 2.6 %collective-permute-start.3 = (bf16[2,1040,256]{2,1,0:T(8,128)(2,1)S(1)}, bf16[2,1040,256]{2,1,0:T(8,128)(2,1)S(1)}, u32[]{:S(2)}, u32[]{:S(2)}) collective-permute-start(bf16[2,1040,256]{2,1,0:T(8,128)(2,1)S(1)} %constant_dynamic-update-slice_fusion.rest_2_), channel_id=1, source_target_pairs={{0,64},{4,68},{8,72},{12,76},{16,80},{20,84},{24,88},{28,92},{32,4... | collective-permute-start | bytes 3194888 | tf_op jit(solution)/shard_map/ppermute | solution.py:229
  41.0 0.3 collective-permute-done.10
  41.3 0.0 copy-start.5
  41.3 4.7 %collective-permute-start.11 = (bf16[2,1040,256]{2,1,0:T(8,128)(2,1)S(1)}, bf16[2,1040,256]{2,1,0:T(8,128)(2,1)S(1)}, u32[]{:S(2)}, u32[]{:S(2)}) collective-permute-start(bf16[2,1040,256]{2,1,0:T(8,128)(2,1)S(1)} %constant_dynamic-update-slice_fusion.2.refs_2_), channel_id=1, source_target_pairs={{0,4},{4,0},{8,12},{12,8},{16,20},{20,16},{24,28},{28,24},{32,60},... | collective-permute-start | bytes 3194888 | tf_op jit(solution)/shard_map/ppermute | solution.py:229
  46.0 0.0 copy-done
  46.0 0.3 pad_maximum_fusion
  46.3 0.0 copy-start.2
  46.3 0.0 copy-start.3
  46.3 0.0 copy-start.4
  46.3 1.9 %collective-permute-start.5 = (bf16[4,1040,256]{2,1,0:T(8,128)(2,1)S(1)}, bf16[4,1040,256]{2,1,0:T(8,128)(2,1)S(1)}, u32[]{:S(2)}, u32[]{:S(2)}) collective-permute-start(bf16[4,1040,256]{2,1,0:T(8,128)(2,1)S(1)} %pad_maximum_fusion), channel_id=1, source_target_pairs={{0,32},{32,0},{64,96},{96,64},{128,160},{160,128},{192,224},{224,1... | collective-permute-start | bytes 6389768 | tf_op jit(solution)/shard_map/ppermute | solution.py:239
  48.3 7.1 %collective-permute-done.3.rest_3_ = bf16[2,1040,256]{2,1,0:T(8,128)(2,1)S(1)} collective-permute-done((bf16[2,1040,256]{2,1,0:T(8,128)(2,1)S(1)}, bf16[2,1040,256]{2,1,0:T(8,128)(2,1)S(1)}, u32[]{:S(2)}, u32[]{:S(2)}) %collective-permute-start.3) | collective-permute-done | bytes 1064992 | tf_op jit(solution)/shard_map/ppermute | solution.py:229
  55.3 1.9 %collective-permute-start.4 = (bf16[2,1040,256]{2,1,0:T(8,128)(2,1)S(1)}, bf16[2,1040,256]{2,1,0:T(8,128)(2,1)S(1)}, u32[]{:S(2)}, u32[]{:S(2)}) collective-permute-start(bf16[2,1040,256]{2,1,0:T(8,128)(2,1)S(1)} %collective-permute-done.3.rest_3_), channel_id=1, source_target_pairs={{0,448},{4,452},{8,456},{12,460},{16,464},{20,468},{24,472},{28,47... | collective-permute-start | bytes 3194888 | tf_op jit(solution)/shard_map/ppermute | solution.py:229
  57.2 1.2 %collective-permute-done.11.refs_3_ = bf16[2,1040,256]{2,1,0:T(8,128)(2,1)S(1)} collective-permute-done((bf16[2,1040,256]{2,1,0:T(8,128)(2,1)S(1)}, bf16[2,1040,256]{2,1,0:T(8,128)(2,1)S(1)}, u32[]{:S(2)}, u32[]{:S(2)}) %collective-permute-start.11) | collective-permute-done | bytes 1064992 | tf_op jit(solution)/shard_map/ppermute | solution.py:229
  58.4 1.9 %collective-permute-start.12 = (bf16[2,1040,256]{2,1,0:T(8,128)(2,1)S(1)}, bf16[2,1040,256]{2,1,0:T(8,128)(2,1)S(1)}, u32[]{:S(2)}, u32[]{:S(2)}) collective-permute-start(bf16[2,1040,256]{2,1,0:T(8,128)(2,1)S(1)} %collective-permute-done.11.refs_3_), channel_id=1, source_target_pairs={{0,28},{4,8},{8,4},{12,16},{16,12},{20,24},{24,20},{28,0},{32,36},... | collective-permute-start | bytes 3194888 | tf_op jit(solution)/shard_map/ppermute | solution.py:229
  60.3 5.9 %collective-permute-start.6 = (bf16[2,1040,256]{2,1,0:T(8,128)(2,1)S(1)}, bf16[2,1040,256]{2,1,0:T(8,128)(2,1)S(1)}, u32[]{:S(2)}, u32[]{:S(2)}) collective-permute-start(bf16[2,1040,256]{2,1,0:T(8,128)(2,1)S(1)} %collective-permute-done.3.rest_3_), channel_id=1, source_target_pairs={{0,32},{32,0},{64,96},{96,64},{128,160},{160,128},{192,224},{224,1... | collective-permute-start | bytes 3194888 | tf_op jit(solution)/shard_map/ppermute | solution.py:239
  66.2 5.1 %collective-permute-done.4.rest_4_ = bf16[2,1040,256]{2,1,0:T(8,128)(2,1)S(1)} collective-permute-done((bf16[2,1040,256]{2,1,0:T(8,128)(2,1)S(1)}, bf16[2,1040,256]{2,1,0:T(8,128)(2,1)S(1)}, u32[]{:S(2)}, u32[]{:S(2)}) %collective-permute-start.4) | collective-permute-done | bytes 1064992 | tf_op jit(solution)/shard_map/ppermute | solution.py:229
  71.3 5.9 %collective-permute-start.7 = (bf16[2,1040,256]{2,1,0:T(8,128)(2,1)S(1)}, bf16[2,1040,256]{2,1,0:T(8,128)(2,1)S(1)}, u32[]{:S(2)}, u32[]{:S(2)}) collective-permute-start(bf16[2,1040,256]{2,1,0:T(8,128)(2,1)S(1)} %collective-permute-done.4.rest_4_), channel_id=1, source_target_pairs={{0,32},{32,0},{64,96},{96,64},{128,160},{160,128},{192,224},{224,1... | collective-permute-start | bytes 3194888 | tf_op jit(solution)/shard_map/ppermute | solution.py:239
  77.2 0.0 collective-permute-done.12.refs_4_
  77.2 0.3 join.1.rest_8_.b_all
  77.5 0.0 collective-permute-done.6.rest_6_
  77.5 0.0 collective-permute-done.5.rest_5_
  77.5 2.0 %collective-permute-done.7.rest_7_ = bf16[2,1040,256]{2,1,0:T(8,128)(2,1)S(1)} collective-permute-done((bf16[2,1040,256]{2,1,0:T(8,128)(2,1)S(1)}, bf16[2,1040,256]{2,1,0:T(8,128)(2,1)S(1)}, u32[]{:S(2)}, u32[]{:S(2)}) %collective-permute-start.7) | collective-permute-done | bytes 1064992 | tf_op jit(solution)/shard_map/ppermute | solution.py:239
  79.5 0.0 copy-done.3
  79.5 3.6 %far.1 = (s16[816,256]{1,0:T(8,128)(2,1)S(1)}, s32[16,128]{1,0:T(8,128)S(1)}, bf16[16,1040,256]{2,1,0:T(8,128)(2,1)S(1)}) custom-call(s32[3]{0:T(128)S(1)} %copy-done.2, s32[12]{0:T(128)S(1)} %bitcast.18, s32[12]{0:T(128)S(1)} %bitcast.19, bf16[1,1040,256]{2,1,0:T(8,128)(2,1)S(1)} %bitcast.16, bf16[1,1040,256]{2,1,0:T(8,128)(2,1)S(1)} %collective-permute-done.rest_1_, ...), custom_call_target="tpu_custom_call" | custom-call | flops 402653184 | bytes 3145728 | tf_op jit(solution)/shard_map/far/pallas_call | solution.py:310
  83.1 4.3 %collective-permute-start.13 = (s16[816,256]{1,0:T(8,128)(2,1)S(1)}, s16[816,256]{1,0:T(8,128)(2,1)S(1)}, u32[]{:S(2)}, u32[]{:S(2)}) collective-permute-start(s16[816,256]{1,0:T(8,128)(2,1)S(1)} %get-tuple-element.14), channel_id=1, source_target_pairs={{0,2},{1,3},{2,0},{3,1},{4,6},{5,7},{6,4},{7,5},{8,10},{9,11},{10,... | collective-permute-start | bytes 1253384 | tf_op jit(solution)/shard_map/ppermute | solution.py:234
  87.4 2.8 %near.1 = (s16[816,256]{1,0:T(8,128)(2,1)S(1)}, s16[816,256]{1,0:T(8,128)(2,1)S(1)}) custom-call(s32[3]{0:T(128)S(1)} %copy-done.2, s32[16,128]{1,0:T(8,128)S(1)} %get-tuple-element.15.lists, bf16[16,1040,256]{2,1,0:T(8,128)(2,1)S(1)} %get-tuple-element.16.a_all, bf16[9,1040,256]{2,1,0:T(8,128)(2,1)S(1)} %join.1.rest_8_.b_all), custom_call_target="tpu_custom_call" | custom-call | flops 805306368 | bytes 6291456 | tf_op jit(solution)/shard_map/near/pallas_call | solution.py:329
  90.2 3.2 %collective-permute-start.14 = (s16[816,256]{1,0:T(8,128)(2,1)S(1)}, s16[816,256]{1,0:T(8,128)(2,1)S(1)}, u32[]{:S(2)}, u32[]{:S(2)}) collective-permute-start(s16[816,256]{1,0:T(8,128)(2,1)S(1)} %get-tuple-element.17), channel_id=1, source_target_pairs={{0,1},{1,2},{2,3},{3,0},{4,5},{5,6},{6,7},{7,4},{8,9},{9,10},{10,1... | collective-permute-start | bytes 1253384 | tf_op jit(solution)/shard_map/ppermute | solution.py:234
  93.5 0.0 copy-start.1
  93.5 3.4 %collective-permute-start.15 = (s16[816,256]{1,0:T(8,128)(2,1)S(1)}, s16[816,256]{1,0:T(8,128)(2,1)S(1)}, u32[]{:S(2)}, u32[]{:S(2)}) collective-permute-start(s16[816,256]{1,0:T(8,128)(2,1)S(1)} %get-tuple-element.18), channel_id=1, source_target_pairs={{0,3},{1,0},{2,1},{3,2},{4,7},{5,4},{6,5},{7,6},{8,11},{9,8},{10,9... | collective-permute-start | bytes 1253384 | tf_op jit(solution)/shard_map/ppermute | solution.py:234
  96.9 1.6 %own.1 = f32[3,256,256]{2,1,0:T(8,128)S(1)} custom-call(s32[3]{0:T(128)S(1)} %copy-done.2, s32[16,128]{1,0:T(8,128)S(1)} %get-tuple-element.15.lists, bf16[16,1040,256]{2,1,0:T(8,128)(2,1)S(1)} %get-tuple-element.16.a_all, bf16[9,1040,256]{2,1,0:T(8,128)(2,1)S(1)} %join.1.rest_8_.b_all), custom_call_target="tpu_custom_call" | custom-call | flops 402653184 | bytes 3145728 | tf_op jit(solution)/shard_map/own/pallas_call | solution.py:341
  98.5 0.0 collective-permute-done.13.far
  98.5 7.4 %collective-permute-done.14.up = s16[816,256]{1,0:T(8,128)(2,1)S(1)} collective-permute-done((s16[816,256]{1,0:T(8,128)(2,1)S(1)}, s16[816,256]{1,0:T(8,128)(2,1)S(1)}, u32[]{:S(2)}, u32[]{:S(2)}) %collective-permute-start.14) | collective-permute-done | bytes 417824 | tf_op jit(solution)/shard_map/ppermute | solution.py:234
  106.0 0.5 collective-permute-done.15.down
  106.5 1.2 %finish.1 = bf16[3,256,256]{2,1,0:T(8,128)(2,1)} custom-call(s16[816,256]{1,0:T(8,128)(2,1)S(1)} %collective-permute-done.13.far, s16[816,256]{1,0:T(8,128)(2,1)S(1)} %collective-permute-done.14.up, s16[816,256]{1,0:T(8,128)(2,1)S(1)} %collective-permute-done.15.down, f32[3,256,256]{2,1,0:T(8,128)S(1)} %own.1, bf16[3,256,256]{2,1,0:T(8,128)(2,1)S(1)} %bitcast.17), custom_call_target="tpu_custom_call" | custom-call | flops 2097152 | bytes 3145728 | tf_op jit(solution)/shard_map/finish/pallas_call | solution.py:350
  (8 shorter events, 0.2 us)
Async XLA Ops:
  3.6 20.5 %collective-permute-start = (bf16[1,1040,256]{2,1,0:T(8,128)(2,1)}, bf16[1,1040,256]{2,1,0:T(8,128)(2,1)S(1)}, u32[]{:S(2)}, u32[]{:S(2)}) collective-permute-start(bf16[1,1040,256]{2,1,0:T(8,128)(2,1)} %bitcast.13), channel_id=1, source_target_pairs={{0,64},{4,68},{8,72},{12,76},{16,80},{20,84},{24,88},{28,92},{32,4... | collective-permute-start | bytes 1597448 | tf_op jit(solution)/shard_map/ppermute | solution.py:229
  9.5 21.8 %collective-permute-start.8 = (bf16[1,1040,256]{2,1,0:T(8,128)(2,1)}, bf16[1,1040,256]{2,1,0:T(8,128)(2,1)S(1)}, u32[]{:S(2)}, u32[]{:S(2)}) collective-permute-start(bf16[1,1040,256]{2,1,0:T(8,128)(2,1)} %bitcast.20), channel_id=1, source_target_pairs={{0,4},{4,0},{8,12},{12,8},{16,20},{20,16},{24,28},{28,24},{32,60},... | collective-permute-start | bytes 1597448 | tf_op jit(solution)/shard_map/ppermute | solution.py:229
  20.2 13.0 %collective-permute-start.9 = (bf16[1,1040,256]{2,1,0:T(8,128)(2,1)}, bf16[1,1040,256]{2,1,0:T(8,128)(2,1)S(1)}, u32[]{:S(2)}, u32[]{:S(2)}) collective-permute-start(bf16[1,1040,256]{2,1,0:T(8,128)(2,1)} %bitcast.21), channel_id=1, source_target_pairs={{0,28},{4,8},{8,4},{12,16},{16,12},{20,24},{24,20},{28,0},{32,36},... | collective-permute-start | bytes 1597448 | tf_op jit(solution)/shard_map/ppermute | solution.py:229
  22.1 11.1 %collective-permute-start.1 = (bf16[1,1040,256]{2,1,0:T(8,128)(2,1)}, bf16[1,1040,256]{2,1,0:T(8,128)(2,1)S(1)}, u32[]{:S(2)}, u32[]{:S(2)}) collective-permute-start(bf16[1,1040,256]{2,1,0:T(8,128)(2,1)} %bitcast.14), channel_id=1, source_target_pairs={{0,448},{4,452},{8,456},{12,460},{16,464},{20,468},{24,472},{28,47... | collective-permute-start | bytes 1597448 | tf_op jit(solution)/shard_map/ppermute | solution.py:229
  24.1 14.3 %collective-permute-start.2 = (bf16[1,1040,256]{2,1,0:T(8,128)(2,1)S(1)}, bf16[1,1040,256]{2,1,0:T(8,128)(2,1)S(1)}, u32[]{:S(2)}, u32[]{:S(2)}) collective-permute-start(bf16[1,1040,256]{2,1,0:T(8,128)(2,1)S(1)} %collective-permute-done.rest_1_), channel_id=1, source_target_pairs={{0,448},{4,452},{8,456},{12,460},{16,464},{20,468},{24,472},{28,47... | collective-permute-start | bytes 1597448 | tf_op jit(solution)/shard_map/ppermute | solution.py:229
  31.3 10.0 %collective-permute-start.10 = (bf16[1,1040,256]{2,1,0:T(8,128)(2,1)S(1)}, bf16[1,1040,256]{2,1,0:T(8,128)(2,1)S(1)}, u32[]{:S(2)}, u32[]{:S(2)}) collective-permute-start(bf16[1,1040,256]{2,1,0:T(8,128)(2,1)S(1)} %collective-permute-done.8.refs_1_), channel_id=1, source_target_pairs={{0,28},{4,8},{8,4},{12,16},{16,12},{20,24},{24,20},{28,0},{32,36},... | collective-permute-start | bytes 1597448 | tf_op jit(solution)/shard_map/ppermute | solution.py:229
  33.3 12.7 %copy-start = (bf16[1040,256]{1,0:T(8,128)(2,1)S(1)}, bf16[1040,256]{1,0:T(8,128)(2,1)}, u32[]{:S(2)}) copy-start(bf16[1040,256]{1,0:T(8,128)(2,1)} %get-tuple-element.12) | copy-start | bytes 1597444
  38.4 16.9 %collective-permute-start.3 = (bf16[2,1040,256]{2,1,0:T(8,128)(2,1)S(1)}, bf16[2,1040,256]{2,1,0:T(8,128)(2,1)S(1)}, u32[]{:S(2)}, u32[]{:S(2)}) collective-permute-start(bf16[2,1040,256]{2,1,0:T(8,128)(2,1)S(1)} %constant_dynamic-update-slice_fusion.rest_2_), channel_id=1, source_target_pairs={{0,64},{4,68},{8,72},{12,76},{16,80},{20,84},{24,88},{28,92},{32,4... | collective-permute-start | bytes 3194888 | tf_op jit(solution)/shard_map/ppermute | solution.py:229
  41.3 35.9 %copy-start.5 = (bf16[1040,256]{1,0:T(8,128)(2,1)S(1)}, bf16[1040,256]{1,0:T(8,128)(2,1)}, u32[]{:S(2)}) copy-start(bf16[1040,256]{1,0:T(8,128)(2,1)} %get-tuple-element.13) | copy-start | bytes 1597444
  41.3 17.1 %collective-permute-start.11 = (bf16[2,1040,256]{2,1,0:T(8,128)(2,1)S(1)}, bf16[2,1040,256]{2,1,0:T(8,128)(2,1)S(1)}, u32[]{:S(2)}, u32[]{:S(2)}) collective-permute-start(bf16[2,1040,256]{2,1,0:T(8,128)(2,1)S(1)} %constant_dynamic-update-slice_fusion.2.refs_2_), channel_id=1, source_target_pairs={{0,4},{4,0},{8,12},{12,8},{16,20},{20,16},{24,28},{28,24},{32,60},... | collective-permute-start | bytes 3194888 | tf_op jit(solution)/shard_map/ppermute | solution.py:229
  46.3 33.2 %copy-start.2 = (s32[3]{0:T(128)S(1)}, s32[3]{0:T(128)}, u32[]{:S(2)}) copy-start(s32[3]{0:T(128)} %pad_add_fusion.place) | copy-start | bytes 40
  46.3 33.2 %copy-start.3 = (s32[1,1,12]{2,1,0:T(1,128)S(1)}, s32[1,1,12]{2,1,0:T(1,128)}, u32[]{:S(2)}) copy-start(s32[1,1,12]{2,1,0:T(1,128)} %param.11) | copy-start | bytes 148
  46.3 33.2 %copy-start.4 = (s32[1,1,12]{2,1,0:T(1,128)S(1)}, s32[1,1,12]{2,1,0:T(1,128)}, u32[]{:S(2)}) copy-start(s32[1,1,12]{2,1,0:T(1,128)} %param.12) | copy-start | bytes 148
  46.3 31.2 %collective-permute-start.5 = (bf16[4,1040,256]{2,1,0:T(8,128)(2,1)S(1)}, bf16[4,1040,256]{2,1,0:T(8,128)(2,1)S(1)}, u32[]{:S(2)}, u32[]{:S(2)}) collective-permute-start(bf16[4,1040,256]{2,1,0:T(8,128)(2,1)S(1)} %pad_maximum_fusion), channel_id=1, source_target_pairs={{0,32},{32,0},{64,96},{96,64},{128,160},{160,128},{192,224},{224,1... | collective-permute-start | bytes 6389768 | tf_op jit(solution)/shard_map/ppermute | solution.py:239
  55.3 16.0 %collective-permute-start.4 = (bf16[2,1040,256]{2,1,0:T(8,128)(2,1)S(1)}, bf16[2,1040,256]{2,1,0:T(8,128)(2,1)S(1)}, u32[]{:S(2)}, u32[]{:S(2)}) collective-permute-start(bf16[2,1040,256]{2,1,0:T(8,128)(2,1)S(1)} %collective-permute-done.3.rest_3_), channel_id=1, source_target_pairs={{0,448},{4,452},{8,456},{12,460},{16,464},{20,468},{24,472},{28,47... | collective-permute-start | bytes 3194888 | tf_op jit(solution)/shard_map/ppermute | solution.py:229
  58.4 18.8 %collective-permute-start.12 = (bf16[2,1040,256]{2,1,0:T(8,128)(2,1)S(1)}, bf16[2,1040,256]{2,1,0:T(8,128)(2,1)S(1)}, u32[]{:S(2)}, u32[]{:S(2)}) collective-permute-start(bf16[2,1040,256]{2,1,0:T(8,128)(2,1)S(1)} %collective-permute-done.11.refs_3_), channel_id=1, source_target_pairs={{0,28},{4,8},{8,4},{12,16},{16,12},{20,24},{24,20},{28,0},{32,36},... | collective-permute-start | bytes 3194888 | tf_op jit(solution)/shard_map/ppermute | solution.py:229
  60.3 17.2 %collective-permute-start.6 = (bf16[2,1040,256]{2,1,0:T(8,128)(2,1)S(1)}, bf16[2,1040,256]{2,1,0:T(8,128)(2,1)S(1)}, u32[]{:S(2)}, u32[]{:S(2)}) collective-permute-start(bf16[2,1040,256]{2,1,0:T(8,128)(2,1)S(1)} %collective-permute-done.3.rest_3_), channel_id=1, source_target_pairs={{0,32},{32,0},{64,96},{96,64},{128,160},{160,128},{192,224},{224,1... | collective-permute-start | bytes 3194888 | tf_op jit(solution)/shard_map/ppermute | solution.py:239
  71.3 8.2 %collective-permute-start.7 = (bf16[2,1040,256]{2,1,0:T(8,128)(2,1)S(1)}, bf16[2,1040,256]{2,1,0:T(8,128)(2,1)S(1)}, u32[]{:S(2)}, u32[]{:S(2)}) collective-permute-start(bf16[2,1040,256]{2,1,0:T(8,128)(2,1)S(1)} %collective-permute-done.4.rest_4_), channel_id=1, source_target_pairs={{0,32},{32,0},{64,96},{96,64},{128,160},{160,128},{192,224},{224,1... | collective-permute-start | bytes 3194888 | tf_op jit(solution)/shard_map/ppermute | solution.py:239
  83.1 15.4 %collective-permute-start.13 = (s16[816,256]{1,0:T(8,128)(2,1)S(1)}, s16[816,256]{1,0:T(8,128)(2,1)S(1)}, u32[]{:S(2)}, u32[]{:S(2)}) collective-permute-start(s16[816,256]{1,0:T(8,128)(2,1)S(1)} %get-tuple-element.14), channel_id=1, source_target_pairs={{0,2},{1,3},{2,0},{3,1},{4,6},{5,7},{6,4},{7,5},{8,10},{9,11},{10,... | collective-permute-start | bytes 1253384 | tf_op jit(solution)/shard_map/ppermute | solution.py:234
  90.2 15.8 %collective-permute-start.14 = (s16[816,256]{1,0:T(8,128)(2,1)S(1)}, s16[816,256]{1,0:T(8,128)(2,1)S(1)}, u32[]{:S(2)}, u32[]{:S(2)}) collective-permute-start(s16[816,256]{1,0:T(8,128)(2,1)S(1)} %get-tuple-element.17), channel_id=1, source_target_pairs={{0,1},{1,2},{2,3},{3,0},{4,5},{5,6},{6,7},{7,4},{8,9},{9,10},{10,1... | collective-permute-start | bytes 1253384 | tf_op jit(solution)/shard_map/ppermute | solution.py:234
  93.5 13.0 %copy-start.1 = (bf16[1,1,3,256,256]{4,3,2,1,0:T(8,128)(2,1)S(1)}, bf16[1,1,3,256,256]{4,3,2,1,0:T(8,128)(2,1)}, u32[]{:S(2)}) copy-start(bf16[1,1,3,256,256]{4,3,2,1,0:T(8,128)(2,1)} %param.13) | copy-start | bytes 1179652
  93.5 13.0 %collective-permute-start.15 = (s16[816,256]{1,0:T(8,128)(2,1)S(1)}, s16[816,256]{1,0:T(8,128)(2,1)S(1)}, u32[]{:S(2)}, u32[]{:S(2)}) collective-permute-start(s16[816,256]{1,0:T(8,128)(2,1)S(1)} %get-tuple-element.18), channel_id=1, source_target_pairs={{0,3},{1,0},{2,1},{3,2},{4,7},{5,4},{6,5},{7,6},{8,11},{9,8},{10,9... | collective-permute-start | bytes 1253384 | tf_op jit(solution)/shard_map/ppermute | solution.py:234

commit v4 on v3

--- a/solution.py
+++ b/solution.py
@@ -145,8 +145,15 @@
     power = jnp.ceil(FINER * jnp.log2(largest / LEVELS))
     values = jnp.round(total[index] * jnp.exp2(power * (-1.0 / FINER)))
     coded[pl.ds(inside * blk, blk), :] = values.astype(jnp.int32).astype(jnp.int16)
-    powers = jnp.broadcast_to(power, (PAD, blk)).astype(jnp.int32).astype(jnp.int16)
-    coded[pl.ds(each * blk + inside * PAD, PAD), :] = powers
+    return power
+
+
+def keep_powers(powers, coded, first):
+    row = lax.broadcasted_iota(jnp.int32, (PAD, coded.shape[1]), 0)
+    value = jnp.zeros(row.shape, jnp.float32)
+    for index, power in enumerate(powers):
+        value = jnp.where(row == index, power, value)
+    coded[pl.ds(first, PAD), :] = value.astype(jnp.int32).astype(jnp.int16)
 
 
 def target(place, steps, shares, each):
@@ -187,17 +194,15 @@
     copy.start()
     copy.wait()
     multiply(sizes, scalar, a_all, b_all, target(place, 2, shares, each), total)
-    for index in range(each):
-        encode(total, index, coded, index, blk, each)
+    keep_powers([encode(total, index, coded, index, blk, each) for index in range(each)], coded, each * blk)
 
 
 def near_kernel(sizes, shares, each, place, lists, a_all, b_all, coded_up, coded_down, total_up, total_down):
     blk = sizes[2]
     multiply(sizes, lists, a_all, b_all, target(place, 1, shares, each), total_up)
     multiply(sizes, lists, a_all, b_all, target(place, shares - 1, shares, each), total_down)
-    for index in range(each):
-        encode(total_up, index, coded_up, index, blk, each)
-        encode(total_down, index, coded_down, index, blk, each)
+    for total, coded in ((total_up, coded_up), (total_down, coded_down)):
+        keep_powers([encode(total, index, coded, index, blk, each) for index in range(each)], coded, each * blk)
 
 
 def own_kernel(sizes, shares, each, place, lists, a_all, b_all, total):
@@ -209,7 +214,7 @@
     for slot in range(each):
         cube = own[slot]
         for coded in (far, up, down):
-            power = coded[pl.ds(each * blk + slot * PAD, PAD), :].astype(jnp.int32).astype(jnp.float32)[:1]
+            power = coded[pl.ds(each * blk, PAD), :].astype(jnp.int32).astype(jnp.float32)[slot : slot + 1]
             values = coded[pl.ds(slot * blk, blk), :].astype(jnp.int32).astype(jnp.float32)
             cube = cube + values * jnp.exp2(power * (1.0 / FINER))
         out[slot] = (3.0 * square_kept[slot].astype(jnp.float32) - 2.0 * cube).astype(out.dtype)
@@ -292,7 +297,7 @@
 
     each = slots // n_depth
     sizes = (held_a, held_b, blk, cut)
-    coded = jax.ShapeDtypeStruct((each * (blk + PAD), blk), jnp.int16)
+    coded = jax.ShapeDtypeStruct((each * blk + PAD, blk), jnp.int16)
     summed = (each, blk, blk)
 
     def cost(count):

time: 108 us -> 108 us (level); the launches traced: 108 us -> 106 us
  waiting for transfers between devices: 32.4 us -> 30.9 us
    ppermute x3, waiting for transfers between devices: 7.99 us -> 6.47 us  [shifted(): lax.ppermute(value, axis, [(source, (source + steps) % count) for source...]
  transfers between devices with their start and end apart: 16 -> 16, of which waited for: 9 -> 8; matrix products, arithmetic and copies ran while one was open for 0% -> 0% of each run, Pallas kernels for 4% -> 4%
where the time goes in v4:
time: 108 us; the launch traced here: 106 us
  starting transfers between devices  61.8 us (57%)
  waiting for transfers between devices  30.9 us (29%)
  Pallas kernels  11.8 us (11%)
    ppermute x10, starting transfers between devices, exchanged(): return lax.ppermute(value, axes, pairs)  36.8 us
    ppermute x10, waiting for transfers between devices, exchanged(): return lax.ppermute(value, axes, pairs)  22.5 us
    ppermute x3, starting transfers between devices, siblings(): lax.ppermute(value, 'row', [(source, source ^ 1) for source in range(coun...  13.7 us
    ppermute x3, starting transfers between devices, shifted(): lax.ppermute(value, axis, [(source, (source + steps) % count) for source...  11.3 us
    ppermute x3, waiting for transfers between devices, shifted(): lax.ppermute(value, axis, [(source, (source + steps) % count) for source...  6.47 us
    pallas_call x1, Pallas kernels, body(): pl.pallas_call(functools.partial(prepare_kernel, (held_a, held_b, blk, cu...  2.94 us
    pallas_call x1, Pallas kernels, body(): pl.pallas_call(functools.partial(far_kernel, sizes, n_depth, len(parts_a)...  2.92 us
    pallas_call x1, Pallas kernels, body(): pl.pallas_call(functools.partial(near_kernel, sizes, n_depth, each), out_...  2.82 us
  transfers between devices with their start and end apart: 16, of which 8 were waited for; matrix products, arithmetic and copies ran while one was open for 0% of the time, Pallas kernels for 4%

profile of v4, /device:TPU:1, one launch (start us, length us, event | category | flops | bytes accessed | tf_op | source)
XLA Modules:
  0.0 105.9 jit_solution(804202636139177633)
XLA Ops:
  0.0 0.6 pad_add_fusion.place
  0.6 2.9 %prepare.1 = (bf16[1040,256]{1,0:T(8,128)(2,1)}, bf16[1040,256]{1,0:T(8,128)(2,1)}) custom-call(s32[3]{0:T(128)} %pad_add_fusion.place, s32[4]{0:T(128)} %bitcast.26, s32[2,2]{1,0:T(2,128)} %bitcast.25, bf16[1024,256]{1,0:T(8,128)(2,1)} %bitcast.23, bf16[1024,256]{1,0:T(8,128)(2,1)} %bitcast.24), custom_call_target="tpu_custom_call" | custom-call | tf_op jit(solution)/shard_map/prepare/pallas_call | solution.py:258
  3.6 5.9 %collective-permute-start = (bf16[1,1040,256]{2,1,0:T(8,128)(2,1)}, bf16[1,1040,256]{2,1,0:T(8,128)(2,1)S(1)}, u32[]{:S(2)}, u32[]{:S(2)}) collective-permute-start(bf16[1,1040,256]{2,1,0:T(8,128)(2,1)} %bitcast.13), channel_id=1, source_target_pairs={{0,64},{4,68},{8,72},{12,76},{16,80},{20,84},{24,88},{28,92},{32,4... | collective-permute-start | bytes 1597448 | tf_op jit(solution)/shard_map/ppermute | solution.py:234
  9.5 10.7 %collective-permute-start.8 = (bf16[1,1040,256]{2,1,0:T(8,128)(2,1)}, bf16[1,1040,256]{2,1,0:T(8,128)(2,1)S(1)}, u32[]{:S(2)}, u32[]{:S(2)}) collective-permute-start(bf16[1,1040,256]{2,1,0:T(8,128)(2,1)} %bitcast.20), channel_id=1, source_target_pairs={{0,4},{4,0},{8,12},{12,8},{16,20},{20,16},{24,28},{28,24},{32,60},... | collective-permute-start | bytes 1597448 | tf_op jit(solution)/shard_map/ppermute | solution.py:234
  20.2 1.9 %collective-permute-start.9 = (bf16[1,1040,256]{2,1,0:T(8,128)(2,1)}, bf16[1,1040,256]{2,1,0:T(8,128)(2,1)S(1)}, u32[]{:S(2)}, u32[]{:S(2)}) collective-permute-start(bf16[1,1040,256]{2,1,0:T(8,128)(2,1)} %bitcast.21), channel_id=1, source_target_pairs={{0,28},{4,8},{8,4},{12,16},{16,12},{20,24},{24,20},{28,0},{32,36},... | collective-permute-start | bytes 1597448 | tf_op jit(solution)/shard_map/ppermute | solution.py:234
  22.1 1.9 %collective-permute-start.1 = (bf16[1,1040,256]{2,1,0:T(8,128)(2,1)}, bf16[1,1040,256]{2,1,0:T(8,128)(2,1)S(1)}, u32[]{:S(2)}, u32[]{:S(2)}) collective-permute-start(bf16[1,1040,256]{2,1,0:T(8,128)(2,1)} %bitcast.14), channel_id=1, source_target_pairs={{0,448},{4,452},{8,456},{12,460},{16,464},{20,468},{24,472},{28,47... | collective-permute-start | bytes 1597448 | tf_op jit(solution)/shard_map/ppermute | solution.py:234
  24.1 0.0 collective-permute-done.rest_1_
  24.1 3.4 %collective-permute-start.2 = (bf16[1,1040,256]{2,1,0:T(8,128)(2,1)S(1)}, bf16[1,1040,256]{2,1,0:T(8,128)(2,1)S(1)}, u32[]{:S(2)}, u32[]{:S(2)}) collective-permute-start(bf16[1,1040,256]{2,1,0:T(8,128)(2,1)S(1)} %collective-permute-done.rest_1_), channel_id=1, source_target_pairs={{0,448},{4,452},{8,456},{12,460},{16,464},{20,468},{24,472},{28,47... | collective-permute-start | bytes 1597448 | tf_op jit(solution)/shard_map/ppermute | solution.py:234
  27.4 3.8 %collective-permute-done.8.refs_1_ = bf16[1,1040,256]{2,1,0:T(8,128)(2,1)S(1)} collective-permute-done((bf16[1,1040,256]{2,1,0:T(8,128)(2,1)}, bf16[1,1040,256]{2,1,0:T(8,128)(2,1)S(1)}, u32[]{:S(2)}, u32[]{:S(2)}) %collective-permute-start.8) | collective-permute-done | bytes 532512 | tf_op jit(solution)/shard_map/ppermute | solution.py:234
  31.3 1.9 %collective-permute-start.10 = (bf16[1,1040,256]{2,1,0:T(8,128)(2,1)S(1)}, bf16[1,1040,256]{2,1,0:T(8,128)(2,1)S(1)}, u32[]{:S(2)}, u32[]{:S(2)}) collective-permute-start(bf16[1,1040,256]{2,1,0:T(8,128)(2,1)S(1)} %collective-permute-done.8.refs_1_), channel_id=1, source_target_pairs={{0,28},{4,8},{8,4},{12,16},{16,12},{20,24},{24,20},{28,0},{32,36},... | collective-permute-start | bytes 1597448 | tf_op jit(solution)/shard_map/ppermute | solution.py:234
  33.2 0.0 collective-permute-done.9
  33.3 0.0 collective-permute-done.1
  33.3 0.0 copy-start
  33.3 5.0 %collective-permute-done.2 = bf16[1,1040,256]{2,1,0:T(8,128)(2,1)S(1)} collective-permute-done((bf16[1,1040,256]{2,1,0:T(8,128)(2,1)S(1)}, bf16[1,1040,256]{2,1,0:T(8,128)(2,1)S(1)}, u32[]{:S(2)}, u32[]{:S(2)}) %collective-permute-start.2) | collective-permute-done | bytes 532512 | tf_op jit(solution)/shard_map/ppermute | solution.py:234
  38.4 2.6 %collective-permute-start.3 = (bf16[2,1040,256]{2,1,0:T(8,128)(2,1)S(1)}, bf16[2,1040,256]{2,1,0:T(8,128)(2,1)S(1)}, u32[]{:S(2)}, u32[]{:S(2)}) collective-permute-start(bf16[2,1040,256]{2,1,0:T(8,128)(2,1)S(1)} %constant_dynamic-update-slice_fusion.rest_2_), channel_id=1, source_target_pairs={{0,64},{4,68},{8,72},{12,76},{16,80},{20,84},{24,88},{28,92},{32,4... | collective-permute-start | bytes 3194888 | tf_op jit(solution)/shard_map/ppermute | solution.py:234
  41.0 0.3 collective-permute-done.10
  41.3 0.0 copy-start.5
  41.3 4.7 %collective-permute-start.11 = (bf16[2,1040,256]{2,1,0:T(8,128)(2,1)S(1)}, bf16[2,1040,256]{2,1,0:T(8,128)(2,1)S(1)}, u32[]{:S(2)}, u32[]{:S(2)}) collective-permute-start(bf16[2,1040,256]{2,1,0:T(8,128)(2,1)S(1)} %constant_dynamic-update-slice_fusion.2.refs_2_), channel_id=1, source_target_pairs={{0,4},{4,0},{8,12},{12,8},{16,20},{20,16},{24,28},{28,24},{32,60},... | collective-permute-start | bytes 3194888 | tf_op jit(solution)/shard_map/ppermute | solution.py:234
  46.0 0.0 copy-done
  46.0 0.3 pad_maximum_fusion
  46.3 0.0 copy-start.3
  46.3 0.0 copy-start.4
  46.3 1.9 %collective-permute-start.5 = (bf16[4,1040,256]{2,1,0:T(8,128)(2,1)S(1)}, bf16[4,1040,256]{2,1,0:T(8,128)(2,1)S(1)}, u32[]{:S(2)}, u32[]{:S(2)}) collective-permute-start(bf16[4,1040,256]{2,1,0:T(8,128)(2,1)S(1)} %pad_maximum_fusion), channel_id=1, source_target_pairs={{0,32},{32,0},{64,96},{96,64},{128,160},{160,128},{192,224},{224,1... | collective-permute-start | bytes 6389768 | tf_op jit(solution)/shard_map/ppermute | solution.py:244
  48.3 7.1 %collective-permute-done.3.rest_3_ = bf16[2,1040,256]{2,1,0:T(8,128)(2,1)S(1)} collective-permute-done((bf16[2,1040,256]{2,1,0:T(8,128)(2,1)S(1)}, bf16[2,1040,256]{2,1,0:T(8,128)(2,1)S(1)}, u32[]{:S(2)}, u32[]{:S(2)}) %collective-permute-start.3) | collective-permute-done | bytes 1064992 | tf_op jit(solution)/shard_map/ppermute | solution.py:234
  55.3 1.9 %collective-permute-start.4 = (bf16[2,1040,256]{2,1,0:T(8,128)(2,1)S(1)}, bf16[2,1040,256]{2,1,0:T(8,128)(2,1)S(1)}, u32[]{:S(2)}, u32[]{:S(2)}) collective-permute-start(bf16[2,1040,256]{2,1,0:T(8,128)(2,1)S(1)} %collective-permute-done.3.rest_3_), channel_id=1, source_target_pairs={{0,448},{4,452},{8,456},{12,460},{16,464},{20,468},{24,472},{28,47... | collective-permute-start | bytes 3194888 | tf_op jit(solution)/shard_map/ppermute | solution.py:234
  57.2 1.2 %collective-permute-done.11.refs_3_ = bf16[2,1040,256]{2,1,0:T(8,128)(2,1)S(1)} collective-permute-done((bf16[2,1040,256]{2,1,0:T(8,128)(2,1)S(1)}, bf16[2,1040,256]{2,1,0:T(8,128)(2,1)S(1)}, u32[]{:S(2)}, u32[]{:S(2)}) %collective-permute-start.11) | collective-permute-done | bytes 1064992 | tf_op jit(solution)/shard_map/ppermute | solution.py:234
  58.4 1.9 %collective-permute-start.12 = (bf16[2,1040,256]{2,1,0:T(8,128)(2,1)S(1)}, bf16[2,1040,256]{2,1,0:T(8,128)(2,1)S(1)}, u32[]{:S(2)}, u32[]{:S(2)}) collective-permute-start(bf16[2,1040,256]{2,1,0:T(8,128)(2,1)S(1)} %collective-permute-done.11.refs_3_), channel_id=1, source_target_pairs={{0,28},{4,8},{8,4},{12,16},{16,12},{20,24},{24,20},{28,0},{32,36},... | collective-permute-start | bytes 3194888 | tf_op jit(solution)/shard_map/ppermute | solution.py:234
  60.3 5.9 %collective-permute-start.6 = (bf16[2,1040,256]{2,1,0:T(8,128)(2,1)S(1)}, bf16[2,1040,256]{2,1,0:T(8,128)(2,1)S(1)}, u32[]{:S(2)}, u32[]{:S(2)}) collective-permute-start(bf16[2,1040,256]{2,1,0:T(8,128)(2,1)S(1)} %collective-permute-done.3.rest_3_), channel_id=1, source_target_pairs={{0,32},{32,0},{64,96},{96,64},{128,160},{160,128},{192,224},{224,1... | collective-permute-start | bytes 3194888 | tf_op jit(solution)/shard_map/ppermute | solution.py:244
  66.2 5.1 %collective-permute-done.4.rest_4_ = bf16[2,1040,256]{2,1,0:T(8,128)(2,1)S(1)} collective-permute-done((bf16[2,1040,256]{2,1,0:T(8,128)(2,1)S(1)}, bf16[2,1040,256]{2,1,0:T(8,128)(2,1)S(1)}, u32[]{:S(2)}, u32[]{:S(2)}) %collective-permute-start.4) | collective-permute-done | bytes 1064992 | tf_op jit(solution)/shard_map/ppermute | solution.py:234
  71.3 5.9 %collective-permute-start.7 = (bf16[2,1040,256]{2,1,0:T(8,128)(2,1)S(1)}, bf16[2,1040,256]{2,1,0:T(8,128)(2,1)S(1)}, u32[]{:S(2)}, u32[]{:S(2)}) collective-permute-start(bf16[2,1040,256]{2,1,0:T(8,128)(2,1)S(1)} %collective-permute-done.4.rest_4_), channel_id=1, source_target_pairs={{0,32},{32,0},{64,96},{96,64},{128,160},{160,128},{192,224},{224,1... | collective-permute-start | bytes 3194888 | tf_op jit(solution)/shard_map/ppermute | solution.py:244
  77.2 0.0 collective-permute-done.12.refs_4_
  77.2 0.3 join.1.rest_8_.b_all
  77.5 0.0 collective-permute-done.6.rest_6_
  77.5 0.0 collective-permute-done.5.rest_5_
  77.5 2.0 %collective-permute-done.7.rest_7_ = bf16[2,1040,256]{2,1,0:T(8,128)(2,1)S(1)} collective-permute-done((bf16[2,1040,256]{2,1,0:T(8,128)(2,1)S(1)}, bf16[2,1040,256]{2,1,0:T(8,128)(2,1)S(1)}, u32[]{:S(2)}, u32[]{:S(2)}) %collective-permute-start.7) | collective-permute-done | bytes 1064992 | tf_op jit(solution)/shard_map/ppermute | solution.py:244
  79.5 0.0 copy-done.3
  79.5 2.9 %far.1 = (s16[784,256]{1,0:T(8,128)(2,1)S(1)}, s32[16,128]{1,0:T(8,128)S(1)}, bf16[16,1040,256]{2,1,0:T(8,128)(2,1)S(1)}) custom-call(s32[3]{0:T(128)S(1)} %copy-done.2, s32[12]{0:T(128)S(1)} %bitcast.18, s32[12]{0:T(128)S(1)} %bitcast.19, bf16[1,1040,256]{2,1,0:T(8,128)(2,1)S(1)} %bitcast.16, bf16[1,1040,256]{2,1,0:T(8,128)(2,1)S(1)} %collective-permute-done.rest_1_, ...), custom_call_target="tpu_custom_call" | custom-call | flops 402653184 | bytes 3145728 | tf_op jit(solution)/shard_map/far/pallas_call | solution.py:315
  82.4 4.7 %collective-permute-start.13 = (s16[784,256]{1,0:T(8,128)(2,1)S(1)}, s16[784,256]{1,0:T(8,128)(2,1)S(1)}, u32[]{:S(2)}, u32[]{:S(2)}) collective-permute-start(s16[784,256]{1,0:T(8,128)(2,1)S(1)} %get-tuple-element.14), channel_id=1, source_target_pairs={{0,2},{1,3},{2,0},{3,1},{4,6},{5,7},{6,4},{7,5},{8,10},{9,11},{10,... | collective-permute-start | bytes 1204232 | tf_op jit(solution)/shard_map/ppermute | solution.py:239
  87.1 2.8 %near.1 = (s16[784,256]{1,0:T(8,128)(2,1)S(1)}, s16[784,256]{1,0:T(8,128)(2,1)S(1)}) custom-call(s32[3]{0:T(128)S(1)} %copy-done.2, s32[16,128]{1,0:T(8,128)S(1)} %get-tuple-element.15.lists, bf16[16,1040,256]{2,1,0:T(8,128)(2,1)S(1)} %get-tuple-element.16.a_all, bf16[9,1040,256]{2,1,0:T(8,128)(2,1)S(1)} %join.1.rest_8_.b_all), custom_call_target="tpu_custom_call" | custom-call | flops 805306368 | bytes 6291456 | tf_op jit(solution)/shard_map/near/pallas_call | solution.py:334
  89.9 2.2 %collective-permute-start.14 = (s16[784,256]{1,0:T(8,128)(2,1)S(1)}, s16[784,256]{1,0:T(8,128)(2,1)S(1)}, u32[]{:S(2)}, u32[]{:S(2)}) collective-permute-start(s16[784,256]{1,0:T(8,128)(2,1)S(1)} %get-tuple-element.17), channel_id=1, source_target_pairs={{0,1},{1,2},{2,3},{3,0},{4,5},{5,6},{6,7},{7,4},{8,9},{9,10},{10,1... | collective-permute-start | bytes 1204232 | tf_op jit(solution)/shard_map/ppermute | solution.py:239
  92.2 0.0 copy-start.1
  92.2 4.4 %collective-permute-start.15 = (s16[784,256]{1,0:T(8,128)(2,1)S(1)}, s16[784,256]{1,0:T(8,128)(2,1)S(1)}, u32[]{:S(2)}, u32[]{:S(2)}) collective-permute-start(s16[784,256]{1,0:T(8,128)(2,1)S(1)} %get-tuple-element.18), channel_id=1, source_target_pairs={{0,3},{1,0},{2,1},{3,2},{4,7},{5,4},{6,5},{7,6},{8,11},{9,8},{10,9... | collective-permute-start | bytes 1204232 | tf_op jit(solution)/shard_map/ppermute | solution.py:239
  96.6 1.6 %own.1 = f32[3,256,256]{2,1,0:T(8,128)S(1)} custom-call(s32[3]{0:T(128)S(1)} %copy-done.2, s32[16,128]{1,0:T(8,128)S(1)} %get-tuple-element.15.lists, bf16[16,1040,256]{2,1,0:T(8,128)(2,1)S(1)} %get-tuple-element.16.a_all, bf16[9,1040,256]{2,1,0:T(8,128)(2,1)S(1)} %join.1.rest_8_.b_all), custom_call_target="tpu_custom_call" | custom-call | flops 402653184 | bytes 3145728 | tf_op jit(solution)/shard_map/own/pallas_call | solution.py:346
  98.2 0.0 collective-permute-done.13.far
  98.2 6.5 %collective-permute-done.14.up = s16[784,256]{1,0:T(8,128)(2,1)S(1)} collective-permute-done((s16[784,256]{1,0:T(8,128)(2,1)S(1)}, s16[784,256]{1,0:T(8,128)(2,1)S(1)}, u32[]{:S(2)}, u32[]{:S(2)}) %collective-permute-start.14) | collective-permute-done | bytes 401440 | tf_op jit(solution)/shard_map/ppermute | solution.py:239
  104.7 0.0 collective-permute-done.15.down
  104.7 0.0 copy-done.1
  104.7 1.2 %finish.1 = bf16[3,256,256]{2,1,0:T(8,128)(2,1)} custom-call(s16[784,256]{1,0:T(8,128)(2,1)S(1)} %collective-permute-done.13.far, s16[784,256]{1,0:T(8,128)(2,1)S(1)} %collective-permute-done.14.up, s16[784,256]{1,0:T(8,128)(2,1)S(1)} %collective-permute-done.15.down, f32[3,256,256]{2,1,0:T(8,128)S(1)} %own.1, bf16[3,256,256]{2,1,0:T(8,128)(2,1)S(1)} %bitcast.17), custom_call_target="tpu_custom_call" | custom-call | flops 2097152 | bytes 3145728 | tf_op jit(solution)/shard_map/finish/pallas_call | solution.py:355
  (8 shorter events, 0.2 us)
Async XLA Ops:
  3.6 20.5 %collective-permute-start = (bf16[1,1040,256]{2,1,0:T(8,128)(2,1)}, bf16[1,1040,256]{2,1,0:T(8,128)(2,1)S(1)}, u32[]{:S(2)}, u32[]{:S(2)}) collective-permute-start(bf16[1,1040,256]{2,1,0:T(8,128)(2,1)} %bitcast.13), channel_id=1, source_target_pairs={{0,64},{4,68},{8,72},{12,76},{16,80},{20,84},{24,88},{28,92},{32,4... | collective-permute-start | bytes 1597448 | tf_op jit(solution)/shard_map/ppermute | solution.py:234
  9.5 21.8 %collective-permute-start.8 = (bf16[1,1040,256]{2,1,0:T(8,128)(2,1)}, bf16[1,1040,256]{2,1,0:T(8,128)(2,1)S(1)}, u32[]{:S(2)}, u32[]{:S(2)}) collective-permute-start(bf16[1,1040,256]{2,1,0:T(8,128)(2,1)} %bitcast.20), channel_id=1, source_target_pairs={{0,4},{4,0},{8,12},{12,8},{16,20},{20,16},{24,28},{28,24},{32,60},... | collective-permute-start | bytes 1597448 | tf_op jit(solution)/shard_map/ppermute | solution.py:234
  20.2 13.0 %collective-permute-start.9 = (bf16[1,1040,256]{2,1,0:T(8,128)(2,1)}, bf16[1,1040,256]{2,1,0:T(8,128)(2,1)S(1)}, u32[]{:S(2)}, u32[]{:S(2)}) collective-permute-start(bf16[1,1040,256]{2,1,0:T(8,128)(2,1)} %bitcast.21), channel_id=1, source_target_pairs={{0,28},{4,8},{8,4},{12,16},{16,12},{20,24},{24,20},{28,0},{32,36},... | collective-permute-start | bytes 1597448 | tf_op jit(solution)/shard_map/ppermute | solution.py:234
  22.1 11.1 %collective-permute-start.1 = (bf16[1,1040,256]{2,1,0:T(8,128)(2,1)}, bf16[1,1040,256]{2,1,0:T(8,128)(2,1)S(1)}, u32[]{:S(2)}, u32[]{:S(2)}) collective-permute-start(bf16[1,1040,256]{2,1,0:T(8,128)(2,1)} %bitcast.14), channel_id=1, source_target_pairs={{0,448},{4,452},{8,456},{12,460},{16,464},{20,468},{24,472},{28,47... | collective-permute-start | bytes 1597448 | tf_op jit(solution)/shard_map/ppermute | solution.py:234
  24.1 14.3 %collective-permute-start.2 = (bf16[1,1040,256]{2,1,0:T(8,128)(2,1)S(1)}, bf16[1,1040,256]{2,1,0:T(8,128)(2,1)S(1)}, u32[]{:S(2)}, u32[]{:S(2)}) collective-permute-start(bf16[1,1040,256]{2,1,0:T(8,128)(2,1)S(1)} %collective-permute-done.rest_1_), channel_id=1, source_target_pairs={{0,448},{4,452},{8,456},{12,460},{16,464},{20,468},{24,472},{28,47... | collective-permute-start | bytes 1597448 | tf_op jit(solution)/shard_map/ppermute | solution.py:234
  31.3 10.0 %collective-permute-start.10 = (bf16[1,1040,256]{2,1,0:T(8,128)(2,1)S(1)}, bf16[1,1040,256]{2,1,0:T(8,128)(2,1)S(1)}, u32[]{:S(2)}, u32[]{:S(2)}) collective-permute-start(bf16[1,1040,256]{2,1,0:T(8,128)(2,1)S(1)} %collective-permute-done.8.refs_1_), channel_id=1, source_target_pairs={{0,28},{4,8},{8,4},{12,16},{16,12},{20,24},{24,20},{28,0},{32,36},... | collective-permute-start | bytes 1597448 | tf_op jit(solution)/shard_map/ppermute | solution.py:234
  33.3 12.7 %copy-start = (bf16[1040,256]{1,0:T(8,128)(2,1)S(1)}, bf16[1040,256]{1,0:T(8,128)(2,1)}, u32[]{:S(2)}) copy-start(bf16[1040,256]{1,0:T(8,128)(2,1)} %get-tuple-element.12) | copy-start | bytes 1597444
  38.4 16.9 %collective-permute-start.3 = (bf16[2,1040,256]{2,1,0:T(8,128)(2,1)S(1)}, bf16[2,1040,256]{2,1,0:T(8,128)(2,1)S(1)}, u32[]{:S(2)}, u32[]{:S(2)}) collective-permute-start(bf16[2,1040,256]{2,1,0:T(8,128)(2,1)S(1)} %constant_dynamic-update-slice_fusion.rest_2_), channel_id=1, source_target_pairs={{0,64},{4,68},{8,72},{12,76},{16,80},{20,84},{24,88},{28,92},{32,4... | collective-permute-start | bytes 3194888 | tf_op jit(solution)/shard_map/ppermute | solution.py:234
  41.3 35.9 %copy-start.5 = (bf16[1040,256]{1,0:T(8,128)(2,1)S(1)}, bf16[1040,256]{1,0:T(8,128)(2,1)}, u32[]{:S(2)}) copy-start(bf16[1040,256]{1,0:T(8,128)(2,1)} %get-tuple-element.13) | copy-start | bytes 1597444
  41.3 17.1 %collective-permute-start.11 = (bf16[2,1040,256]{2,1,0:T(8,128)(2,1)S(1)}, bf16[2,1040,256]{2,1,0:T(8,128)(2,1)S(1)}, u32[]{:S(2)}, u32[]{:S(2)}) collective-permute-start(bf16[2,1040,256]{2,1,0:T(8,128)(2,1)S(1)} %constant_dynamic-update-slice_fusion.2.refs_2_), channel_id=1, source_target_pairs={{0,4},{4,0},{8,12},{12,8},{16,20},{20,16},{24,28},{28,24},{32,60},... | collective-permute-start | bytes 3194888 | tf_op jit(solution)/shard_map/ppermute | solution.py:234
  46.3 33.2 %copy-start.2 = (s32[3]{0:T(128)S(1)}, s32[3]{0:T(128)}, u32[]{:S(2)}) copy-start(s32[3]{0:T(128)} %pad_add_fusion.place) | copy-start | bytes 40
  46.3 33.2 %copy-start.3 = (s32[1,1,12]{2,1,0:T(1,128)S(1)}, s32[1,1,12]{2,1,0:T(1,128)}, u32[]{:S(2)}) copy-start(s32[1,1,12]{2,1,0:T(1,128)} %param.11) | copy-start | bytes 148
  46.3 33.2 %copy-start.4 = (s32[1,1,12]{2,1,0:T(1,128)S(1)}, s32[1,1,12]{2,1,0:T(1,128)}, u32[]{:S(2)}) copy-start(s32[1,1,12]{2,1,0:T(1,128)} %param.12) | copy-start | bytes 148
  46.3 31.2 %collective-permute-start.5 = (bf16[4,1040,256]{2,1,0:T(8,128)(2,1)S(1)}, bf16[4,1040,256]{2,1,0:T(8,128)(2,1)S(1)}, u32[]{:S(2)}, u32[]{:S(2)}) collective-permute-start(bf16[4,1040,256]{2,1,0:T(8,128)(2,1)S(1)} %pad_maximum_fusion), channel_id=1, source_target_pairs={{0,32},{32,0},{64,96},{96,64},{128,160},{160,128},{192,224},{224,1... | collective-permute-start | bytes 6389768 | tf_op jit(solution)/shard_map/ppermute | solution.py:244
  55.3 16.0 %collective-permute-start.4 = (bf16[2,1040,256]{2,1,0:T(8,128)(2,1)S(1)}, bf16[2,1040,256]{2,1,0:T(8,128)(2,1)S(1)}, u32[]{:S(2)}, u32[]{:S(2)}) collective-permute-start(bf16[2,1040,256]{2,1,0:T(8,128)(2,1)S(1)} %collective-permute-done.3.rest_3_), channel_id=1, source_target_pairs={{0,448},{4,452},{8,456},{12,460},{16,464},{20,468},{24,472},{28,47... | collective-permute-start | bytes 3194888 | tf_op jit(solution)/shard_map/ppermute | solution.py:234
  58.4 18.8 %collective-permute-start.12 = (bf16[2,1040,256]{2,1,0:T(8,128)(2,1)S(1)}, bf16[2,1040,256]{2,1,0:T(8,128)(2,1)S(1)}, u32[]{:S(2)}, u32[]{:S(2)}) collective-permute-start(bf16[2,1040,256]{2,1,0:T(8,128)(2,1)S(1)} %collective-permute-done.11.refs_3_), channel_id=1, source_target_pairs={{0,28},{4,8},{8,4},{12,16},{16,12},{20,24},{24,20},{28,0},{32,36},... | collective-permute-start | bytes 3194888 | tf_op jit(solution)/shard_map/ppermute | solution.py:234
  60.3 17.2 %collective-permute-start.6 = (bf16[2,1040,256]{2,1,0:T(8,128)(2,1)S(1)}, bf16[2,1040,256]{2,1,0:T(8,128)(2,1)S(1)}, u32[]{:S(2)}, u32[]{:S(2)}) collective-permute-start(bf16[2,1040,256]{2,1,0:T(8,128)(2,1)S(1)} %collective-permute-done.3.rest_3_), channel_id=1, source_target_pairs={{0,32},{32,0},{64,96},{96,64},{128,160},{160,128},{192,224},{224,1... | collective-permute-start | bytes 3194888 | tf_op jit(solution)/shard_map/ppermute | solution.py:244
  71.3 8.2 %collective-permute-start.7 = (bf16[2,1040,256]{2,1,0:T(8,128)(2,1)S(1)}, bf16[2,1040,256]{2,1,0:T(8,128)(2,1)S(1)}, u32[]{:S(2)}, u32[]{:S(2)}) collective-permute-start(bf16[2,1040,256]{2,1,0:T(8,128)(2,1)S(1)} %collective-permute-done.4.rest_4_), channel_id=1, source_target_pairs={{0,32},{32,0},{64,96},{96,64},{128,160},{160,128},{192,224},{224,1... | collective-permute-start | bytes 3194888 | tf_op jit(solution)/shard_map/ppermute | solution.py:244
  82.4 15.8 %collective-permute-start.13 = (s16[784,256]{1,0:T(8,128)(2,1)S(1)}, s16[784,256]{1,0:T(8,128)(2,1)S(1)}, u32[]{:S(2)}, u32[]{:S(2)}) collective-permute-start(s16[784,256]{1,0:T(8,128)(2,1)S(1)} %get-tuple-element.14), channel_id=1, source_target_pairs={{0,2},{1,3},{2,0},{3,1},{4,6},{5,7},{6,4},{7,5},{8,10},{9,11},{10,... | collective-permute-start | bytes 1204232 | tf_op jit(solution)/shard_map/ppermute | solution.py:239
  89.9 14.8 %collective-permute-start.14 = (s16[784,256]{1,0:T(8,128)(2,1)S(1)}, s16[784,256]{1,0:T(8,128)(2,1)S(1)}, u32[]{:S(2)}, u32[]{:S(2)}) collective-permute-start(s16[784,256]{1,0:T(8,128)(2,1)S(1)} %get-tuple-element.17), channel_id=1, source_target_pairs={{0,1},{1,2},{2,3},{3,0},{4,5},{5,6},{6,7},{7,4},{8,9},{9,10},{10,1... | collective-permute-start | bytes 1204232 | tf_op jit(solution)/shard_map/ppermute | solution.py:239
  92.2 12.5 %copy-start.1 = (bf16[1,1,3,256,256]{4,3,2,1,0:T(8,128)(2,1)S(1)}, bf16[1,1,3,256,256]{4,3,2,1,0:T(8,128)(2,1)}, u32[]{:S(2)}) copy-start(bf16[1,1,3,256,256]{4,3,2,1,0:T(8,128)(2,1)} %param.13) | copy-start | bytes 1179652
  92.2 12.5 %collective-permute-start.15 = (s16[784,256]{1,0:T(8,128)(2,1)S(1)}, s16[784,256]{1,0:T(8,128)(2,1)S(1)}, u32[]{:S(2)}, u32[]{:S(2)}) collective-permute-start(s16[784,256]{1,0:T(8,128)(2,1)S(1)} %get-tuple-element.18), channel_id=1, source_target_pairs={{0,3},{1,0},{2,1},{3,2},{4,7},{5,4},{6,5},{7,6},{8,11},{9,8},{10,9... | collective-permute-start | bytes 1204232 | tf_op jit(solution)/shard_map/ppermute | solution.py:239

commit v5 on v4

--- a/solution.py
+++ b/solution.py
@@ -205,19 +205,25 @@
         keep_powers([encode(total, index, coded, index, blk, each) for index in range(each)], coded, each * blk)
 
 
-def own_kernel(sizes, shares, each, place, lists, a_all, b_all, total):
+def decoded(coded, slot, blk, each):
+    power = coded[pl.ds(each * blk, PAD), :].astype(jnp.int32).astype(jnp.float32)[slot : slot + 1]
+    values = coded[pl.ds(slot * blk, blk), :].astype(jnp.int32).astype(jnp.float32)
+    return values * jnp.exp2(power * (1.0 / FINER))
+
+
+def own_kernel(sizes, shares, each, place, lists, a_all, b_all, far, square_kept, total):
+    blk = sizes[2]
     multiply(sizes, lists, a_all, b_all, target(place, 0, shares, each), total)
-
-
-def finish_kernel(far, up, down, own, square_kept, out):
-    each, blk = square_kept.shape[0], square_kept.shape[1]
     for slot in range(each):
-        cube = own[slot]
-        for coded in (far, up, down):
-            power = coded[pl.ds(each * blk, PAD), :].astype(jnp.int32).astype(jnp.float32)[slot : slot + 1]
-            values = coded[pl.ds(slot * blk, blk), :].astype(jnp.int32).astype(jnp.float32)
-            cube = cube + values * jnp.exp2(power * (1.0 / FINER))
-        out[slot] = (3.0 * square_kept[slot].astype(jnp.float32) - 2.0 * cube).astype(out.dtype)
+        cube = total[slot] + decoded(far, slot, blk, each)
+        total[slot] = 3.0 * square_kept[slot].astype(jnp.float32) - 2.0 * cube
+
+
+def finish_kernel(up, down, rest, out):
+    each, blk = rest.shape[0], rest.shape[1]
+    for slot in range(each):
+        cube = decoded(up, slot, blk, each) + decoded(down, slot, blk, each)
+        out[slot] = (rest[slot] - 2.0 * cube).astype(out.dtype)
 
 
 def exchanged(value, axes, sizes, axis, first):
@@ -346,19 +352,19 @@
     own = pl.pallas_call(
         functools.partial(own_kernel, sizes, n_depth, each),
         out_shape=jax.ShapeDtypeStruct(summed, jnp.float32),
-        in_specs=[smem] * 2 + [whole] * 2,
+        in_specs=[smem] * 2 + [whole] * 4,
         out_specs=whole,
         compiler_params=params,
         cost_estimate=cost(each),
         name="own",
-    )(place, lists, a_all, b_all)
+    )(place, lists, a_all, b_all, far, square_kept[0, 0])
     result = pl.pallas_call(
         finish_kernel,
         out_shape=jax.ShapeDtypeStruct(summed, jnp.bfloat16),
         compiler_params=params,
         cost_estimate=pl.CostEstimate(flops=2**21, bytes_accessed=3 * 2**20, transcendentals=0),
         name="finish",
-    )(far, up, down, own, square_kept[0, 0])
+    )(up, down, own)
     return result[None, None]
 
 

time: 108 us -> 108 us (level)
  transfers between devices with their start and end apart: 16 -> 16, of which waited for: 8 -> 8; matrix products, arithmetic and copies ran while one was open for 0% -> 0% of each run, Pallas kernels for 4% -> 5%
where the time goes in v5:
time: 108 us; the launch traced here: 107 us
  starting transfers between devices  62 us (57%)
  waiting for transfers between devices  31.4 us (29%)
  Pallas kernels  11.8 us (11%)
    ppermute x10, starting transfers between devices, exchanged(): return lax.ppermute(value, axes, pairs)  36.8 us
    ppermute x10, waiting for transfers between devices, exchanged(): return lax.ppermute(value, axes, pairs)  22.5 us
    ppermute x3, starting transfers between devices, siblings(): lax.ppermute(value, 'row', [(source, source ^ 1) for source in range(coun...  13.7 us
    ppermute x3, starting transfers between devices, shifted(): lax.ppermute(value, axis, [(source, (source + steps) % count) for source...  11.5 us
    ppermute x3, waiting for transfers between devices, shifted(): lax.ppermute(value, axis, [(source, (source + steps) % count) for source...  6.91 us
    pallas_call x1, Pallas kernels, body(): pl.pallas_call(functools.partial(near_kernel, sizes, n_depth, each), out_...  3.14 us
    pallas_call x1, Pallas kernels, body(): pl.pallas_call(functools.partial(prepare_kernel, (held_a, held_b, blk, cu...  2.94 us
    pallas_call x1, Pallas kernels, body(): pl.pallas_call(functools.partial(far_kernel, sizes, n_depth, len(parts_a)...  2.92 us
  transfers between devices with their start and end apart: 16, of which 8 were waited for; matrix products, arithmetic and copies ran while one was open for 0% of the time, Pallas kernels for 5%

profile of v5, /device:TPU:1, one launch (start us, length us, event | category | flops | bytes accessed | tf_op | source)
XLA Modules:
  0.0 106.6 jit_solution(3771232051830351211)
XLA Ops:
  0.0 0.6 pad_add_fusion.place
  0.6 2.9 %prepare.1 = (bf16[1040,256]{1,0:T(8,128)(2,1)}, bf16[1040,256]{1,0:T(8,128)(2,1)}) custom-call(s32[3]{0:T(128)} %pad_add_fusion.place, s32[4]{0:T(128)} %bitcast.26, s32[2,2]{1,0:T(2,128)} %bitcast.25, bf16[1024,256]{1,0:T(8,128)(2,1)} %bitcast.23, bf16[1024,256]{1,0:T(8,128)(2,1)} %bitcast.24), custom_call_target="tpu_custom_call" | custom-call | tf_op jit(solution)/shard_map/prepare/pallas_call | solution.py:264
  3.6 5.9 %collective-permute-start = (bf16[1,1040,256]{2,1,0:T(8,128)(2,1)}, bf16[1,1040,256]{2,1,0:T(8,128)(2,1)S(1)}, u32[]{:S(2)}, u32[]{:S(2)}) collective-permute-start(bf16[1,1040,256]{2,1,0:T(8,128)(2,1)} %bitcast.13), channel_id=1, source_target_pairs={{0,64},{4,68},{8,72},{12,76},{16,80},{20,84},{24,88},{28,92},{32,4... | collective-permute-start | bytes 1597448 | tf_op jit(solution)/shard_map/ppermute | solution.py:240
  9.5 10.7 %collective-permute-start.8 = (bf16[1,1040,256]{2,1,0:T(8,128)(2,1)}, bf16[1,1040,256]{2,1,0:T(8,128)(2,1)S(1)}, u32[]{:S(2)}, u32[]{:S(2)}) collective-permute-start(bf16[1,1040,256]{2,1,0:T(8,128)(2,1)} %bitcast.20), channel_id=1, source_target_pairs={{0,4},{4,0},{8,12},{12,8},{16,20},{20,16},{24,28},{28,24},{32,60},... | collective-permute-start | bytes 1597448 | tf_op jit(solution)/shard_map/ppermute | solution.py:240
  20.2 1.9 %collective-permute-start.9 = (bf16[1,1040,256]{2,1,0:T(8,128)(2,1)}, bf16[1,1040,256]{2,1,0:T(8,128)(2,1)S(1)}, u32[]{:S(2)}, u32[]{:S(2)}) collective-permute-start(bf16[1,1040,256]{2,1,0:T(8,128)(2,1)} %bitcast.21), channel_id=1, source_target_pairs={{0,28},{4,8},{8,4},{12,16},{16,12},{20,24},{24,20},{28,0},{32,36},... | collective-permute-start | bytes 1597448 | tf_op jit(solution)/shard_map/ppermute | solution.py:240
  22.1 1.9 %collective-permute-start.1 = (bf16[1,1040,256]{2,1,0:T(8,128)(2,1)}, bf16[1,1040,256]{2,1,0:T(8,128)(2,1)S(1)}, u32[]{:S(2)}, u32[]{:S(2)}) collective-permute-start(bf16[1,1040,256]{2,1,0:T(8,128)(2,1)} %bitcast.14), channel_id=1, source_target_pairs={{0,448},{4,452},{8,456},{12,460},{16,464},{20,468},{24,472},{28,47... | collective-permute-start | bytes 1597448 | tf_op jit(solution)/shard_map/ppermute | solution.py:240
  24.1 0.0 collective-permute-done.rest_1_
  24.1 3.4 %collective-permute-start.2 = (bf16[1,1040,256]{2,1,0:T(8,128)(2,1)S(1)}, bf16[1,1040,256]{2,1,0:T(8,128)(2,1)S(1)}, u32[]{:S(2)}, u32[]{:S(2)}) collective-permute-start(bf16[1,1040,256]{2,1,0:T(8,128)(2,1)S(1)} %collective-permute-done.rest_1_), channel_id=1, source_target_pairs={{0,448},{4,452},{8,456},{12,460},{16,464},{20,468},{24,472},{28,47... | collective-permute-start | bytes 1597448 | tf_op jit(solution)/shard_map/ppermute | solution.py:240
  27.4 3.8 %collective-permute-done.8.refs_1_ = bf16[1,1040,256]{2,1,0:T(8,128)(2,1)S(1)} collective-permute-done((bf16[1,1040,256]{2,1,0:T(8,128)(2,1)}, bf16[1,1040,256]{2,1,0:T(8,128)(2,1)S(1)}, u32[]{:S(2)}, u32[]{:S(2)}) %collective-permute-start.8) | collective-permute-done | bytes 532512 | tf_op jit(solution)/shard_map/ppermute | solution.py:240
  31.3 1.9 %collective-permute-start.10 = (bf16[1,1040,256]{2,1,0:T(8,128)(2,1)S(1)}, bf16[1,1040,256]{2,1,0:T(8,128)(2,1)S(1)}, u32[]{:S(2)}, u32[]{:S(2)}) collective-permute-start(bf16[1,1040,256]{2,1,0:T(8,128)(2,1)S(1)} %collective-permute-done.8.refs_1_), channel_id=1, source_target_pairs={{0,28},{4,8},{8,4},{12,16},{16,12},{20,24},{24,20},{28,0},{32,36},... | collective-permute-start | bytes 1597448 | tf_op jit(solution)/shard_map/ppermute | solution.py:240
  33.2 0.0 collective-permute-done.9
  33.3 0.0 collective-permute-done.1
  33.3 0.0 copy-start
  33.3 5.0 %collective-permute-done.2 = bf16[1,1040,256]{2,1,0:T(8,128)(2,1)S(1)} collective-permute-done((bf16[1,1040,256]{2,1,0:T(8,128)(2,1)S(1)}, bf16[1,1040,256]{2,1,0:T(8,128)(2,1)S(1)}, u32[]{:S(2)}, u32[]{:S(2)}) %collective-permute-start.2) | collective-permute-done | bytes 532512 | tf_op jit(solution)/shard_map/ppermute | solution.py:240
  38.4 2.6 %collective-permute-start.3 = (bf16[2,1040,256]{2,1,0:T(8,128)(2,1)S(1)}, bf16[2,1040,256]{2,1,0:T(8,128)(2,1)S(1)}, u32[]{:S(2)}, u32[]{:S(2)}) collective-permute-start(bf16[2,1040,256]{2,1,0:T(8,128)(2,1)S(1)} %constant_dynamic-update-slice_fusion.rest_2_), channel_id=1, source_target_pairs={{0,64},{4,68},{8,72},{12,76},{16,80},{20,84},{24,88},{28,92},{32,4... | collective-permute-start | bytes 3194888 | tf_op jit(solution)/shard_map/ppermute | solution.py:240
  41.0 0.3 collective-permute-done.10
  41.3 0.0 copy-start.5
  41.3 4.7 %collective-permute-start.11 = (bf16[2,1040,256]{2,1,0:T(8,128)(2,1)S(1)}, bf16[2,1040,256]{2,1,0:T(8,128)(2,1)S(1)}, u32[]{:S(2)}, u32[]{:S(2)}) collective-permute-start(bf16[2,1040,256]{2,1,0:T(8,128)(2,1)S(1)} %constant_dynamic-update-slice_fusion.2.refs_2_), channel_id=1, source_target_pairs={{0,4},{4,0},{8,12},{12,8},{16,20},{20,16},{24,28},{28,24},{32,60},... | collective-permute-start | bytes 3194888 | tf_op jit(solution)/shard_map/ppermute | solution.py:240
  46.0 0.0 copy-done
  46.0 0.3 pad_maximum_fusion
  46.3 0.0 copy-start.2
  46.3 0.0 copy-start.3
  46.3 0.0 copy-start.4
  46.3 1.9 %collective-permute-start.5 = (bf16[4,1040,256]{2,1,0:T(8,128)(2,1)S(1)}, bf16[4,1040,256]{2,1,0:T(8,128)(2,1)S(1)}, u32[]{:S(2)}, u32[]{:S(2)}) collective-permute-start(bf16[4,1040,256]{2,1,0:T(8,128)(2,1)S(1)} %pad_maximum_fusion), channel_id=1, source_target_pairs={{0,32},{32,0},{64,96},{96,64},{128,160},{160,128},{192,224},{224,1... | collective-permute-start | bytes 6389768 | tf_op jit(solution)/shard_map/ppermute | solution.py:250
  48.3 7.1 %collective-permute-done.3.rest_3_ = bf16[2,1040,256]{2,1,0:T(8,128)(2,1)S(1)} collective-permute-done((bf16[2,1040,256]{2,1,0:T(8,128)(2,1)S(1)}, bf16[2,1040,256]{2,1,0:T(8,128)(2,1)S(1)}, u32[]{:S(2)}, u32[]{:S(2)}) %collective-permute-start.3) | collective-permute-done | bytes 1064992 | tf_op jit(solution)/shard_map/ppermute | solution.py:240
  55.3 1.9 %collective-permute-start.4 = (bf16[2,1040,256]{2,1,0:T(8,128)(2,1)S(1)}, bf16[2,1040,256]{2,1,0:T(8,128)(2,1)S(1)}, u32[]{:S(2)}, u32[]{:S(2)}) collective-permute-start(bf16[2,1040,256]{2,1,0:T(8,128)(2,1)S(1)} %collective-permute-done.3.rest_3_), channel_id=1, source_target_pairs={{0,448},{4,452},{8,456},{12,460},{16,464},{20,468},{24,472},{28,47... | collective-permute-start | bytes 3194888 | tf_op jit(solution)/shard_map/ppermute | solution.py:240
  57.2 1.2 %collective-permute-done.11.refs_3_ = bf16[2,1040,256]{2,1,0:T(8,128)(2,1)S(1)} collective-permute-done((bf16[2,1040,256]{2,1,0:T(8,128)(2,1)S(1)}, bf16[2,1040,256]{2,1,0:T(8,128)(2,1)S(1)}, u32[]{:S(2)}, u32[]{:S(2)}) %collective-permute-start.11) | collective-permute-done | bytes 1064992 | tf_op jit(solution)/shard_map/ppermute | solution.py:240
  58.4 1.9 %collective-permute-start.12 = (bf16[2,1040,256]{2,1,0:T(8,128)(2,1)S(1)}, bf16[2,1040,256]{2,1,0:T(8,128)(2,1)S(1)}, u32[]{:S(2)}, u32[]{:S(2)}) collective-permute-start(bf16[2,1040,256]{2,1,0:T(8,128)(2,1)S(1)} %collective-permute-done.11.refs_3_), channel_id=1, source_target_pairs={{0,28},{4,8},{8,4},{12,16},{16,12},{20,24},{24,20},{28,0},{32,36},... | collective-permute-start | bytes 3194888 | tf_op jit(solution)/shard_map/ppermute | solution.py:240
  60.3 5.9 %collective-permute-start.6 = (bf16[2,1040,256]{2,1,0:T(8,128)(2,1)S(1)}, bf16[2,1040,256]{2,1,0:T(8,128)(2,1)S(1)}, u32[]{:S(2)}, u32[]{:S(2)}) collective-permute-start(bf16[2,1040,256]{2,1,0:T(8,128)(2,1)S(1)} %collective-permute-done.3.rest_3_), channel_id=1, source_target_pairs={{0,32},{32,0},{64,96},{96,64},{128,160},{160,128},{192,224},{224,1... | collective-permute-start | bytes 3194888 | tf_op jit(solution)/shard_map/ppermute | solution.py:250
  66.2 5.1 %collective-permute-done.4.rest_4_ = bf16[2,1040,256]{2,1,0:T(8,128)(2,1)S(1)} collective-permute-done((bf16[2,1040,256]{2,1,0:T(8,128)(2,1)S(1)}, bf16[2,1040,256]{2,1,0:T(8,128)(2,1)S(1)}, u32[]{:S(2)}, u32[]{:S(2)}) %collective-permute-start.4) | collective-permute-done | bytes 1064992 | tf_op jit(solution)/shard_map/ppermute | solution.py:240
  71.3 5.9 %collective-permute-start.7 = (bf16[2,1040,256]{2,1,0:T(8,128)(2,1)S(1)}, bf16[2,1040,256]{2,1,0:T(8,128)(2,1)S(1)}, u32[]{:S(2)}, u32[]{:S(2)}) collective-permute-start(bf16[2,1040,256]{2,1,0:T(8,128)(2,1)S(1)} %collective-permute-done.4.rest_4_), channel_id=1, source_target_pairs={{0,32},{32,0},{64,96},{96,64},{128,160},{160,128},{192,224},{224,1... | collective-permute-start | bytes 3194888 | tf_op jit(solution)/shard_map/ppermute | solution.py:250
  77.2 0.0 collective-permute-done.12.refs_4_
  77.2 0.3 join.1.rest_8_.b_all
  77.5 0.0 collective-permute-done.6.rest_6_
  77.5 0.0 collective-permute-done.5.rest_5_
  77.5 2.0 %collective-permute-done.7.rest_7_ = bf16[2,1040,256]{2,1,0:T(8,128)(2,1)S(1)} collective-permute-done((bf16[2,1040,256]{2,1,0:T(8,128)(2,1)S(1)}, bf16[2,1040,256]{2,1,0:T(8,128)(2,1)S(1)}, u32[]{:S(2)}, u32[]{:S(2)}) %collective-permute-start.7) | collective-permute-done | bytes 1064992 | tf_op jit(solution)/shard_map/ppermute | solution.py:250
  79.5 0.0 copy-done.3
  79.5 2.9 %far.1 = (s16[784,256]{1,0:T(8,128)(2,1)S(1)}, s32[16,128]{1,0:T(8,128)S(1)}, bf16[16,1040,256]{2,1,0:T(8,128)(2,1)S(1)}) custom-call(s32[3]{0:T(128)S(1)} %copy-done.2, s32[12]{0:T(128)S(1)} %bitcast.18, s32[12]{0:T(128)S(1)} %bitcast.19, bf16[1,1040,256]{2,1,0:T(8,128)(2,1)S(1)} %bitcast.16, bf16[1,1040,256]{2,1,0:T(8,128)(2,1)S(1)} %collective-permute-done.rest_1_, ...), custom_call_target="tpu_custom_call" | custom-call | flops 402653184 | bytes 3145728 | tf_op jit(solution)/shard_map/far/pallas_call | solution.py:321
  82.4 5.0 %collective-permute-start.15 = (s16[784,256]{1,0:T(8,128)(2,1)S(1)}, s16[784,256]{1,0:T(8,128)(2,1)S(1)}, u32[]{:S(2)}, u32[]{:S(2)}) collective-permute-start(s16[784,256]{1,0:T(8,128)(2,1)S(1)} %get-tuple-element.18), channel_id=1, source_target_pairs={{0,2},{1,3},{2,0},{3,1},{4,6},{5,7},{6,4},{7,5},{8,10},{9,11},{10,... | collective-permute-start | bytes 1204232 | tf_op jit(solution)/shard_map/ppermute | solution.py:245
  87.4 0.0 copy-start.1
  87.4 3.1 %near.1 = (s16[784,256]{1,0:T(8,128)(2,1)S(1)}, s16[784,256]{1,0:T(8,128)(2,1)S(1)}) custom-call(s32[3]{0:T(128)S(1)} %copy-done.2, s32[16,128]{1,0:T(8,128)S(1)} %get-tuple-element.14.lists, bf16[16,1040,256]{2,1,0:T(8,128)(2,1)S(1)} %get-tuple-element.15.a_all, bf16[9,1040,256]{2,1,0:T(8,128)(2,1)S(1)} %join.1.rest_8_.b_all), custom_call_target="tpu_custom_call" | custom-call | flops 805306368 | bytes 6291456 | tf_op jit(solution)/shard_map/near/pallas_call | solution.py:340
  90.6 1.9 %collective-permute-start.13 = (s16[784,256]{1,0:T(8,128)(2,1)S(1)}, s16[784,256]{1,0:T(8,128)(2,1)S(1)}, u32[]{:S(2)}, u32[]{:S(2)}) collective-permute-start(s16[784,256]{1,0:T(8,128)(2,1)S(1)} %get-tuple-element.16), channel_id=1, source_target_pairs={{0,1},{1,2},{2,3},{3,0},{4,5},{5,6},{6,7},{7,4},{8,9},{9,10},{10,1... | collective-permute-start | bytes 1204232 | tf_op jit(solution)/shard_map/ppermute | solution.py:245
  92.5 4.6 %collective-permute-start.14 = (s16[784,256]{1,0:T(8,128)(2,1)S(1)}, s16[784,256]{1,0:T(8,128)(2,1)S(1)}, u32[]{:S(2)}, u32[]{:S(2)}) collective-permute-start(s16[784,256]{1,0:T(8,128)(2,1)S(1)} %get-tuple-element.17), channel_id=1, source_target_pairs={{0,3},{1,0},{2,1},{3,2},{4,7},{5,4},{6,5},{7,6},{8,11},{9,8},{10,9... | collective-permute-start | bytes 1204232 | tf_op jit(solution)/shard_map/ppermute | solution.py:245
  97.1 0.0 collective-permute-done.15.far
  97.1 1.5 %own.1.rest = f32[3,256,256]{2,1,0:T(8,128)S(1)} custom-call(s32[3]{0:T(128)S(1)} %copy-done.2, s32[16,128]{1,0:T(8,128)S(1)} %get-tuple-element.14.lists, bf16[16,1040,256]{2,1,0:T(8,128)(2,1)S(1)} %get-tuple-element.15.a_all, bf16[9,1040,256]{2,1,0:T(8,128)(2,1)S(1)} %join.1.rest_8_.b_all, s16[784,256]{1,0:T(8,128)(2,1)S(1)} %collective-permute-done.15.far, ...), custom_call_target="tpu_custom_call" | custom-call | flops 402653184 | bytes 3145728 | tf_op jit(solution)/shard_map/own/pallas_call | solution.py:352
  98.6 6.9 %collective-permute-done.13.up = s16[784,256]{1,0:T(8,128)(2,1)S(1)} collective-permute-done((s16[784,256]{1,0:T(8,128)(2,1)S(1)}, s16[784,256]{1,0:T(8,128)(2,1)S(1)}, u32[]{:S(2)}, u32[]{:S(2)}) %collective-permute-start.13) | collective-permute-done | bytes 401440 | tf_op jit(solution)/shard_map/ppermute | solution.py:245
  105.5 0.0 collective-permute-done.14.down
  105.5 1.0 finish.1
  (8 shorter events, 0.2 us)
Async XLA Ops:
  3.6 20.5 %collective-permute-start = (bf16[1,1040,256]{2,1,0:T(8,128)(2,1)}, bf16[1,1040,256]{2,1,0:T(8,128)(2,1)S(1)}, u32[]{:S(2)}, u32[]{:S(2)}) collective-permute-start(bf16[1,1040,256]{2,1,0:T(8,128)(2,1)} %bitcast.13), channel_id=1, source_target_pairs={{0,64},{4,68},{8,72},{12,76},{16,80},{20,84},{24,88},{28,92},{32,4... | collective-permute-start | bytes 1597448 | tf_op jit(solution)/shard_map/ppermute | solution.py:240
  9.5 21.8 %collective-permute-start.8 = (bf16[1,1040,256]{2,1,0:T(8,128)(2,1)}, bf16[1,1040,256]{2,1,0:T(8,128)(2,1)S(1)}, u32[]{:S(2)}, u32[]{:S(2)}) collective-permute-start(bf16[1,1040,256]{2,1,0:T(8,128)(2,1)} %bitcast.20), channel_id=1, source_target_pairs={{0,4},{4,0},{8,12},{12,8},{16,20},{20,16},{24,28},{28,24},{32,60},... | collective-permute-start | bytes 1597448 | tf_op jit(solution)/shard_map/ppermute | solution.py:240
  20.2 13.0 %collective-permute-start.9 = (bf16[1,1040,256]{2,1,0:T(8,128)(2,1)}, bf16[1,1040,256]{2,1,0:T(8,128)(2,1)S(1)}, u32[]{:S(2)}, u32[]{:S(2)}) collective-permute-start(bf16[1,1040,256]{2,1,0:T(8,128)(2,1)} %bitcast.21), channel_id=1, source_target_pairs={{0,28},{4,8},{8,4},{12,16},{16,12},{20,24},{24,20},{28,0},{32,36},... | collective-permute-start | bytes 1597448 | tf_op jit(solution)/shard_map/ppermute | solution.py:240
  22.1 11.1 %collective-permute-start.1 = (bf16[1,1040,256]{2,1,0:T(8,128)(2,1)}, bf16[1,1040,256]{2,1,0:T(8,128)(2,1)S(1)}, u32[]{:S(2)}, u32[]{:S(2)}) collective-permute-start(bf16[1,1040,256]{2,1,0:T(8,128)(2,1)} %bitcast.14), channel_id=1, source_target_pairs={{0,448},{4,452},{8,456},{12,460},{16,464},{20,468},{24,472},{28,47... | collective-permute-start | bytes 1597448 | tf_op jit(solution)/shard_map/ppermute | solution.py:240
  24.1 14.3 %collective-permute-start.2 = (bf16[1,1040,256]{2,1,0:T(8,128)(2,1)S(1)}, bf16[1,1040,256]{2,1,0:T(8,128)(2,1)S(1)}, u32[]{:S(2)}, u32[]{:S(2)}) collective-permute-start(bf16[1,1040,256]{2,1,0:T(8,128)(2,1)S(1)} %collective-permute-done.rest_1_), channel_id=1, source_target_pairs={{0,448},{4,452},{8,456},{12,460},{16,464},{20,468},{24,472},{28,47... | collective-permute-start | bytes 1597448 | tf_op jit(solution)/shard_map/ppermute | solution.py:240
  31.3 10.0 %collective-permute-start.10 = (bf16[1,1040,256]{2,1,0:T(8,128)(2,1)S(1)}, bf16[1,1040,256]{2,1,0:T(8,128)(2,1)S(1)}, u32[]{:S(2)}, u32[]{:S(2)}) collective-permute-start(bf16[1,1040,256]{2,1,0:T(8,128)(2,1)S(1)} %collective-permute-done.8.refs_1_), channel_id=1, source_target_pairs={{0,28},{4,8},{8,4},{12,16},{16,12},{20,24},{24,20},{28,0},{32,36},... | collective-permute-start | bytes 1597448 | tf_op jit(solution)/shard_map/ppermute | solution.py:240
  33.3 12.7 %copy-start = (bf16[1040,256]{1,0:T(8,128)(2,1)S(1)}, bf16[1040,256]{1,0:T(8,128)(2,1)}, u32[]{:S(2)}) copy-start(bf16[1040,256]{1,0:T(8,128)(2,1)} %get-tuple-element.12) | copy-start | bytes 1597444
  38.4 16.9 %collective-permute-start.3 = (bf16[2,1040,256]{2,1,0:T(8,128)(2,1)S(1)}, bf16[2,1040,256]{2,1,0:T(8,128)(2,1)S(1)}, u32[]{:S(2)}, u32[]{:S(2)}) collective-permute-start(bf16[2,1040,256]{2,1,0:T(8,128)(2,1)S(1)} %constant_dynamic-update-slice_fusion.rest_2_), channel_id=1, source_target_pairs={{0,64},{4,68},{8,72},{12,76},{16,80},{20,84},{24,88},{28,92},{32,4... | collective-permute-start | bytes 3194888 | tf_op jit(solution)/shard_map/ppermute | solution.py:240
  41.3 35.9 %copy-start.5 = (bf16[1040,256]{1,0:T(8,128)(2,1)S(1)}, bf16[1040,256]{1,0:T(8,128)(2,1)}, u32[]{:S(2)}) copy-start(bf16[1040,256]{1,0:T(8,128)(2,1)} %get-tuple-element.13) | copy-start | bytes 1597444
  41.3 17.1 %collective-permute-start.11 = (bf16[2,1040,256]{2,1,0:T(8,128)(2,1)S(1)}, bf16[2,1040,256]{2,1,0:T(8,128)(2,1)S(1)}, u32[]{:S(2)}, u32[]{:S(2)}) collective-permute-start(bf16[2,1040,256]{2,1,0:T(8,128)(2,1)S(1)} %constant_dynamic-update-slice_fusion.2.refs_2_), channel_id=1, source_target_pairs={{0,4},{4,0},{8,12},{12,8},{16,20},{20,16},{24,28},{28,24},{32,60},... | collective-permute-start | bytes 3194888 | tf_op jit(solution)/shard_map/ppermute | solution.py:240
  46.3 33.2 %copy-start.2 = (s32[3]{0:T(128)S(1)}, s32[3]{0:T(128)}, u32[]{:S(2)}) copy-start(s32[3]{0:T(128)} %pad_add_fusion.place) | copy-start | bytes 40
  46.3 33.2 %copy-start.3 = (s32[1,1,12]{2,1,0:T(1,128)S(1)}, s32[1,1,12]{2,1,0:T(1,128)}, u32[]{:S(2)}) copy-start(s32[1,1,12]{2,1,0:T(1,128)} %param.11) | copy-start | bytes 148
  46.3 33.2 %copy-start.4 = (s32[1,1,12]{2,1,0:T(1,128)S(1)}, s32[1,1,12]{2,1,0:T(1,128)}, u32[]{:S(2)}) copy-start(s32[1,1,12]{2,1,0:T(1,128)} %param.12) | copy-start | bytes 148
  46.3 31.2 %collective-permute-start.5 = (bf16[4,1040,256]{2,1,0:T(8,128)(2,1)S(1)}, bf16[4,1040,256]{2,1,0:T(8,128)(2,1)S(1)}, u32[]{:S(2)}, u32[]{:S(2)}) collective-permute-start(bf16[4,1040,256]{2,1,0:T(8,128)(2,1)S(1)} %pad_maximum_fusion), channel_id=1, source_target_pairs={{0,32},{32,0},{64,96},{96,64},{128,160},{160,128},{192,224},{224,1... | collective-permute-start | bytes 6389768 | tf_op jit(solution)/shard_map/ppermute | solution.py:250
  55.3 16.0 %collective-permute-start.4 = (bf16[2,1040,256]{2,1,0:T(8,128)(2,1)S(1)}, bf16[2,1040,256]{2,1,0:T(8,128)(2,1)S(1)}, u32[]{:S(2)}, u32[]{:S(2)}) collective-permute-start(bf16[2,1040,256]{2,1,0:T(8,128)(2,1)S(1)} %collective-permute-done.3.rest_3_), channel_id=1, source_target_pairs={{0,448},{4,452},{8,456},{12,460},{16,464},{20,468},{24,472},{28,47... | collective-permute-start | bytes 3194888 | tf_op jit(solution)/shard_map/ppermute | solution.py:240
  58.4 18.8 %collective-permute-start.12 = (bf16[2,1040,256]{2,1,0:T(8,128)(2,1)S(1)}, bf16[2,1040,256]{2,1,0:T(8,128)(2,1)S(1)}, u32[]{:S(2)}, u32[]{:S(2)}) collective-permute-start(bf16[2,1040,256]{2,1,0:T(8,128)(2,1)S(1)} %collective-permute-done.11.refs_3_), channel_id=1, source_target_pairs={{0,28},{4,8},{8,4},{12,16},{16,12},{20,24},{24,20},{28,0},{32,36},... | collective-permute-start | bytes 3194888 | tf_op jit(solution)/shard_map/ppermute | solution.py:240
  60.3 17.2 %collective-permute-start.6 = (bf16[2,1040,256]{2,1,0:T(8,128)(2,1)S(1)}, bf16[2,1040,256]{2,1,0:T(8,128)(2,1)S(1)}, u32[]{:S(2)}, u32[]{:S(2)}) collective-permute-start(bf16[2,1040,256]{2,1,0:T(8,128)(2,1)S(1)} %collective-permute-done.3.rest_3_), channel_id=1, source_target_pairs={{0,32},{32,0},{64,96},{96,64},{128,160},{160,128},{192,224},{224,1... | collective-permute-start | bytes 3194888 | tf_op jit(solution)/shard_map/ppermute | solution.py:250
  71.3 8.2 %collective-permute-start.7 = (bf16[2,1040,256]{2,1,0:T(8,128)(2,1)S(1)}, bf16[2,1040,256]{2,1,0:T(8,128)(2,1)S(1)}, u32[]{:S(2)}, u32[]{:S(2)}) collective-permute-start(bf16[2,1040,256]{2,1,0:T(8,128)(2,1)S(1)} %collective-permute-done.4.rest_4_), channel_id=1, source_target_pairs={{0,32},{32,0},{64,96},{96,64},{128,160},{160,128},{192,224},{224,1... | collective-permute-start | bytes 3194888 | tf_op jit(solution)/shard_map/ppermute | solution.py:250
  82.4 14.7 %collective-permute-start.15 = (s16[784,256]{1,0:T(8,128)(2,1)S(1)}, s16[784,256]{1,0:T(8,128)(2,1)S(1)}, u32[]{:S(2)}, u32[]{:S(2)}) collective-permute-start(s16[784,256]{1,0:T(8,128)(2,1)S(1)} %get-tuple-element.18), channel_id=1, source_target_pairs={{0,2},{1,3},{2,0},{3,1},{4,6},{5,7},{6,4},{7,5},{8,10},{9,11},{10,... | collective-permute-start | bytes 1204232 | tf_op jit(solution)/shard_map/ppermute | solution.py:245
  87.4 9.7 %copy-start.1 = (bf16[1,1,3,256,256]{4,3,2,1,0:T(8,128)(2,1)S(1)}, bf16[1,1,3,256,256]{4,3,2,1,0:T(8,128)(2,1)}, u32[]{:S(2)}) copy-start(bf16[1,1,3,256,256]{4,3,2,1,0:T(8,128)(2,1)} %param.13) | copy-start | bytes 1179652
  90.6 15.0 %collective-permute-start.13 = (s16[784,256]{1,0:T(8,128)(2,1)S(1)}, s16[784,256]{1,0:T(8,128)(2,1)S(1)}, u32[]{:S(2)}, u32[]{:S(2)}) collective-permute-start(s16[784,256]{1,0:T(8,128)(2,1)S(1)} %get-tuple-element.16), channel_id=1, source_target_pairs={{0,1},{1,2},{2,3},{3,0},{4,5},{5,6},{6,7},{7,4},{8,9},{9,10},{10,1... | collective-permute-start | bytes 1204232 | tf_op jit(solution)/shard_map/ppermute | solution.py:245
  92.5 13.0 %collective-permute-start.14 = (s16[784,256]{1,0:T(8,128)(2,1)S(1)}, s16[784,256]{1,0:T(8,128)(2,1)S(1)}, u32[]{:S(2)}, u32[]{:S(2)}) collective-permute-start(s16[784,256]{1,0:T(8,128)(2,1)S(1)} %get-tuple-element.17), channel_id=1, source_target_pairs={{0,3},{1,0},{2,1},{3,2},{4,7},{5,4},{6,5},{7,6},{8,11},{9,8},{10,9... | collective-permute-start | bytes 1204232 | tf_op jit(solution)/shard_map/ppermute | solution.py:245
